TPU v7x, 32 devices: a whole 2x2x4 slice. The times are simulated.
32 devices in a mesh: cores: 2 (over y), gz: 4 (over z), gy: 2 (over x), col: 2 (over core).
Axes of the slice: x: 2, y: 2, z: 4, core: 2. Of those that a mesh axis runs over, the one named last changes fastest.
Arguments:
- density: bfloat16 [32, 64, 512], P(('cores', 'gz'), 'gy', 'col'), parts along dimension 0, may hold values from -6 to 6
- first_kernel: bfloat16 [27, 8, 1], replicated, may hold values from -1.25 to 1.25
- first_bias: float32 [8], replicated, may hold values from -3 to 3
- second_kernel: bfloat16 [27, 2, 8], replicated, may hold values from -0.625 to 0.625
- second_bias: float32 [2], replicated, may hold values from -3 to 3
- owners: int32 [8, 2, 2, 16, 1], P(('cores', 'gz'), 'gy', 'col'), parts along dimension 0, may hold values from 0 to 3; in each aligned block of 16 rows (0 to 15, 16 to 31, ..., all dimensions but the last counted through in order) at most 8 rows name the same one
- solutes: float32 [8, 2, 2, 32, 2, 4, 4, 128], P(('cores', 'gz'), 'gy', 'col'), parts along dimension 0, may hold values from 0.2 to 2
- biomass: bfloat16 [8, 2, 2, 32, 4, 4, 128], P(('cores', 'gz'), 'gy', 'col'), parts along dimension 0, may hold values from 0.099609375 to 1
Outputs:
- fractions: bfloat16 [2, 32, 64, 512], P(None, ('cores', 'gz'), 'gy', 'col'), parts along dimension 1
- solutes_next: float32 [8, 2, 2, 32, 2, 4, 4, 128], P(('cores', 'gz'), 'gy', 'col'), parts along dimension 0
There are 2 independent parts, one for each index of `cores`. A program takes and returns all parts, laid end to end along the dimension named above; an argument that names none is the same for every part. Nothing has to cross between parts.
Inputs may be any that keep to these rules, and one draw needn't show every extreme that they name: `owners`: among the 16 bricks of one device at most 8 name the same owner, and some device reaches 8.
All inputs are finite; a program needn't handle non-finite values.
Results may differ from a plain program's by a relative error of at most 0.0034.
Values may be sent and summed in bfloat16 or wider, within the bound.
No kernel may reach another device: no remote copies, remote signals or barrier semaphores. Data moves between devices by JAX's collectives and lax.ppermute only.
A program may use at most 64 MiB of HBM per device.

v0:
```python
import jax
import jax.numpy as jnp
from jax import lax
from jax.sharding import PartitionSpec as P

BY = 4
BX = 128
STEPS = 4


def extended(array, sides, width):
    for axis, dim in sides:
        size, length = (lax.axis_size(axis), array.shape[dim])
        up = [(i, (i + 1) % size) for i in range(size - 1)]
        down = [(j, i) for i, j in up]
        last = lax.slice_in_dim(array, length - width, length, axis=dim)
        initial = lax.slice_in_dim(array, 0, width, axis=dim)
        before = lax.ppermute(last, axis, up)
        after = lax.ppermute(initial, axis, down)
        array = jnp.concatenate([before, array, after], axis=dim)
    return array


def conv_layer(padded, weights, depth, rows, columns):
    total = jnp.zeros((weights.shape[1], depth, rows, columns), jnp.float32)
    for offset in range(27):
        shift_z = offset // 9
        shift_y = offset // 3 % 3
        shift_x = offset % 3
        window = padded[
            :, shift_z : shift_z + depth, shift_y : shift_y + rows, shift_x : shift_x + columns
        ]
        total = total + jnp.einsum(
            "oc,czyx->ozyx", weights[offset], window, preferred_element_type=jnp.float32
        )
    return total


def single_channel_conv(padded, weights, depth, rows, columns):
    windows = []
    for offset in range(27):
        shift_z = offset // 9
        shift_y = offset // 3 % 3
        shift_x = offset % 3
        windows.append(
            padded[shift_z : shift_z + depth, shift_y : shift_y + rows, shift_x : shift_x + columns]
        )
    stacked = jnp.stack(windows, axis=0)
    return jnp.einsum(
        "ko,kzyx->ozyx", weights[:, :, 0], stacked, preferred_element_type=jnp.float32
    )


def laplace(field):
    padded = jnp.pad(field, [(0, 0)] * (field.ndim - 3) + [(1, 1), (1, 1), (1, 1)], mode="edge")
    centre = padded[..., 1:-1, 1:-1, 1:-1]
    beside_all = padded[..., 2:, 1:-1, 1:-1] + padded[..., :-2, 1:-1, 1:-1]
    beside_all = beside_all + padded[..., 1:-1, 2:, 1:-1] + padded[..., 1:-1, :-2, 1:-1]
    beside_all = beside_all + padded[..., 1:-1, 1:-1, 2:] + padded[..., 1:-1, 1:-1, :-2]
    return beside_all - 6.0 * centre


def advance(state, arrived, biomass):
    pore = arrived[..., 0, :, :, :].astype(jnp.float32)
    organic = arrived[..., 1, :, :, :].astype(jnp.float32)
    mass = biomass.astype(jnp.float32)
    carbon = state[..., 0, :, :, :]
    oxygen = state[..., 1, :, :, :]
    for step in range(STEPS):
        uptake = 0.25 * mass * carbon / (0.5 + jnp.abs(carbon)) * oxygen / (0.3 + jnp.abs(oxygen))
        carbon_new = carbon + 0.12 * pore * laplace(carbon) + 0.3 * organic - uptake
        oxygen_new = oxygen + 0.16 * pore * laplace(oxygen) - uptake
        carbon, oxygen = (carbon_new, oxygen_new)
    return jnp.stack([carbon, oxygen], axis=-4)


def per_device(
    density, first_kernel, first_bias, second_kernel, second_bias, owners, solutes, biomass
):
    depth, rows, columns = density.shape
    padded = extended(density, (("gz", 0), ("gy", 1), ("col", 2)), 1)
    first = single_channel_conv(padded, first_kernel, depth, rows, columns)
    hidden = jnp.maximum(first + first_bias[:, None, None, None], 0.0).astype(jnp.bfloat16)
    hidden_pad = extended(hidden, (("gz", 1), ("gy", 2), ("col", 3)), 1)
    second = conv_layer(hidden_pad, second_kernel, depth, rows, columns)
    fractions = jax.nn.sigmoid(second + second_bias[:, None, None, None]).astype(jnp.bfloat16)
    count_gz = lax.axis_size("gz")
    slots = solutes.shape[3]
    capacity = slots // count_gz
    brick_count = rows // BY * (columns // BX)
    feature = 2 * depth * BY * BX
    bricks = fractions.reshape(2, depth, rows // BY, BY, columns // BX, BX)
    bricks = bricks.transpose(2, 4, 0, 1, 3, 5).reshape(brick_count, feature)
    target = owners.reshape(brick_count)
    onehot = (target[:, None] == jnp.arange(count_gz, dtype=jnp.int32)[None, :]).astype(jnp.float32)
    lower = (jnp.arange(brick_count)[:, None] > jnp.arange(brick_count)[None, :]).astype(
        jnp.float32
    )
    before = jnp.dot(lower, onehot, preferred_element_type=jnp.float32)
    rank = jnp.sum(before * onehot, axis=1).astype(jnp.int32)
    slot_index = target * capacity + rank
    placing = (jnp.arange(slots, dtype=jnp.int32)[:, None] == slot_index[None, :]).astype(
        jnp.bfloat16
    )
    outgoing = jnp.dot(placing, bricks, preferred_element_type=jnp.float32).astype(jnp.bfloat16)
    arrived = lax.all_to_all(outgoing, "gz", split_axis=0, concat_axis=0, tiled=True)
    arrived = arrived.reshape(slots, 2, depth, BY, BX)
    state = solutes.reshape(slots, 2, depth, BY, BX)
    mass = biomass.reshape(slots, depth, BY, BX)
    solutes_next = advance(state, arrived, mass).reshape(solutes.shape)
    return (fractions, solutes_next)


def solution(mesh):
    return jax.shard_map(
        per_device,
        mesh=mesh,
        in_specs=(
            P(("cores", "gz"), "gy", "col"),
            P(),
            P(),
            P(),
            P(),
            P(("cores", "gz"), "gy", "col", None, None),
            P(("cores", "gz"), "gy", "col", None, None, None, None, None),
            P(("cores", "gz"), "gy", "col", None, None, None, None),
        ),
        out_specs=(
            P(None, ("cores", "gz"), "gy", "col"),
            P(("cores", "gz"), "gy", "col", None, None, None, None, None),
        ),
        check_vma=False,
    )
```

profile of v0, /device:TPU:0, one launch (start us, length us, event | category | flops | bytes accessed | tf_op | source)
XLA Modules:
  0.0 125.8 jit_solution(12690100801937874496)
XLA Ops:
  1.4 4.9 %collective-permute-start = (bf16[1,32,256]{2,1,0:T(8,128)(2,1)S(1)}, bf16[1,32,256]{2,1,0:T(8,128)(2,1)S(1)}, u32[]{:S(2)}, u32[]{:S(2)}) collective-permute-start(bf16[1,32,256]{2,1,0:T(8,128)(2,1)S(1)} %get-tuple-element.180), channel_id=1, source_target_pairs={{0,4},{4,8},{8,12},{1,5},{5,9},{9,13},{2,6},{6,10},{10,14},{3,7},{... | collective-permute-start | bytes 49160 | tf_op jit(solution)/shard_map/ppermute | solution.py:18
  6.3 1.3 %collective-permute-start.1 = (bf16[1,32,256]{2,1,0:T(8,128)(2,1)S(1)}, bf16[1,32,256]{2,1,0:T(8,128)(2,1)S(1)}, u32[]{:S(2)}, u32[]{:S(2)}) collective-permute-start(bf16[1,32,256]{2,1,0:T(8,128)(2,1)S(1)} %get-tuple-element.179), channel_id=1, source_target_pairs={{4,0},{8,4},{12,8},{5,1},{9,5},{13,9},{6,2},{10,6},{14,10},{7,3},{... | collective-permute-start | bytes 49160 | tf_op jit(solution)/shard_map/ppermute | solution.py:19
  8.5 1.2 convert_add_fusion
  9.7 1.1 copy.812
  11.3 1.4 %pad_maximum_fusion.3 = (f32[32,6,6,128]{3,2,1,0:T(8,128)}, f32[32,6,6,128]{3,2,1,0:T(8,128)S(1)}) fusion(f32[32,6,1,128]{3,2,1,0:T(1,128)S(1)} %get-tuple-element.126, f32[32,1,4,128]{3,2,1,0:T(4,128)S(1)} %get-tuple-element.142, f32[32,4,4,128]{3,2,1,0:T(4,128)S(1)} %get-tuple-element.108, f32[32,1,4,128]{3,2,1,0:T(4,128)S(1)} %get-tuple-element.141, ...), kind=kLoop, calls=%fused_computation.56 | loop fusion | flops 1179648 | bytes 2359296 | tf_op jit(solution)/shard_map/jit(_pad)/concatenate | solution.py:55
  13.6 3.4 %collective-permute-start.2 = (bf16[6,1,256]{2,1,0:T(2,128)(2,1)S(1)}, bf16[6,1,256]{2,1,0:T(2,128)(2,1)S(1)}, u32[]{:S(2)}, u32[]{:S(2)}) collective-permute-start(bf16[6,1,256]{2,1,0:T(2,128)(2,1)S(1)} %get-tuple-element.174), channel_id=1, source_target_pairs={{0,2},{1,3},{4,6},{5,7},{8,10},{9,11},{12,14},{13,15},{16,18},{17,... | collective-permute-start | bytes 9224 | tf_op jit(solution)/shard_map/ppermute | solution.py:18
  17.0 1.3 %collective-permute-start.3 = (bf16[6,1,256]{2,1,0:T(2,128)(2,1)S(1)}, bf16[6,1,256]{2,1,0:T(2,128)(2,1)S(1)}, u32[]{:S(2)}, u32[]{:S(2)}) collective-permute-start(bf16[6,1,256]{2,1,0:T(2,128)(2,1)S(1)} %get-tuple-element.175), channel_id=1, source_target_pairs={{2,0},{3,1},{6,4},{7,5},{10,8},{11,9},{14,12},{15,13},{18,16},{19,... | collective-permute-start | bytes 9224 | tf_op jit(solution)/shard_map/ppermute | solution.py:19
  21.3 1.2 collective-permute-done.3
  22.7 1.3 %collective-permute-start.4 = (bf16[6,34,1]{2,1,0:T(8,128)(2,1)S(1)}, bf16[6,34,1]{2,1,0:T(8,128)(2,1)S(1)}, u32[]{:S(2)}, u32[]{:S(2)}) collective-permute-start(bf16[6,34,1]{2,1,0:T(8,128)(2,1)S(1)} %get-tuple-element.162), channel_id=1, source_target_pairs={{0,1},{2,3},{4,5},{6,7},{8,9},{10,11},{12,13},{14,15},{16,17},{18,... | collective-permute-start | bytes 1232 | tf_op jit(solution)/shard_map/ppermute | solution.py:18
  24.0 1.3 %collective-permute-start.5 = (bf16[6,34,1]{2,1,0:T(8,128)(2,1)S(1)}, bf16[6,34,1]{2,1,0:T(8,128)(2,1)S(1)}, u32[]{:S(2)}, u32[]{:S(2)}) collective-permute-start(bf16[6,34,1]{2,1,0:T(8,128)(2,1)S(1)} %get-tuple-element.161), channel_id=1, source_target_pairs={{1,0},{3,2},{5,4},{7,6},{9,8},{11,10},{13,12},{15,14},{17,16},{19,... | collective-permute-start | bytes 1232 | tf_op jit(solution)/shard_map/ppermute | solution.py:19
  43.8 10.8 %stack.120 = bf16[27,4,32,256]{3,0,2,1:T(8,128)(2,1)S(1)} concatenate(bf16[1,4,32,256]{3,0,2,1:T(2,128)(2,1)} %copy.749, bf16[1,4,32,256]{3,0,2,1:T(2,128)(2,1)} %copy.750, bf16[1,4,32,256]{3,0,2,1:T(2,128)(2,1)} %copy.751, bf16[1,4,32,256]{3,0,2,1:T(2,128)(2,1)} %copy.752, bf16[1,4,32,256]{3,0,2,1:T(2,128)(2,1)} %copy.753, bf16[1,4,32,256]{3,0,2,1:T(2,128)(2,1)} %copy.754, ...), dimensions={0} | concatenate | bytes 3538944 | tf_op jit(solution)/shard_map/stack | solution.py:48
  54.7 1.0 fusion.3
  55.8 4.6 %collective-permute-start.6 = (bf16[8,1,32,256]{3,0,2,1:T(8,128)(2,1)S(1)}, bf16[8,1,32,256]{3,0,2,1:T(8,128)(2,1)S(1)}, u32[]{:S(2)}, u32[]{:S(2)}) collective-permute-start(bf16[8,1,32,256]{3,0,2,1:T(8,128)(2,1)S(1)} %get-tuple-element.109), channel_id=1, source_target_pairs={{0,4},{4,8},{8,12},{1,5},{5,9},{9,13},{2,6},{6,10},{10,14},{3,7},{... | collective-permute-start | bytes 393224 | tf_op jit(solution)/shard_map/ppermute | solution.py:18
  60.4 1.3 %collective-permute-start.7 = (bf16[8,1,32,256]{3,0,2,1:T(8,128)(2,1)S(1)}, bf16[8,1,32,256]{3,0,2,1:T(8,128)(2,1)S(1)}, u32[]{:S(2)}, u32[]{:S(2)}) collective-permute-start(bf16[8,1,32,256]{3,0,2,1:T(8,128)(2,1)S(1)} %get-tuple-element.110), channel_id=1, source_target_pairs={{4,0},{8,4},{12,8},{5,1},{9,5},{13,9},{6,2},{10,6},{14,10},{7,3},{... | collective-permute-start | bytes 393224 | tf_op jit(solution)/shard_map/ppermute | solution.py:19
  62.0 2.1 %collective-permute-done.6 = bf16[8,1,32,256]{3,0,2,1:T(8,128)(2,1)S(1)} collective-permute-done((bf16[8,1,32,256]{3,0,2,1:T(8,128)(2,1)S(1)}, bf16[8,1,32,256]{3,0,2,1:T(8,128)(2,1)S(1)}, u32[]{:S(2)}, u32[]{:S(2)}) %collective-permute-start.6) | collective-permute-done | bytes 131104 | tf_op jit(solution)/shard_map/ppermute | solution.py:18
  64.1 4.4 %collective-permute-done.7 = bf16[8,1,32,256]{3,0,2,1:T(8,128)(2,1)S(1)} collective-permute-done((bf16[8,1,32,256]{3,0,2,1:T(8,128)(2,1)S(1)}, bf16[8,1,32,256]{3,0,2,1:T(8,128)(2,1)S(1)}, u32[]{:S(2)}, u32[]{:S(2)}) %collective-permute-start.7) | collective-permute-done | bytes 131104 | tf_op jit(solution)/shard_map/ppermute | solution.py:19
  68.5 3.4 %collective-permute-start.8 = (bf16[8,6,1,256]{3,0,2,1:T(8,128)(2,1)S(1)}, bf16[8,6,1,256]{3,0,2,1:T(8,128)(2,1)S(1)}, u32[]{:S(2)}, u32[]{:S(2)}) collective-permute-start(bf16[8,6,1,256]{3,0,2,1:T(8,128)(2,1)S(1)} %get-tuple-element.105), channel_id=1, source_target_pairs={{0,2},{1,3},{4,6},{5,7},{8,10},{9,11},{12,14},{13,15},{16,18},{17,... | collective-permute-start | bytes 73736 | tf_op jit(solution)/shard_map/ppermute | solution.py:18
  71.9 1.3 %collective-permute-start.9 = (bf16[8,6,1,256]{3,0,2,1:T(8,128)(2,1)S(1)}, bf16[8,6,1,256]{3,0,2,1:T(8,128)(2,1)S(1)}, u32[]{:S(2)}, u32[]{:S(2)}) collective-permute-start(bf16[8,6,1,256]{3,0,2,1:T(8,128)(2,1)S(1)} %get-tuple-element.106), channel_id=1, source_target_pairs={{2,0},{3,1},{6,4},{7,5},{10,8},{11,9},{14,12},{15,13},{18,16},{19,... | collective-permute-start | bytes 73736 | tf_op jit(solution)/shard_map/ppermute | solution.py:19
  73.8 3.8 %collective-permute-done.9 = bf16[8,6,1,256]{3,0,2,1:T(8,128)(2,1)S(1)} collective-permute-done((bf16[8,6,1,256]{3,0,2,1:T(8,128)(2,1)S(1)}, bf16[8,6,1,256]{3,0,2,1:T(8,128)(2,1)S(1)}, u32[]{:S(2)}, u32[]{:S(2)}) %collective-permute-start.9) | collective-permute-done | bytes 24608 | tf_op jit(solution)/shard_map/ppermute | solution.py:19
  78.0 1.3 %collective-permute-start.10 = (bf16[8,6,34,1]{3,0,2,1:T(8,128)(2,1)S(1)}, bf16[8,6,34,1]{3,0,2,1:T(8,128)(2,1)S(1)}, u32[]{:S(2)}, u32[]{:S(2)}) collective-permute-start(bf16[8,6,34,1]{3,0,2,1:T(8,128)(2,1)S(1)} %get-tuple-element.87), channel_id=1, source_target_pairs={{0,1},{2,3},{4,5},{6,7},{8,9},{10,11},{12,13},{14,15},{16,17},{18,... | collective-permute-start | bytes 9800 | tf_op jit(solution)/shard_map/ppermute | solution.py:18
  79.3 1.5 %collective-permute-start.11 = (bf16[8,6,34,1]{3,0,2,1:T(8,128)(2,1)S(1)}, bf16[8,6,34,1]{3,0,2,1:T(8,128)(2,1)S(1)}, u32[]{:S(2)}, u32[]{:S(2)}) collective-permute-start(bf16[8,6,34,1]{3,0,2,1:T(8,128)(2,1)S(1)} %get-tuple-element.88), channel_id=1, source_target_pairs={{1,0},{3,2},{5,4},{7,6},{9,8},{11,10},{13,12},{15,14},{17,16},{19,... | collective-permute-start | bytes 9800 | tf_op jit(solution)/shard_map/ppermute | solution.py:19
  83.3 1.6 %maximum_maximum_fusion = (bf16[8,6,34,257]{3,0,2,1:T(8,128)(2,1)S(1)}, bf16[8,6,34,257]{3,0,2,1:T(8,128)(2,1)S(1)}) fusion(bf16[8,6,1,256]{3,0,2,1:T(8,128)(2,1)S(1)} %collective-permute-done.9, bf16[8,1,32,256]{3,0,2,1:T(8,128)(2,1)S(1)} %collective-permute-done.7, bf16[8,4,32,256]{3,0,2,1:T(8,128)(2,1)S(1)} %fusion.3, ...), kind=kLoop, calls=%fused_computation.5 | loop fusion | flops 10066176 | bytes 2519808 | tf_op jit(solution)/shard_map/concatenate | solution.py:20
  91.3 1.0 fusion.35
  93.5 3.9 %all-to-all-start = ((bf16[4,8,4096]{2,1,0:T(8,128)(2,1)}), bf16[4,8,4096]{2,1,0:T(8,128)(2,1)S(1)}, u32[]{:S(2)}, u32[]{:S(2)}) async-start(bf16[4,8,4096]{2,1,0:T(8,128)(2,1)} %fusion), calls=%async_computation | async-start | bytes 524288 | tf_op jit(solution)/shard_map/all_to_all | solution.py:106
  97.3 1.1 fusion.222
  98.5 1.4 %fusion.220 = (f32[32,6,6,1]{3,2,1,0:T(8,128)}, f32[32,6,6,1]{3,2,1,0:T(8,128)}) fusion(f32[32,6,6,128]{3,2,1,0:T(8,128)S(1)} %get-tuple-element.191), kind=kLoop, calls=%fused_computation.497 | loop fusion | bytes 18432 | tf_op jit(solution)/shard_map/jit(_pad)/slice | solution.py:55
  100.5 7.0 %all-to-all-done = bf16[4,8,4096]{2,1,0:T(8,128)(2,1)S(1)} async-done(((bf16[4,8,4096]{2,1,0:T(8,128)(2,1)}), bf16[4,8,4096]{2,1,0:T(8,128)(2,1)S(1)}, u32[]{:S(2)}, u32[]{:S(2)}) %all-to-all-start) | async-done | bytes 262176 | tf_op jit(solution)/shard_map/all_to_all | solution.py:106
  107.8 2.3 %fusion.77 = f32[32,4,4,128]{3,2,1,0:T(4,128)S(1)} fusion(f32[32,4,4,128]{3,2,1,0:T(4,128)S(1)} %copy-done.5, f32[32,6,6,1]{3,2,1,0:T(8,128)} %get-tuple-element.104, f32[32,6,1,128]{3,2,1,0:T(1,128)S(1)} %copy-done.17, f32[32,6,1,128]{3,2,1,0:T(1,128)S(1)} %copy-done.15, f32[32,1,4,128]{3,2,1,0:T(4,128)S(1)} %copy-done.13, ...), kind=kLoop, calls=%fused_computation.109 | loop fusion | flops 2818048 | bytes 1778688 | tf_op jit(solution)/shard_map/sub | solution.py:71
  112.0 2.6 %fusion.80 = (f32[32,4,4,128]{3,2,1,0:T(4,128)S(1)}, f32[32,4,4,128]{3,2,1,0:T(4,128)S(1)}) fusion(f32[32,4,4,128]{3,2,1,0:T(4,128)S(1)} %fusion.77, f32[32,6,6,1]{3,2,1,0:T(8,128)S(1)} %get-tuple-element.102, f32[32,6,1,128]{3,2,1,0:T(1,128)S(1)} %get-tuple-element.124, f32[32,6,1,128]{3,2,1,0:T(1,128)S(1)} %get-tuple-element.123, ...), kind=kLoop, calls=%fused_computation.112 | loop fusion | flops 5242880 | bytes 2639872 | tf_op jit(solution)/shard_map/sub | solution.py:71
  116.0 2.7 %fusion.83 = (f32[32,4,4,128]{3,2,1,0:T(4,128)S(1)}, f32[32,4,4,128]{3,2,1,0:T(4,128)S(1)}) fusion(f32[32,4,4,128]{3,2,1,0:T(4,128)S(1)} %get-tuple-element.83, f32[32,6,6,1]{3,2,1,0:T(8,128)S(1)} %get-tuple-element.98, f32[32,6,1,128]{3,2,1,0:T(1,128)S(1)} %get-tuple-element.120, f32[32,6,1,128]{3,2,1,0:T(1,128)S(1)} %get-tuple-element.119, ...), kind=kLoop, calls=%fused_computation.115 | loop fusion | flops 5242880 | bytes 2377728 | tf_op jit(solution)/shard_map/sub | solution.py:71
  120.2 2.7 %fusion.87 = (f32[32,1,4,4,128]{4,3,2,0,1:T(4,128)S(1)}, f32[32,4,4,128]{3,2,1,0:T(4,128)S(1)}) fusion(f32[32,4,4,128]{3,2,1,0:T(4,128)S(1)} %get-tuple-element.81, f32[32,6,6,1]{3,2,1,0:T(8,128)S(1)} %get-tuple-element.94, f32[32,6,1,128]{3,2,1,0:T(1,128)S(1)} %get-tuple-element.116, f32[32,6,1,128]{3,2,1,0:T(1,128)S(1)} %get-tuple-element.115, ...), kind=kLoop, calls=%fused_computation.119 | loop fusion | flops 5242880 | bytes 2377728 | tf_op jit(solution)/shard_map/stack | solution.py:74
  123.6 1.2 fusion.101
  (213 shorter events, 42.7 us)
Async XLA Ops:
  0.6 54.1 %copy-start = (bf16[27,8,1]{0,1,2:T(8,128)(2,1)S(1)}, bf16[27,8,1]{0,1,2:T(8,128)(2,1)}, u32[]{:S(2)}) copy-start(bf16[27,8,1]{0,1,2:T(8,128)(2,1)} %param.9) | copy-start | bytes 1300
  1.4 12.1 %collective-permute-start = (bf16[1,32,256]{2,1,0:T(8,128)(2,1)S(1)}, bf16[1,32,256]{2,1,0:T(8,128)(2,1)S(1)}, u32[]{:S(2)}, u32[]{:S(2)}) collective-permute-start(bf16[1,32,256]{2,1,0:T(8,128)(2,1)S(1)} %get-tuple-element.180), channel_id=1, source_target_pairs={{0,4},{4,8},{8,12},{1,5},{5,9},{9,13},{2,6},{6,10},{10,14},{3,7},{... | collective-permute-start | bytes 49160 | tf_op jit(solution)/shard_map/ppermute | solution.py:18
  6.3 7.2 %collective-permute-start.1 = (bf16[1,32,256]{2,1,0:T(8,128)(2,1)S(1)}, bf16[1,32,256]{2,1,0:T(8,128)(2,1)S(1)}, u32[]{:S(2)}, u32[]{:S(2)}) collective-permute-start(bf16[1,32,256]{2,1,0:T(8,128)(2,1)S(1)} %get-tuple-element.179), channel_id=1, source_target_pairs={{4,0},{8,4},{12,8},{5,1},{9,5},{13,9},{6,2},{10,6},{14,10},{7,3},{... | collective-permute-start | bytes 49160 | tf_op jit(solution)/shard_map/ppermute | solution.py:19
  10.8 1.9 %copy-start.2 = (f32[32,4,4,128]{3,2,1,0:T(4,128)}, f32[32,4,4,128]{3,2,1,0:T(4,128)S(1)}, u32[]{:S(2)}) copy-start(f32[32,4,4,128]{3,2,1,0:T(4,128)S(1)} %get-tuple-element.107) | copy-start | bytes 786436
  11.1 2.4 %copy-start.22 = (bf16[4,32,256]{2,1,0:T(8,128)(2,1)S(1)}, bf16[4,32,256]{2,1,0:T(8,128)(2,1)}, u32[]{:S(2)}) copy-start(bf16[4,32,256]{2,1,0:T(8,128)(2,1)} %param.8) | copy-start | bytes 196612
  11.3 7.8 %copy-start.14 = (f32[32,6,1,128]{3,2,1,0:T(1,128)}, f32[32,6,1,128]{3,2,1,0:T(1,128)S(1)}, u32[]{:S(2)}) copy-start(f32[32,6,1,128]{3,2,1,0:T(1,128)S(1)} %get-tuple-element.125) | copy-start | bytes 294916
  11.3 7.8 %copy-start.16 = (f32[32,6,1,128]{3,2,1,0:T(1,128)}, f32[32,6,1,128]{3,2,1,0:T(1,128)S(1)}, u32[]{:S(2)}) copy-start(f32[32,6,1,128]{3,2,1,0:T(1,128)S(1)} %get-tuple-element.126) | copy-start | bytes 294916
  13.6 7.7 %collective-permute-start.2 = (bf16[6,1,256]{2,1,0:T(2,128)(2,1)S(1)}, bf16[6,1,256]{2,1,0:T(2,128)(2,1)S(1)}, u32[]{:S(2)}, u32[]{:S(2)}) collective-permute-start(bf16[6,1,256]{2,1,0:T(2,128)(2,1)S(1)} %get-tuple-element.174), channel_id=1, source_target_pairs={{0,2},{1,3},{4,6},{5,7},{8,10},{9,11},{12,14},{13,15},{16,18},{17,... | collective-permute-start | bytes 9224 | tf_op jit(solution)/shard_map/ppermute | solution.py:18
  17.0 5.5 %collective-permute-start.3 = (bf16[6,1,256]{2,1,0:T(2,128)(2,1)S(1)}, bf16[6,1,256]{2,1,0:T(2,128)(2,1)S(1)}, u32[]{:S(2)}, u32[]{:S(2)}) collective-permute-start(bf16[6,1,256]{2,1,0:T(2,128)(2,1)S(1)} %get-tuple-element.175), channel_id=1, source_target_pairs={{2,0},{3,1},{6,4},{7,5},{10,8},{11,9},{14,12},{15,13},{18,16},{19,... | collective-permute-start | bytes 9224 | tf_op jit(solution)/shard_map/ppermute | solution.py:19
  22.7 7.2 %collective-permute-start.4 = (bf16[6,34,1]{2,1,0:T(8,128)(2,1)S(1)}, bf16[6,34,1]{2,1,0:T(8,128)(2,1)S(1)}, u32[]{:S(2)}, u32[]{:S(2)}) collective-permute-start(bf16[6,34,1]{2,1,0:T(8,128)(2,1)S(1)} %get-tuple-element.162), channel_id=1, source_target_pairs={{0,1},{2,3},{4,5},{6,7},{8,9},{10,11},{12,13},{14,15},{16,17},{18,... | collective-permute-start | bytes 1232 | tf_op jit(solution)/shard_map/ppermute | solution.py:18
  24.0 5.9 %collective-permute-start.5 = (bf16[6,34,1]{2,1,0:T(8,128)(2,1)S(1)}, bf16[6,34,1]{2,1,0:T(8,128)(2,1)S(1)}, u32[]{:S(2)}, u32[]{:S(2)}) collective-permute-start(bf16[6,34,1]{2,1,0:T(8,128)(2,1)S(1)} %get-tuple-element.161), channel_id=1, source_target_pairs={{1,0},{3,2},{5,4},{7,6},{9,8},{11,10},{13,12},{15,14},{17,16},{19,... | collective-permute-start | bytes 1232 | tf_op jit(solution)/shard_map/ppermute | solution.py:19
  54.7 7.0 %copy-start.36 = (bf16[2,8]{1,0:T(2,128)(2,1)S(1)}, bf16[2,8]{1,0:T(2,128)(2,1)}, u32[]{:S(2)}) copy-start(bf16[2,8]{1,0:T(2,128)(2,1)} %get-tuple-element.63) | copy-start | bytes 100
  55.8 17.4 %copy-start.47 = (bf16[2,8]{1,0:T(2,128)(2,1)S(1)}, bf16[2,8]{1,0:T(2,128)(2,1)}, u32[]{:S(2)}) copy-start(bf16[2,8]{1,0:T(2,128)(2,1)} %get-tuple-element.73) | copy-start | bytes 100
  55.8 17.7 %copy-start.44 = (bf16[2,8]{1,0:T(2,128)(2,1)S(1)}, bf16[2,8]{1,0:T(2,128)(2,1)}, u32[]{:S(2)}) copy-start(bf16[2,8]{1,0:T(2,128)(2,1)} %get-tuple-element.55) | copy-start | bytes 100
  55.8 8.3 %collective-permute-start.6 = (bf16[8,1,32,256]{3,0,2,1:T(8,128)(2,1)S(1)}, bf16[8,1,32,256]{3,0,2,1:T(8,128)(2,1)S(1)}, u32[]{:S(2)}, u32[]{:S(2)}) collective-permute-start(bf16[8,1,32,256]{3,0,2,1:T(8,128)(2,1)S(1)} %get-tuple-element.109), channel_id=1, source_target_pairs={{0,4},{4,8},{8,12},{1,5},{5,9},{9,13},{2,6},{6,10},{10,14},{3,7},{... | collective-permute-start | bytes 393224 | tf_op jit(solution)/shard_map/ppermute | solution.py:18
  60.4 8.1 %collective-permute-start.7 = (bf16[8,1,32,256]{3,0,2,1:T(8,128)(2,1)S(1)}, bf16[8,1,32,256]{3,0,2,1:T(8,128)(2,1)S(1)}, u32[]{:S(2)}, u32[]{:S(2)}) collective-permute-start(bf16[8,1,32,256]{3,0,2,1:T(8,128)(2,1)S(1)} %get-tuple-element.110), channel_id=1, source_target_pairs={{4,0},{8,4},{12,8},{5,1},{9,5},{13,9},{6,2},{10,6},{14,10},{7,3},{... | collective-permute-start | bytes 393224 | tf_op jit(solution)/shard_map/ppermute | solution.py:19
  68.5 5.3 %collective-permute-start.8 = (bf16[8,6,1,256]{3,0,2,1:T(8,128)(2,1)S(1)}, bf16[8,6,1,256]{3,0,2,1:T(8,128)(2,1)S(1)}, u32[]{:S(2)}, u32[]{:S(2)}) collective-permute-start(bf16[8,6,1,256]{3,0,2,1:T(8,128)(2,1)S(1)} %get-tuple-element.105), channel_id=1, source_target_pairs={{0,2},{1,3},{4,6},{5,7},{8,10},{9,11},{12,14},{13,15},{16,18},{17,... | collective-permute-start | bytes 73736 | tf_op jit(solution)/shard_map/ppermute | solution.py:18
  71.9 5.7 %collective-permute-start.9 = (bf16[8,6,1,256]{3,0,2,1:T(8,128)(2,1)S(1)}, bf16[8,6,1,256]{3,0,2,1:T(8,128)(2,1)S(1)}, u32[]{:S(2)}, u32[]{:S(2)}) collective-permute-start(bf16[8,6,1,256]{3,0,2,1:T(8,128)(2,1)S(1)} %get-tuple-element.106), channel_id=1, source_target_pairs={{2,0},{3,1},{6,4},{7,5},{10,8},{11,9},{14,12},{15,13},{18,16},{19,... | collective-permute-start | bytes 73736 | tf_op jit(solution)/shard_map/ppermute | solution.py:19
  73.8 7.0 %copy-start.46 = (bf16[2,8]{1,0:T(2,128)(2,1)S(1)}, bf16[2,8]{1,0:T(2,128)(2,1)}, u32[]{:S(2)}) copy-start(bf16[2,8]{1,0:T(2,128)(2,1)} %get-tuple-element.76) | copy-start | bytes 100
  77.8 3.3 %copy-start.43 = (bf16[2,8]{1,0:T(2,128)(2,1)S(1)}, bf16[2,8]{1,0:T(2,128)(2,1)}, u32[]{:S(2)}) copy-start(bf16[2,8]{1,0:T(2,128)(2,1)} %get-tuple-element.69) | copy-start | bytes 100
  78.0 5.3 %collective-permute-start.10 = (bf16[8,6,34,1]{3,0,2,1:T(8,128)(2,1)S(1)}, bf16[8,6,34,1]{3,0,2,1:T(8,128)(2,1)S(1)}, u32[]{:S(2)}, u32[]{:S(2)}) collective-permute-start(bf16[8,6,34,1]{3,0,2,1:T(8,128)(2,1)S(1)} %get-tuple-element.87), channel_id=1, source_target_pairs={{0,1},{2,3},{4,5},{6,7},{8,9},{10,11},{12,13},{14,15},{16,17},{18,... | collective-permute-start | bytes 9800 | tf_op jit(solution)/shard_map/ppermute | solution.py:18
  79.3 4.0 %collective-permute-start.11 = (bf16[8,6,34,1]{3,0,2,1:T(8,128)(2,1)S(1)}, bf16[8,6,34,1]{3,0,2,1:T(8,128)(2,1)S(1)}, u32[]{:S(2)}, u32[]{:S(2)}) collective-permute-start(bf16[8,6,34,1]{3,0,2,1:T(8,128)(2,1)S(1)} %get-tuple-element.88), channel_id=1, source_target_pairs={{1,0},{3,2},{5,4},{7,6},{9,8},{11,10},{13,12},{15,14},{17,16},{19,... | collective-permute-start | bytes 9800 | tf_op jit(solution)/shard_map/ppermute | solution.py:19
  83.3 2.0 %copy-start.30 = (bf16[2,8]{1,0:T(2,128)(2,1)S(1)}, bf16[2,8]{1,0:T(2,128)(2,1)}, u32[]{:S(2)}) copy-start(bf16[2,8]{1,0:T(2,128)(2,1)} %get-tuple-element.67) | copy-start | bytes 100
  83.3 2.3 %copy-start.29 = (bf16[2,8]{1,0:T(2,128)(2,1)S(1)}, bf16[2,8]{1,0:T(2,128)(2,1)}, u32[]{:S(2)}) copy-start(bf16[2,8]{1,0:T(2,128)(2,1)} %get-tuple-element.65) | copy-start | bytes 100
  92.3 5.0 %copy-start.1 = (f32[32,6,6,128]{3,2,1,0:T(8,128)S(1)}, f32[32,6,6,128]{3,2,1,0:T(8,128)}, u32[]{:S(2)}) copy-start(f32[32,6,6,128]{3,2,1,0:T(8,128)} %get-tuple-element.190) | copy-start | bytes 1769476
  93.5 14.0 %all-to-all-start = ((bf16[4,8,4096]{2,1,0:T(8,128)(2,1)}), bf16[4,8,4096]{2,1,0:T(8,128)(2,1)S(1)}, u32[]{:S(2)}, u32[]{:S(2)}) async-start(bf16[4,8,4096]{2,1,0:T(8,128)(2,1)} %fusion), calls=%async_computation | async-start | bytes 524288 | tf_op jit(solution)/shard_map/all_to_all | solution.py:106
  98.4 9.2 %copy-start.5 = (f32[32,4,4,128]{3,2,1,0:T(4,128)S(1)}, f32[32,4,4,128]{3,2,1,0:T(4,128)}, u32[]{:S(2)}) copy-start(f32[32,4,4,128]{3,2,1,0:T(4,128)} %copy-done.4) | copy-start | bytes 786436
  98.4 9.3 %copy-start.6 = (bf16[1,1,1,32,4,4,128]{6,5,4,3,2,1,0:T(4,128)(2,1)S(1)}, bf16[1,1,1,32,4,4,128]{6,5,4,3,2,1,0:T(4,128)(2,1)}, u32[]{:S(2)}) copy-start(bf16[1,1,1,32,4,4,128]{6,5,4,3,2,1,0:T(4,128)(2,1)} %param.15) | copy-start | bytes 393220
  98.5 9.3 %copy-start.11 = (f32[32,1,4,128]{3,2,1,0:T(4,128)S(1)}, f32[32,1,4,128]{3,2,1,0:T(4,128)}, u32[]{:S(2)}) copy-start(f32[32,1,4,128]{3,2,1,0:T(4,128)} %copy-done.10) | copy-start | bytes 196612
  98.5 9.3 %copy-start.13 = (f32[32,1,4,128]{3,2,1,0:T(4,128)S(1)}, f32[32,1,4,128]{3,2,1,0:T(4,128)}, u32[]{:S(2)}) copy-start(f32[32,1,4,128]{3,2,1,0:T(4,128)} %copy-done.12) | copy-start | bytes 196612
  98.5 9.3 %copy-start.15 = (f32[32,6,1,128]{3,2,1,0:T(1,128)S(1)}, f32[32,6,1,128]{3,2,1,0:T(1,128)}, u32[]{:S(2)}) copy-start(f32[32,6,1,128]{3,2,1,0:T(1,128)} %copy-done.14) | copy-start | bytes 294916
  98.5 9.3 %copy-start.17 = (f32[32,6,1,128]{3,2,1,0:T(1,128)S(1)}, f32[32,6,1,128]{3,2,1,0:T(1,128)}, u32[]{:S(2)}) copy-start(f32[32,6,1,128]{3,2,1,0:T(1,128)} %copy-done.16) | copy-start | bytes 294916
  (30 other events, 38.9 us)
where the time goes:
time: 127 us; the launch traced here: 126 us
  local copies, waits for them, and re-layouts  43.4 us (34%)
  starting transfers between devices  30.6 us (24%)
  other arithmetic  19.1 us (15%)
  waiting for transfers between devices  18.5 us (15%)
  matrix products  12.3 us (10%)
  between operations  1.86 us (1%)
    another operation x29, local copies, waits for them, and re-layouts, single_channel_conv(): stacked = jnp.stack(windows, axis=0)  31.4 us
    ppermute x6, starting transfers between devices, extended(): before = lax.ppermute(last, axis, up)  18.8 us
    dot_general x27, matrix products, conv_layer(): jnp.einsum('oc,czyx->ozyx', weights[offset], window, preferred_element_ty...  9.45 us
    ppermute x6, waiting for transfers between devices, extended(): after = lax.ppermute(initial, axis, down)  9.45 us
    ppermute x6, starting transfers between devices, extended(): after = lax.ppermute(initial, axis, down)  7.93 us
    sub x3, other arithmetic, advance(): carbon_new = carbon + 0.12 * pore * laplace(carbon) + 0.3 * organic - uptake  7.56 us
    all_to_all x1, waiting for transfers between devices, per_device(): lax.all_to_all(outgoing, 'gz', split_axis=0, concat_axis=0, tiled=True)  6.98 us
    unnamed x102, local copies, waits for them, and re-layouts  4.66 us
  transfers between devices with their start and end apart: 13, of which 5 were waited for; matrix products, arithmetic and copies ran while one was open for 15% of the time, Pallas kernels for 0%

commit v1 on v0

v1 whole, which is shorter than its diff:
```python
import functools

import jax
import jax.numpy as jnp
from jax import lax
from jax.experimental import pallas as pl
from jax.experimental.pallas import tpu as pltpu
from jax.sharding import PartitionSpec as P

BY = 4
BX = 128
STEPS = 4
TILE = 16
OUTSIDE = -3e38


def step_index(values, width, count):
    index = jnp.zeros(values.shape, jnp.int32)
    for k in range(1, count):
        index = index + (values >= k * width).astype(jnp.int32)
    return index


def one_hot(condition):
    return jnp.where(condition, 1.0, 0.0).astype(jnp.bfloat16)


def iotas(shape):
    return (
        lax.broadcasted_iota(jnp.int32, shape, 0),
        lax.broadcasted_iota(jnp.int32, shape, 1),
    )


def banded_kernel(dims, w1_ref, b1_ref, w2_ref, t1_ref, bias_ref, t2_ref):
    rows, window, edges, count_gy, channels = dims
    g = lax.axis_index("gy")
    part = rows + TILE * edges
    tall = (rows + 2) * channels
    row, _ = iotas((tall, channels))
    _, channel = iotas((tall, channels))
    spread = one_hot((row & (channels - 1)) == channel)
    w1 = lax.dot_general(
        spread, w1_ref[...], (((1,), (1,)), ((), ())), preferred_element_type=jnp.float32
    ).astype(jnp.bfloat16)
    tap, column = iotas((27, 9 * part))
    block = step_index(column, part, 9)
    dz = step_index(block, 3, 3)
    dx = block - 3 * dz
    row, column = iotas((tall, 9 * part))
    place = column - part * step_index(column, part, 9)
    below = jnp.where(g < count_gy - 1, place, 1000)
    above = jnp.where(g > 0, place - part, 1000)
    if edges == 1:
        outer = jnp.where(g == 0, below, above)
    else:
        outer = jnp.where(place < rows + TILE, below, above)
    input_row = jnp.where(place < rows, place, outer)
    distance = input_row - (row >> (channels.bit_length() - 1)) + 2
    total = jnp.zeros((tall, 9 * part), jnp.float32)
    for dy in range(3):
        pick = one_hot(tap == 9 * dz + 3 * dy + dx)
        values = jnp.dot(w1, pick, preferred_element_type=jnp.float32)
        total = jnp.where(distance == dy, values, total)
    t1_ref[...] = total.astype(jnp.bfloat16)
    row, _ = iotas((tall, window))
    bias = jnp.zeros((tall, window), jnp.float32)
    for k in range(channels):
        bias = jnp.where((row & (channels - 1)) == k, b1_ref[k], bias)
    outside = ((row < channels) & (g == 0)) | (
        (row >= tall - channels) & (g == count_gy - 1)
    )
    bias_ref[...] = jnp.where(outside, OUTSIDE, bias)
    channel, column = iotas((channels, 3 * tall))
    spread = one_hot((column & (channels - 1)) == channel)
    wide = jnp.dot(w2_ref[...], spread, preferred_element_type=jnp.float32)
    tap, column = iotas((54, 3 * tall))
    wide = jnp.where(
        step_index(tap, 18, 3) == step_index(column, tall, 3), wide, 0.0
    ).astype(jnp.bfloat16)
    row, tap = iotas((6 * rows, 54))
    tap_z = step_index(tap, 18, 3)
    tap_y = step_index(tap - 18 * tap_z, 6, 3)
    inside = tap - 18 * tap_z - 6 * tap_y
    tap_x, tap_o = inside >> 1, inside & 1
    row_x = step_index(row, 2 * rows, 3)
    same = (row_x == tap_x) & (((row >> 2) & 1) == tap_o)
    row, column = iotas((6 * rows, 3 * tall))
    local = row - 2 * rows * step_index(row, 2 * rows, 3)
    y = (local >> 3) * BY + (local & 3)
    hidden_row = (column - tall * step_index(column, tall, 3)) >> (channels.bit_length() - 1)
    total = jnp.zeros((6 * rows, 3 * tall), jnp.float32)
    for dy in range(3):
        values = jnp.dot(
            one_hot(same & (tap_y == dy)), wide, preferred_element_type=jnp.float32
        )
        total = jnp.where(hidden_row - y == dy, values, total)
    t2_ref[...] = total.astype(jnp.bfloat16)


def column_kernel(
    dims,
    b2_ref,
    gathered_ref,
    t1_ref,
    bias_ref,
    t2_ref,
    solutes_ref,
    biomass_ref,
    fractions_ref,
    next_ref,
    tiles,
    shifted,
    hidden,
    bricks,
    arrived,
    mass,
    owner_rows,
    owner_table,
    brick_of_slot,
    tile_sems,
    owner_sem,
):
    count_gz, count_gy, depth, rows, columns, channels, edges, segment, slots = dims
    z_index = lax.axis_index("gz")
    g = lax.axis_index("gy")
    c = lax.axis_index("col")
    window = columns + BX
    part = rows + TILE * edges
    tall = (rows + 2) * channels
    brick_rows = rows // BY
    brick_columns = columns // BX
    capacity = slots // count_gz
    segments = count_gz // segment
    single = segments == 1
    lead = 0 if single else 1
    held = segment + 2 * lead
    below, above = jnp.minimum(g + 1, count_gy - 1), jnp.maximum(g - 1, 0)
    if edges == 1:
        sides = [(g, c), (g, 1 - c), (1 - g, c), (1 - g, 1 - c)]
    else:
        sides = [(g, c), (g, 1 - c), (below, c), (below, 1 - c), (above, c), (above, 1 - c)]

    lane = lax.broadcasted_iota(jnp.int32, (TILE, window), 1)
    zero_slice = jnp.zeros((3 * part, window), jnp.bfloat16)
    zero_hidden = jnp.zeros((tall, window), jnp.bfloat16)

    def one_segment(q):
        copies = []
        for t in range(held):
            tile = jnp.clip(q * segment + t - lead, 0, count_gz - 1)
            for k, (gy, col) in enumerate(sides):
                copy = pltpu.make_async_copy(
                    gathered_ref.at[tile, gy, col], tiles.at[t, k], tile_sems.at[t, k]
                )
                copy.start()
                copies.append(copy)
        for copy in copies:
            copy.wait()

        for t in range(segment):
            row = tiles[t + lead, 0, depth * rows : depth * rows + TILE, 0:BX]
            owner_rows[t] = row[0:8].astype(jnp.float32).astype(jnp.int32)
        table = pltpu.make_async_copy(owner_rows, owner_table, owner_sem)
        table.start()

        def shifts(z, valid):
            t, zz = z // depth, z % depth
            for r in range(part // TILE):
                if r < rows // TILE:
                    side, start = 0, zz * rows + r * TILE
                elif edges == 1:
                    side, start = 2, zz * rows + jnp.where(g == 0, 0, rows - TILE)
                elif r == rows // TILE:
                    side, start = 2, zz * rows
                else:
                    side, start = 4, zz * rows + rows - TILE
                pieces = []
                for j in range(window // BX):
                    from_other = jnp.where(c == 0, int(j == window // BX - 1), int(j == 0))
                    offset = jnp.where(
                        c == 0,
                        j * BX if j < window // BX - 1 else 0,
                        (j - 1) * BX if j > 0 else columns - BX,
                    )
                    pieces.append(
                        tiles[
                            t,
                            side + from_other,
                            pl.ds(pl.multiple_of(start, TILE), TILE),
                            pl.ds(pl.multiple_of(offset, BX), BX),
                        ]
                    )
                centre = jnp.concatenate(pieces, axis=1).astype(jnp.float32)
                if valid is not None:
                    centre = centre * valid
                left = jnp.where(lane == 0, 0.0, pltpu.roll(centre, 1, 1))
                right = jnp.where(lane == window - 1, 0.0, pltpu.roll(centre, window - 1, 1))
                slot = z - depth * lead + 2
                for dx, value in enumerate((left, centre, right)):
                    at = slot * (3 * part) + dx * part + r * TILE
                    shifted[pl.ds(pl.multiple_of(at, TILE), TILE), :] = value.astype(jnp.bfloat16)

        if single:
            shifted[3 * part : 6 * part, :] = zero_slice
            at = (segment * depth + 2) * 3 * part
            shifted[at : at + 3 * part, :] = zero_slice

            @pl.loop(0, segment * depth, unroll=4)
            def _(z):
                shifts(z, None)
        else:

            @pl.loop(depth - 2, depth + segment * depth + 2)
            def _(z):
                at = q * segment * depth + z - depth
                valid = ((at >= 0) & (at < count_gz * depth)).astype(jnp.float32)
                shifts(z, valid)

        def first(z, valid):
            at = pl.multiple_of((z + 1) * (3 * part), TILE)
            total = jnp.dot(
                t1_ref[...], shifted[pl.ds(at, 9 * part), :], preferred_element_type=jnp.float32
            )
            values = jnp.maximum(total + bias_ref[...], 0.0)
            if valid is not None:
                values = values * valid
            at = pl.multiple_of((z + 1) * tall, TILE)
            hidden[pl.ds(at, tall), :] = values.astype(jnp.bfloat16)

        if single:
            hidden[0:tall, :] = zero_hidden
            at = (segment * depth + 1) * tall
            hidden[at : at + tall, :] = zero_hidden

            @pl.loop(0, segment * depth, unroll=2)
            def _(z):
                first(z, None)
        else:

            @pl.loop(-1, segment * depth + 1)
            def _(z):
                at = q * segment * depth + z
                first(z, ((at >= 0) & (at < count_gz * depth)).astype(jnp.float32))

        height = 2 * rows
        wide_lane = lax.broadcasted_iota(jnp.int32, (height, window), 1)
        fraction = (lax.broadcasted_iota(jnp.int32, (height, columns), 0) >> 2) & 1
        second_bias = jnp.where(fraction == 0, b2_ref[0], b2_ref[1])

        @pl.loop(0, segment * depth, unroll=2)
        def _(z):
            at = pl.multiple_of(z * tall, TILE)
            total = jnp.dot(
                t2_ref[...], hidden[pl.ds(at, 3 * tall), :], preferred_element_type=jnp.float32
            )
            before = pltpu.roll(total[0:height], 1, 1)
            after = pltpu.roll(total[2 * height :], window - 1, 1)
            total = total[height : 2 * height]
            total = total + jnp.where(wide_lane == 0, 0.0, before)
            total = total + jnp.where(wide_lane == window - 1, 0.0, after)
            own = jnp.where(c == 0, total[:, 0:columns], total[:, BX:window])
            values = 0.5 + 0.5 * jnp.tanh(0.5 * (own + second_bias))
            values = values.astype(jnp.bfloat16).astype(jnp.float32)
            t, zz = q * segment + z // depth, z % depth
            for yb in range(brick_rows):
                for xb in range(brick_columns):
                    bricks[t, yb * brick_columns + xb, zz] = values[
                        yb * 8 : yb * 8 + 8, xb * BX : (xb + 1) * BX
                    ]

        table.wait()

        @pl.loop(0, segment * capacity)
        def _(k):
            brick_of_slot[q * segment * capacity + k] = -1

        @pl.loop(0, segment)
        def _(t):
            rank = jnp.int32(0)
            for b in range(brick_rows * brick_columns):
                mine = owner_table[t, 0, b] == z_index

                @pl.when(mine)
                def _():
                    brick_of_slot[(q * segment + t) * capacity + rank] = b

                rank = rank + mine.astype(jnp.int32)

    if single:
        one_segment(0)
    else:

        @pl.loop(0, segments)
        def _(q):
            one_segment(q)

    for zz in range(depth):
        for xb in range(brick_columns):
            own = [bricks[z_index, yb * brick_columns + xb, zz] for yb in range(brick_rows)]
            for o in range(2):
                values = jnp.concatenate([v[o * BY : o * BY + BY] for v in own], axis=0)
                fractions_ref[o, zz, :, xb * BX : (xb + 1) * BX] = values.astype(jnp.bfloat16)

    size = depth * BY

    @pl.loop(0, slots)
    def _(j):
        brick = brick_of_slot[j]
        values = bricks[j // capacity, jnp.maximum(brick, 0)]
        values = jnp.where(brick >= 0, values, 0.0)
        at = pl.multiple_of(j * (2 * size), 8)
        arrived[pl.ds(at, 2 * size), :] = values.reshape(2 * size, BX)
        at = pl.multiple_of(j * size, size)
        mass[pl.ds(at, size), :] = 0.25 * biomass_ref[pl.ds(at, size), :].astype(jnp.float32)

    last = lax.broadcasted_iota(jnp.int32, (8, BX), 1) == BX - 1

    def laplace(field, z, y):
        centre = field[z][y]
        ahead = jnp.where(last, 0.0, pltpu.roll(centre, BX - 1, 1) - centre)
        result = ahead - pltpu.roll(ahead, 1, 1)
        beside = [
            field[zz][yy]
            for zz, yy in ((z - 1, y), (z + 1, y), (z, y - 1), (z, y + 1))
            if 0 <= zz < depth and 0 <= yy < BY
        ]
        return result + (functools.reduce(jnp.add, beside) - float(len(beside)) * centre)

    @pl.loop(0, slots // 8)
    def _(group):
        def load(ref, pitch, offset):
            return ref[pl.ds(group * 8 * pitch + offset, 8, stride=pitch), :]

        grid = [(z, y) for z in range(depth) for y in range(BY)]
        carbon = [[load(solutes_ref, 2 * size, z * BY + y) for y in range(BY)] for z in range(depth)]
        oxygen = [
            [load(solutes_ref, 2 * size, size + z * BY + y) for y in range(BY)]
            for z in range(depth)
        ]
        for _ in range(STEPS):
            carbon_new = [[None] * BY for _ in range(depth)]
            oxygen_new = [[None] * BY for _ in range(depth)]
            for z, y in grid:
                doc, oxy = carbon[z][y], oxygen[z][y]
                pore = load(arrived, 2 * size, z * 8 + y)
                organic = load(arrived, 2 * size, z * 8 + BY + y)
                quarter = load(mass, size, z * BY + y)
                uptake = (quarter * doc * oxy) / ((0.5 + jnp.abs(doc)) * (0.3 + jnp.abs(oxy)))
                carbon_new[z][y] = doc + (0.12 * pore) * laplace(carbon, z, y) + (
                    0.3 * organic - uptake
                )
                oxygen_new[z][y] = oxy + (0.16 * pore) * laplace(oxygen, z, y) - uptake
            carbon, oxygen = carbon_new, oxygen_new
        for z, y in grid:
            at = group * 16 * size + z * BY + y
            next_ref[pl.ds(at, 8, stride=2 * size), :] = carbon[z][y]
            next_ref[pl.ds(at + size, 8, stride=2 * size), :] = oxygen[z][y]


def vmem(shape, dtype):
    return pltpu.VMEM(shape, dtype)


def per_device(
    sizes, density, first_kernel, first_bias, second_kernel, second_bias, owners, solutes, biomass
):
    count_gz, count_gy, count_col = sizes
    depth, rows, columns = density.shape
    channels = first_kernel.shape[1]
    slots = solutes.shape[3]
    window = columns + BX
    edges = 1 if count_gy == 2 else 2
    part = rows + TILE * edges
    tall = (rows + 2) * channels
    segment = min(count_gz, 4)
    held = segment if segment == count_gz else segment + 2
    brick_count = (rows // BY) * (columns // BX)
    height = depth * rows

    named = jnp.zeros((TILE, columns), jnp.bfloat16)
    named = named.at[0, 0:brick_count].set(owners.reshape(brick_count).astype(jnp.bfloat16))
    payload = jnp.concatenate([density.reshape(height, columns), named], axis=0)
    gathered = lax.all_gather(payload, ("gz", "gy", "col"), axis=0, tiled=False)
    gathered = gathered.reshape(count_gz, count_gy, count_col, height + TILE, columns)

    in_vmem = pl.BlockSpec(memory_space=pltpu.VMEM)
    in_smem = pl.BlockSpec(memory_space=pltpu.SMEM)
    t1, bias, t2 = pl.pallas_call(
        functools.partial(banded_kernel, (rows, window, edges, count_gy, channels)),
        out_shape=(
            jax.ShapeDtypeStruct((tall, 9 * part), jnp.bfloat16),
            jax.ShapeDtypeStruct((tall, window), jnp.float32),
            jax.ShapeDtypeStruct((6 * rows, 3 * tall), jnp.bfloat16),
        ),
        in_specs=[in_vmem, in_smem, in_vmem],
        out_specs=(in_vmem, in_vmem, in_vmem),
        compiler_params=pltpu.CompilerParams(vmem_limit_bytes=24 * 2**20),
        cost_estimate=pl.CostEstimate(
            flops=2 * tall * 9 * part * 27 * 4, bytes_accessed=4 * 2**20, transcendentals=0
        ),
        name="banded",
    )(
        first_kernel.reshape(27, channels),
        first_bias,
        second_kernel.reshape(54, channels),
    )

    cells = depth * BY
    fractions, solutes_next = pl.pallas_call(
        functools.partial(
            column_kernel,
            (count_gz, count_gy, depth, rows, columns, channels, edges, segment, slots),
        ),
        out_shape=(
            jax.ShapeDtypeStruct((2, depth, rows, columns), jnp.bfloat16),
            jax.ShapeDtypeStruct((slots * 2 * cells, BX), jnp.float32),
        ),
        in_specs=[in_smem, pl.BlockSpec(memory_space=pl.ANY)] + [in_vmem] * 5,
        out_specs=(in_vmem, in_vmem),
        scratch_shapes=[
            vmem((held, 2 + 2 * edges, height + TILE, columns), jnp.bfloat16),
            vmem(((segment * depth + 4) * 3 * part, window), jnp.bfloat16),
            vmem(((segment * depth + 2) * tall, window), jnp.bfloat16),
            vmem((count_gz, brick_count, depth, 8, BX), jnp.float32),
            vmem((slots * 2 * cells, BX), jnp.float32),
            vmem((slots * cells, BX), jnp.float32),
            vmem((segment, 8, BX), jnp.int32),
            pltpu.SMEM((segment, 8, BX), jnp.int32),
            pltpu.SMEM((slots,), jnp.int32),
            pltpu.SemaphoreType.DMA((held, 2 + 2 * edges)),
            pltpu.SemaphoreType.DMA,
        ],
        compiler_params=pltpu.CompilerParams(vmem_limit_bytes=40 * 2**20),
        cost_estimate=pl.CostEstimate(
            flops=2 * count_gz * depth * window * tall * 9 * part,
            bytes_accessed=4 * 2**20,
            transcendentals=0,
        ),
        name="column",
    )(
        second_bias,
        gathered,
        t1,
        bias,
        t2,
        solutes.reshape(slots * 2 * cells, BX),
        biomass.reshape(slots * cells, BX),
    )
    return fractions, solutes_next.reshape(solutes.shape)


def solution(mesh):
    sizes = (mesh.shape["gz"], mesh.shape["gy"], mesh.shape["col"])
    assert sizes[2] == 2
    return jax.shard_map(
        functools.partial(per_device, sizes),
        mesh=mesh,
        in_specs=(
            P(("cores", "gz"), "gy", "col"),
            P(),
            P(),
            P(),
            P(),
            P(("cores", "gz"), "gy", "col", None, None),
            P(("cores", "gz"), "gy", "col", None, None, None, None, None),
            P(("cores", "gz"), "gy", "col", None, None, None, None),
        ),
        out_specs=(
            P(None, ("cores", "gz"), "gy", "col"),
            P(("cores", "gz"), "gy", "col", None, None, None, None, None),
        ),
        check_vma=False,
    )
```

time: 127 us -> 79.4 us (0.63)
  local copies, waits for them, and re-layouts: 43.4 us -> 6.12 us
  starting transfers between devices: 30.6 us -> 0.04 us
  waiting for transfers between devices: 18.5 us -> 38.9 us
  Pallas kernels: 0 us -> 17.8 us
  other arithmetic: 19.1 us -> 2.14 us
  matrix products: 12.3 us -> 0 us
  between operations: 1.86 us -> 14.1 us
    all_gather x0 -> x1, waiting for transfers between devices: none -> 38.9 us  [per_device(): gathered = lax.all_gather(payload, ('gz', 'gy', 'col'), axis=0, tiled=False)]
    another operation x29 -> x0, local copies, waits for them, and re-layouts: 31.4 us -> none  [single_channel_conv(): stacked = jnp.stack(windows, axis=0)]
    ppermute x12 -> x0, starting transfers between devices: 26.8 us -> none  [the longest x6 18.8 us: extended(): before = lax.ppermute(last, axis, up)]
    pallas_call x0 -> x2, Pallas kernels: none -> 17.8 us  [the longest x1 16.4 us: per_device(): pl.pallas_call(functools.partial(column_kernel, (count_gz, count_gy, dept...]
    dot_general x30 -> x0, matrix products: 12.3 us -> none  [the longest x27 9.45 us: conv_layer(): jnp.einsum('oc,czyx->ozyx', weights[offset], window, preferred_element_ty...]
    ppermute x12 -> x0, waiting for transfers between devices: 11.6 us -> none  [the longest x6 9.45 us: extended(): after = lax.ppermute(initial, axis, down)]
    sub x3 -> x0, other arithmetic: 7.56 us -> none  [advance(): carbon_new = carbon + 0.12 * pore * laplace(carbon) + 0.3 * organic - uptake]
    all_to_all x1 -> x0, waiting for transfers between devices: 6.98 us -> none  [per_device(): lax.all_to_all(outgoing, 'gz', split_axis=0, concat_axis=0, tiled=True)]
  transfers between devices with their start and end apart: 13 -> 1, of which waited for: 5 -> 1; matrix products, arithmetic and copies ran while one was open for 15% -> 2% of each run, Pallas kernels for 0% -> 2%
where the time goes in v1:
time: 79.4 us; the launch traced here: 79.1 us
  waiting for transfers between devices  38.9 us (49%)
  Pallas kernels  17.8 us (22%)
  between operations  14.1 us (18%)
  local copies, waits for them, and re-layouts  6.12 us (8%)
  other arithmetic  2.14 us (3%)
    all_gather x1, waiting for transfers between devices, per_device(): gathered = lax.all_gather(payload, ('gz', 'gy', 'col'), axis=0, tiled=False)  38.9 us
    pallas_call x1, Pallas kernels, per_device(): pl.pallas_call(functools.partial(column_kernel, (count_gz, count_gy, dept...  16.4 us
    unnamed x12, local copies, waits for them, and re-layouts  6.08 us
  transfers between devices with their start and end apart: 1, of which 1 were waited for; matrix products, arithmetic and copies ran while one was open for 2% of the time, Pallas kernels for 2%

profile of v1, /device:TPU:0, one launch (start us, length us, event | category | flops | bytes accessed | tf_op | source)
XLA Modules:
  0.0 79.1 jit_solution(11372541256786583835)
XLA Ops:
  7.2 0.0 all-gather.3.cloned.1.call-start
  7.2 0.7 convert_bitcast_fusion
  7.9 1.5 %fusion.1 = bf16[144,256]{1,0:T(8,128)(2,1)} fusion(bf16[1,16]{1,0:T(2,128)(2,1)S(1)} %convert_bitcast_fusion, bf16[128,256]{1,0:T(8,128)(2,1)} %bitcast.12), kind=kLoop, calls=%fused_computation.2 | loop fusion | flops 221184 | bytes 139296 | tf_op jit(solution)/shard_map/concatenate | solution.py:383
  9.3 0.0 all-gather.3.cloned.1.call-update
  9.4 0.8 copy.12
  10.1 0.8 copy.13
  11.0 0.0 copy-start.3
  11.0 0.6 copy-done.3
  11.6 1.4 %banded.1 = (bf16[272,432]{1,0:T(8,128)(2,1)S(1)}, f32[272,384]{1,0:T(8,128)S(1)}, bf16[192,816]{1,0:T(8,128)(2,1)S(1)}) custom-call(bf16[27,8]{1,0:T(8,128)(2,1)S(1)} %bitcast.8, f32[8]{0:T(128)S(1)} %copy-done.3, bf16[54,8]{1,0:T(8,128)(2,1)S(1)} %reshape.65.w2_ref), custom_call_target="tpu_custom_call" | custom-call | flops 25380864 | bytes 4194304 | tf_op jit(solution)/shard_map/banded/pallas_call | solution.py:389
  13.0 38.9 %all-gather.3.cloned.1.call-done = bf16[2304,256]{1,0:T(8,128)(2,1)} async-done(((bf16[144,256]{1,0:T(8,128)(2,1)}), bf16[2304,256]{1,0:T(8,128)(2,1)}) %all-gather.3.cloned.1.call-update) | async-done | bytes 1179664 | tf_op jit(solution)/shard_map/all_gather | solution.py:384
  51.9 0.0 copy-start
  51.9 1.3 %copy-done = bf16[2304,256]{1,0:T(8,128)(2,1)S(1)} copy-done((bf16[2304,256]{1,0:T(8,128)(2,1)S(1)}, bf16[2304,256]{1,0:T(8,128)(2,1)}, u32[]{:S(2)}) %copy-start) | copy-done | bytes 1179672
  53.2 0.0 copy-start.1
  53.2 1.0 %copy-done.1 = f32[1,1,1,32,2,4,4,128]{7,6,5,4,3,2,1,0:T(4,128)S(1)} copy-done((f32[1,1,1,32,2,4,4,128]{7,6,5,4,3,2,1,0:T(4,128)S(1)}, f32[1,1,1,32,2,4,4,128]{7,6,5,4,3,2,1,0:T(4,128)}, u32[]{:S(2)}) %copy-start.1) | copy-done | bytes 524312
  54.2 0.0 copy-start.2
  54.2 0.9 %copy-done.2 = bf16[1,1,1,32,4,4,128]{6,5,4,3,2,1,0:T(4,128)(2,1)S(1)} copy-done((bf16[1,1,1,32,4,4,128]{6,5,4,3,2,1,0:T(4,128)(2,1)S(1)}, bf16[1,1,1,32,4,4,128]{6,5,4,3,2,1,0:T(4,128)(2,1)}, u32[]{:S(2)}) %copy-start.2) | copy-done | bytes 131096
  55.1 0.0 copy-start.4
  55.1 0.7 copy-done.4
  55.8 16.4 %column.1 = (bf16[2,4,32,256]{3,2,1,0:T(8,128)(2,1)}, f32[1024,128]{1,0:T(8,128)}) custom-call(f32[2]{0:T(128)S(1)} %copy-done.4, bf16[4,2,2,144,256]{4,3,2,1,0:T(8,128)(2,1)S(1)} %bitcast.9, bf16[272,432]{1,0:T(8,128)(2,1)S(1)} %get-tuple-element.19.t1_ref, f32[272,384]{1,0:T(8,128)S(1)} %get-tuple-element.20.bias_ref, ...), custom_call_target="tpu_custom_call" | custom-call | flops 1443889152 | bytes 4194304 | tf_op jit(solution)/shard_map/column/pallas_call | solution.py:410
  (1 shorter events, 0.0 us)
Async XLA Ops:
  7.2 44.7 %all-gather.3.cloned.1.call-start = ((), (), s32[]{:S(2)}) async-start(), calls=%async_computation | async-start | bytes 1253376 | tf_op jit(solution)/shard_map/all_gather | solution.py:384
  11.0 0.7 copy-start.3
  51.9 1.3 %copy-start = (bf16[2304,256]{1,0:T(8,128)(2,1)S(1)}, bf16[2304,256]{1,0:T(8,128)(2,1)}, u32[]{:S(2)}) copy-start(bf16[2304,256]{1,0:T(8,128)(2,1)} %all-gather.3.cloned.1.call-done) | copy-start | bytes 3538948
  53.2 1.0 %copy-start.1 = (f32[1,1,1,32,2,4,4,128]{7,6,5,4,3,2,1,0:T(4,128)S(1)}, f32[1,1,1,32,2,4,4,128]{7,6,5,4,3,2,1,0:T(4,128)}, u32[]{:S(2)}) copy-start(f32[1,1,1,32,2,4,4,128]{7,6,5,4,3,2,1,0:T(4,128)} %param.16) | copy-start | bytes 1572868
  54.2 0.9 %copy-start.2 = (bf16[1,1,1,32,4,4,128]{6,5,4,3,2,1,0:T(4,128)(2,1)S(1)}, bf16[1,1,1,32,4,4,128]{6,5,4,3,2,1,0:T(4,128)(2,1)}, u32[]{:S(2)}) copy-start(bf16[1,1,1,32,4,4,128]{6,5,4,3,2,1,0:T(4,128)(2,1)} %param.17) | copy-start | bytes 393220
  55.1 0.7 copy-start.4
Sparse Core Ops, SparseCore 0:
  10.9 41.0 all-gather.2

commit v2 on v0

v2 whole, which is shorter than its diff:
```python
import functools

import jax
import jax.numpy as jnp
from jax import lax
from jax.experimental import pallas as pl
from jax.experimental.pallas import tpu as pltpu
from jax.sharding import PartitionSpec as P

BY = 4
BX = 128
STEPS = 4
TILE = 16
HALF = 16
CHANNELS = 8
REACH = HALF + 2
PART = 3 * HALF + TILE
TALL = REACH * CHANNELS
OUTSIDE = -3e38

VMEM = pl.BlockSpec(memory_space=pltpu.VMEM)
SMEM = pl.BlockSpec(memory_space=pltpu.SMEM)
HBM = pl.BlockSpec(memory_space=pltpu.HBM)


def step_index(values, width, count):
    index = jnp.zeros(values.shape, jnp.int32)
    for k in range(1, count):
        index = index + (values >= k * width).astype(jnp.int32)
    return index


def one_hot(condition):
    return jnp.where(condition, 1.0, 0.0).astype(jnp.bfloat16)


def iotas(shape):
    return (
        lax.broadcasted_iota(jnp.int32, shape, 0),
        lax.broadcasted_iota(jnp.int32, shape, 1),
    )


def tap_parts(tap):
    dz = step_index(tap, 9, 3)
    dy = step_index(tap - 9 * dz, 3, 3)
    return dz, dy, tap - 9 * dz - 3 * dy


def pack_kernel(density_ref, owners_ref, payload_ref, sem):
    height, columns = density_ref.shape
    copy = pltpu.make_async_copy(density_ref, payload_ref.at[0:height], sem)
    copy.start()
    named = owners_ref[...].astype(jnp.float32)
    count = named.shape[1]
    payload_ref[height : height + TILE, 0:BX] = jnp.concatenate(
        [
            jnp.broadcast_to(named, (TILE, count)),
            jnp.zeros((TILE, BX - count), jnp.float32),
        ],
        axis=1,
    ).astype(jnp.bfloat16)
    payload_ref[height : height + TILE, BX:columns] = jnp.zeros(
        (TILE, columns - BX), jnp.bfloat16
    )
    copy.wait()


def banded_kernel(dims, w1_ref, b1_ref, w2_ref, b2_ref, t1_ref, bias_ref, t2_ref, bias2_ref):
    window, count_gy = dims
    g = lax.axis_index("gy")
    row, channel = iotas((TALL, CHANNELS))
    spread = one_hot((row & (CHANNELS - 1)) == channel)
    w1 = jnp.dot(spread, w1_ref[...], preferred_element_type=jnp.float32).astype(jnp.bfloat16)
    tap, column = iotas((27, 3 * PART))
    dz = step_index(column, PART, 3)
    place = column - PART * dz
    dx = jnp.where(place < 3 * HALF, place >> 4, (place - 3 * HALF) >> 2)
    base = 9 * dz + dx
    row, column = iotas((TALL, 3 * PART))
    place = column & (PART - 1)
    seam = (place - 3 * HALF) & 3
    seam_row = jnp.where(seam < 2, seam - 2, seam + HALF - 2)
    input_row = jnp.where(place < 3 * HALF, place & (HALF - 1), seam_row)
    distance = jnp.where(place < 3 * HALF + 12, input_row - (row >> 3) + 2, -1)
    total = jnp.zeros((TALL, 3 * PART), jnp.float32)
    for dy in range(3):
        values = jnp.dot(w1, one_hot(tap == base + 3 * dy), preferred_element_type=jnp.float32)
        total = jnp.where(distance == dy, values, total)
    t1_ref[...] = total.astype(jnp.bfloat16)
    row, column = iotas((TALL, 2 * window))
    bias = jnp.zeros((TALL, 2 * window), jnp.float32)
    for k in range(CHANNELS):
        bias = jnp.where((row & (CHANNELS - 1)) == k, b1_ref[k], bias)
    outside = ((row < CHANNELS) & (column < window) & (g == 0)) | (
        (row >= TALL - CHANNELS) & (column >= window) & (g == count_gy - 1)
    )
    bias_ref[...] = jnp.where(outside, OUTSIDE, bias)
    channel, column = iotas((CHANNELS, 3 * TALL))
    spread = one_hot((column & (CHANNELS - 1)) == channel)
    tap, column = iotas((27, 3 * TALL))
    same_z = tap_parts(tap)[0] == step_index(column, TALL, 3)
    row, tap = iotas((6 * HALF, 27))
    _, tap_y, tap_x = tap_parts(tap)
    same_x = (row >> 5) == tap_x
    wide = []
    for o in range(2):
        values = lax.dot_general(
            w2_ref[o * CHANNELS : (o + 1) * CHANNELS, :],
            spread,
            (((0,), (0,)), ((), ())),
            preferred_element_type=jnp.float32,
        )
        wide.append(jnp.where(same_z, values, 0.0).astype(jnp.bfloat16))
    out_row, column = iotas((6 * HALF, 3 * TALL))
    y = ((out_row >> 3) & 3) * BY + (out_row & 3)
    hidden_row = (column - TALL * step_index(column, TALL, 3)) >> 3
    total = jnp.zeros((6 * HALF, 3 * TALL), jnp.float32)
    for dy in range(3):
        values = 0.0
        for o in range(2):
            pick = one_hot(same_x & (tap_y == dy) & (((row >> 2) & 1) == o))
            values = values + jnp.dot(pick, wide[o], preferred_element_type=jnp.float32)
        total = jnp.where(hidden_row - y == dy, values, total)
    t2_ref[...] = total.astype(jnp.bfloat16)
    row, _ = iotas((2 * HALF, 2 * window))
    bias2_ref[...] = jnp.where(((row >> 2) & 1) == 0, b2_ref[0], b2_ref[1])


def edges_kernel(dims, *refs):
    count_gy, depth, rows, columns, few, count = dims
    tiles, outs = refs[:few], refs[few:]
    g = lax.axis_index("gy")
    c = lax.axis_index("col")
    block = pl.multiple_of((1 - c) * BX, BX)

    def take(i, start, size, lanes):
        if few > 1:
            return tiles[i][pl.ds(start, size), lanes]
        return tiles[0][i, pl.ds(start, size), lanes]

    def pair(i):
        whole = pl.ds(0, columns)
        some = pl.ds(block, BX)
        for k in range(2):
            height = depth * rows
            at = (2 * i + k) * height
            if not isinstance(at, int):
                at = pl.multiple_of(at, TILE)
            outs[0][pl.ds(at, height), :] = take(2 * i + k, 0, height, some)
        low, high = ([], []), ([], [])
        for k in range(2):
            for zz in range(depth):
                for n, lanes in enumerate((whole, some)):
                    first = take(2 * i + k, zz * rows, TILE, lanes).astype(jnp.float32)
                    last = take(2 * i + k, (zz + 1) * rows - TILE, TILE, lanes).astype(jnp.float32)
                    low[n].append(first[0:2])
                    high[n].append(last[TILE - 2 :])
        at = 2 * i * 2 * depth
        if not isinstance(at, int):
            at = pl.multiple_of(at, TILE)
        for n in range(2):
            first = jnp.concatenate(low[n], axis=0)
            last = jnp.concatenate(high[n], axis=0)
            if count_gy == 2:
                send = jnp.where(g == 0, last, first)
                outs[1 + n][pl.ds(at, TILE), :] = send.astype(jnp.bfloat16)
            else:
                outs[1 + n][pl.ds(at, TILE), :] = last.astype(jnp.bfloat16)
                outs[3 + n][pl.ds(at, TILE), :] = first.astype(jnp.bfloat16)

    if few > 1:
        for i in range(count // 2):
            pair(i)
    else:
        pl.loop(0, count // 2)(pair)


def column_kernel(dims, few, *refs):
    count_gz, count_gy, depth, rows, columns, segment, slots = dims
    tiles, refs = refs[:few], refs[few:]
    x_ref, refs = refs[0], refs[1:]
    top_refs, refs = refs[:2], refs[2:]
    if count_gy == 2:
        bottom_refs = top_refs
    else:
        bottom_refs, refs = refs[:2], refs[2:]
    t1_ref, bias_ref, t2_ref, bias2_ref, solutes_ref, biomass_ref, *refs = refs
    fractions_ref, next_ref, *refs = refs
    (
        edge_rows,
        shifted,
        hidden,
        bricks,
        arrived,
        state,
        biomass,
        mass,
        fractions,
        owner_rows,
        owner_table,
        brick_of_slot,
        sems,
        group_sems,
    ) = refs
    z_index = lax.axis_index("gz")
    g = lax.axis_index("gy")
    c = lax.axis_index("col")
    window = columns + BX
    brick_rows = HALF // BY
    brick_columns = columns // BX
    brick_count = rows // BY * brick_columns
    capacity = slots // count_gz
    single = segment == count_gz
    first_tile = z_index if few > 1 else 0
    size = depth * BY

    state_copy = pltpu.make_async_copy(solutes_ref, state, sems.at[0])
    state_copy.start()
    biomass_copy = pltpu.make_async_copy(biomass_ref, biomass, sems.at[1])
    biomass_copy.start()

    def tile_rows(i, start, size, lanes):
        if not isinstance(start, int):
            start = pl.multiple_of(start, TILE)
        if few > 1:
            return tiles[i][pl.ds(start, size), lanes]
        return tiles[0][i, pl.ds(start, size), lanes]

    def read_owners(i):
        row = tile_rows(i, depth * rows, TILE, pl.ds(0, BX))
        owner_rows[i] = row.astype(jnp.float32)[0:8].astype(jnp.int32)

    if few > 1:
        for i in range(count_gz):
            read_owners(i)
    else:
        pl.loop(0, count_gz)(read_owners)
    table_copy = pltpu.make_async_copy(owner_rows, owner_table, sems.at[2])
    table_copy.start()

    def arrange(own, other):
        left, right = own[:, 0:BX], own[:, BX:columns]
        return jnp.concatenate(
            [
                jnp.where(c == 0, left, other),
                jnp.where(c == 0, right, left),
                jnp.where(c == 0, other, right),
            ],
            axis=1,
        )

    for k, pair in enumerate((top_refs, bottom_refs)):
        exists = (g > 0) if k == 0 else (g < count_gy - 1)
        values = arrange(pair[0][...].astype(jnp.float32), pair[1][...].astype(jnp.float32))
        edge_rows[k] = values * exists.astype(jnp.float32)

    def moved(values):
        lane = lax.broadcasted_iota(jnp.int32, values.shape, 1)
        return (
            jnp.where(lane == 0, 0.0, pltpu.roll(values, 1, 1)),
            values,
            jnp.where(lane == window - 1, 0.0, pltpu.roll(values, window - 1, 1)),
        )

    def edge_pair(k, at):
        if isinstance(at, int):
            return edge_rows[k, at : at + 2, :]
        group = edge_rows[k, pl.ds(pl.multiple_of(at // 8 * 8, 8), 8), :]
        return pltpu.roll(group, lax.rem(8 - at % 8, 8), 0)[0:2]

    def shifts(i, zz, slot, valid):
        z = i * depth + zz
        halves = []
        for h in range(2):
            own = tile_rows(i, zz * rows + h * HALF, HALF, pl.ds(0, columns))
            at = z * rows + h * HALF
            if not isinstance(at, int):
                at = pl.multiple_of(at, TILE)
            values = arrange(own, x_ref[pl.ds(at, HALF), :]).astype(jnp.float32)
            halves.append(values if valid is None else values * valid)
        top, bottom = edge_pair(0, 2 * z), edge_pair(1, 2 * z)
        if valid is not None:
            top, bottom = top * valid, bottom * valid
        seams = [
            jnp.concatenate([top, halves[1][0:2]], axis=0),
            jnp.concatenate([halves[0][HALF - 2 :], bottom], axis=0),
        ]
        for h in range(2):
            lanes = slice(h * window, (h + 1) * window)
            for dx, values in enumerate(moved(halves[h])):
                shifted[slot, dx * HALF : (dx + 1) * HALF, lanes] = values.astype(jnp.bfloat16)
            values = jnp.concatenate(
                [*moved(seams[h]), jnp.zeros((4, window), jnp.float32)], axis=0
            )
            shifted[slot, 3 * HALF : PART, lanes] = values.astype(jnp.bfloat16)

    def first(z, valid):
        total = jnp.dot(
            t1_ref[...],
            shifted[pl.ds(z + 1, 3)].reshape(3 * PART, 2 * window),
            preferred_element_type=jnp.float32,
        )
        values = jnp.maximum(total + bias_ref[...], 0.0)
        if valid is not None:
            values = values * valid
        hidden[z + 1] = values.astype(jnp.bfloat16)

    height = 2 * HALF
    lane = lax.broadcasted_iota(jnp.int32, (height, 2 * window), 1)
    left_edge = (lane == 0) | (lane == window)
    right_edge = (lane == window - 1) | (lane == 2 * window - 1)

    def second(z, t, zz):
        total = jnp.dot(
            t2_ref[...],
            hidden[pl.ds(z, 3)].reshape(3 * TALL, 2 * window),
            preferred_element_type=jnp.float32,
        )
        before = pltpu.roll(total[0:height], 1, 1)
        after = pltpu.roll(total[2 * height :], 2 * window - 1, 1)
        total = total[height : 2 * height] + bias2_ref[...]
        total = total + jnp.where(left_edge, 0.0, before)
        total = total + jnp.where(right_edge, 0.0, after)
        for h in range(2):
            at = h * window
            own = jnp.where(
                c == 0, total[:, at : at + columns], total[:, at + BX : at + window]
            )
            values = 0.5 + 0.5 * jnp.tanh(0.5 * own)
            values = values.astype(jnp.bfloat16).astype(jnp.float32)
            for yb in range(brick_rows):
                for xb in range(brick_columns):
                    b = (h * brick_rows + yb) * brick_columns + xb
                    bricks[t, b, zz] = values[yb * 8 : yb * 8 + 8, xb * BX : (xb + 1) * BX]

    def valid_slice(z):
        return ((z >= 0) & (z < count_gz * depth)).astype(jnp.float32)

    depths = segment * depth
    if single:
        shifted[1] = jnp.zeros((PART, 2 * window), jnp.bfloat16)
        shifted[depths + 2] = jnp.zeros((PART, 2 * window), jnp.bfloat16)
        hidden[0] = jnp.zeros((TALL, 2 * window), jnp.bfloat16)
        hidden[depths + 1] = jnp.zeros((TALL, 2 * window), jnp.bfloat16)
        for i in range(count_gz):
            tile = lax.rem(first_tile + i, count_gz)
            for zz in range(depth):
                shifts(i, zz, tile * depth + zz + 2, None)

        @pl.loop(0, depths, unroll=4)
        def _(z):
            first(z, None)

        @pl.loop(0, depths, unroll=4)
        def _(z):
            second(z, z // depth, z % depth)
    else:

        @pl.loop(0, count_gz // segment)
        def _(q):
            @pl.loop(-2, depths + 2)
            def _(z):
                at = q * depths + z
                inside = jnp.clip(at, 0, count_gz * depth - 1)
                shifts(inside // depth, inside % depth, z + 2, valid_slice(at))

            @pl.loop(-1, depths + 1)
            def _(z):
                first(z, valid_slice(q * depths + z))

            @pl.loop(0, depths)
            def _(z):
                second(z, q * segment + z // depth, z % depth)

    for zz in range(depth):
        for xb in range(brick_columns):
            own = [
                bricks[z_index, yb * brick_columns + xb, zz] for yb in range(rows // BY)
            ]
            for o in range(2):
                values = jnp.concatenate([v[o * BY : o * BY + BY] for v in own], axis=0)
                fractions[o, zz, :, xb * BX : (xb + 1) * BX] = values.astype(jnp.bfloat16)
    fractions_copy = pltpu.make_async_copy(fractions, fractions_ref, sems.at[3])
    fractions_copy.start()

    table_copy.wait()

    @pl.loop(0, slots)
    def _(j):
        brick_of_slot[j] = -1

    @pl.loop(0, count_gz)
    def _(i):
        tile = lax.rem(first_tile + i, count_gz)
        rank = jnp.int32(0)
        for b in range(brick_count):
            mine = owner_table[i, 0, b] == z_index

            @pl.when(mine)
            def _():
                brick_of_slot[tile * capacity + rank] = b

            rank = rank + mine.astype(jnp.int32)

    biomass_copy.wait()

    @pl.loop(0, slots)
    def _(j):
        brick = brick_of_slot[j]
        values = bricks[j // capacity, jnp.maximum(brick, 0)]
        values = jnp.where(brick >= 0, values, 0.0)
        at = pl.multiple_of(j * (2 * size), 8)
        arrived[pl.ds(at, 2 * size), :] = values.reshape(2 * size, BX)
        at = pl.multiple_of(j * size, size)
        mass[pl.ds(at, size), :] = 0.25 * biomass[pl.ds(at, size), :].astype(jnp.float32)

    last = lax.broadcasted_iota(jnp.int32, (8, BX), 1) == BX - 1

    def laplace(field, z, y):
        centre = field[z][y]
        ahead = jnp.where(last, 0.0, pltpu.roll(centre, BX - 1, 1) - centre)
        result = ahead - pltpu.roll(ahead, 1, 1)
        beside = [
            field[zz][yy]
            for zz, yy in ((z - 1, y), (z + 1, y), (z, y - 1), (z, y + 1))
            if 0 <= zz < depth and 0 <= yy < BY
        ]
        return result + (functools.reduce(jnp.add, beside) - float(len(beside)) * centre)

    state_copy.wait()

    def next_copy(group):
        at = pl.ds(pl.multiple_of(group * 16 * size, 16 * size), 16 * size)
        return pltpu.make_async_copy(state.at[at], next_ref.at[at], group_sems.at[group])

    @pl.loop(0, slots // 8)
    def _(group):
        def rows_of(pitch, offset):
            return pl.ds(group * 8 * pitch + offset, 8, stride=pitch)

        grid = [(z, y) for z in range(depth) for y in range(BY)]
        carbon = [
            [state[rows_of(2 * size, z * BY + y), :] for y in range(BY)] for z in range(depth)
        ]
        oxygen = [
            [state[rows_of(2 * size, size + z * BY + y), :] for y in range(BY)]
            for z in range(depth)
        ]
        for _ in range(STEPS):
            carbon_new = [[None] * BY for _ in range(depth)]
            oxygen_new = [[None] * BY for _ in range(depth)]
            for z, y in grid:
                doc, oxy = carbon[z][y], oxygen[z][y]
                pore = arrived[rows_of(2 * size, z * 8 + y), :]
                organic = arrived[rows_of(2 * size, z * 8 + BY + y), :]
                quarter = mass[rows_of(size, z * BY + y), :]
                uptake = (quarter * doc * oxy) / ((0.5 + jnp.abs(doc)) * (0.3 + jnp.abs(oxy)))
                carbon_new[z][y] = doc + (0.12 * pore) * laplace(carbon, z, y) + (
                    0.3 * organic - uptake
                )
                oxygen_new[z][y] = oxy + (0.16 * pore) * laplace(oxygen, z, y) - uptake
            carbon, oxygen = carbon_new, oxygen_new
        for z, y in grid:
            state[rows_of(2 * size, z * BY + y), :] = carbon[z][y]
            state[rows_of(2 * size, size + z * BY + y), :] = oxygen[z][y]
        next_copy(group).start()

    @pl.loop(0, slots // 8)
    def _(group):
        next_copy(group).wait()

    fractions_copy.wait()


def per_device(
    sizes, density, first_kernel, first_bias, second_kernel, second_bias, owners, solutes, biomass
):
    count_gz, count_gy, count_col = sizes
    depth, rows, columns = density.shape
    slots = solutes.shape[3]
    window = columns + BX
    segment = min(count_gz, 4)
    brick_count = (rows // BY) * (columns // BX)
    height = depth * rows
    depths = count_gz * depth
    bf16, f32 = jnp.bfloat16, jnp.float32
    shape = jax.ShapeDtypeStruct

    payload = pl.pallas_call(
        pack_kernel,
        out_shape=shape((height + TILE, columns), bf16),
        in_specs=[HBM, VMEM],
        out_specs=VMEM,
        scratch_shapes=[pltpu.SemaphoreType.DMA],
        compiler_params=pltpu.CompilerParams(vmem_limit_bytes=4 * 2**20),
        name="pack",
    )(density.reshape(height, columns), owners.reshape(1, brick_count))

    few = count_gz if count_gz == segment else 1
    if few > 1:
        tiles = [payload] + [
            lax.ppermute(payload, "gz", [((i + s) % count_gz, i) for i in range(count_gz)])
            for s in range(1, count_gz)
        ]
    else:
        tiles = [lax.all_gather(payload, "gz", axis=0, tiled=False)]

    t1, bias, t2, bias2 = pl.pallas_call(
        functools.partial(banded_kernel, (window, count_gy)),
        out_shape=(
            shape((TALL, 3 * PART), bf16),
            shape((TALL, 2 * window), f32),
            shape((6 * HALF, 3 * TALL), bf16),
            shape((2 * HALF, 2 * window), f32),
        ),
        in_specs=[VMEM, SMEM, VMEM, SMEM],
        out_specs=(VMEM, VMEM, VMEM, VMEM),
        compiler_params=pltpu.CompilerParams(vmem_limit_bytes=16 * 2**20),
        cost_estimate=pl.CostEstimate(
            flops=20 * 2**20, bytes_accessed=4 * 2**20, transcendentals=0
        ),
        name="banded",
    )(
        first_kernel.transpose(2, 1, 0).reshape(CHANNELS, 27),
        first_bias,
        second_kernel.transpose(1, 2, 0).reshape(2 * CHANNELS, 27),
        second_bias,
    )

    edge_shapes = [shape((2 * depths, columns), bf16), shape((2 * depths, BX), bf16)]
    sent = pl.pallas_call(
        functools.partial(edges_kernel, (count_gy, depth, rows, columns, few, count_gz)),
        out_shape=[shape((depths * rows, BX), bf16)] + edge_shapes * (1 if count_gy == 2 else 2),
        in_specs=[VMEM] * few,
        out_specs=[VMEM] * (3 if count_gy == 2 else 5),
        compiler_params=pltpu.CompilerParams(vmem_limit_bytes=16 * 2**20),
        name="edges",
    )(*tiles)

    def over(pairs):
        return [
            (gy * count_col + col, to * count_col + 1 - col)
            for gy, to in pairs
            for col in range(count_col)
        ]

    beside = lax.ppermute(sent[0], "col", [(0, 1), (1, 0)])
    if count_gy == 2:
        directions = [[(0, 1), (1, 0)]]
    else:
        up = [(i, i + 1) for i in range(count_gy - 1)]
        directions = [up, [(j, i) for i, j in up]]
    edges = []
    for k, pairs in enumerate(directions):
        edges.append(lax.ppermute(sent[1 + 2 * k], "gy", pairs))
        edges.append(lax.ppermute(sent[2 + 2 * k], ("gy", "col"), over(pairs)))

    cells = depth * BY
    fractions, solutes_next = pl.pallas_call(
        functools.partial(
            column_kernel, (count_gz, count_gy, depth, rows, columns, segment, slots), few
        ),
        out_shape=(
            shape((2, depth, rows, columns), bf16),
            shape((slots * 2 * cells, BX), f32),
        ),
        in_specs=[VMEM] * (few + 1 + len(edges) + 4) + [HBM, HBM],
        out_specs=(HBM, HBM),
        scratch_shapes=[
            pltpu.VMEM((2, 2 * depths, window), f32),
            pltpu.VMEM((segment * depth + 4, PART, 2 * window), bf16),
            pltpu.VMEM((segment * depth + 2, TALL, 2 * window), bf16),
            pltpu.VMEM((count_gz, brick_count, depth, 8, BX), f32),
            pltpu.VMEM((slots * 2 * cells, BX), f32),
            pltpu.VMEM((slots * 2 * cells, BX), f32),
            pltpu.VMEM((slots * cells, BX), bf16),
            pltpu.VMEM((slots * cells, BX), f32),
            pltpu.VMEM((2, depth, rows, columns), bf16),
            pltpu.VMEM((count_gz, 8, BX), jnp.int32),
            pltpu.SMEM((count_gz, 8, BX), jnp.int32),
            pltpu.SMEM((slots,), jnp.int32),
            pltpu.SemaphoreType.DMA((4,)),
            pltpu.SemaphoreType.DMA((slots // 8,)),
        ],
        compiler_params=pltpu.CompilerParams(vmem_limit_bytes=40 * 2**20),
        cost_estimate=pl.CostEstimate(
            flops=2 * depths * 2 * window * TALL * (3 * PART + 3 * 6 * HALF),
            bytes_accessed=4 * 2**20,
            transcendentals=0,
        ),
        name="column",
    )(
        *tiles,
        beside,
        *edges,
        t1,
        bias,
        t2,
        bias2,
        solutes.reshape(slots * 2 * cells, BX),
        biomass.reshape(slots * cells, BX),
    )
    return fractions, solutes_next.reshape(solutes.shape)


def solution(mesh):
    sizes = (mesh.shape["gz"], mesh.shape["gy"], mesh.shape["col"])
    assert sizes[2] == 2
    return jax.shard_map(
        functools.partial(per_device, sizes),
        mesh=mesh,
        in_specs=(
            P(("cores", "gz"), "gy", "col"),
            P(),
            P(),
            P(),
            P(),
            P(("cores", "gz"), "gy", "col", None, None),
            P(("cores", "gz"), "gy", "col", None, None, None, None, None),
            P(("cores", "gz"), "gy", "col", None, None, None, None),
        ),
        out_specs=(
            P(None, ("cores", "gz"), "gy", "col"),
            P(("cores", "gz"), "gy", "col", None, None, None, None, None),
        ),
        check_vma=False,
    )
```

time: 127 us -> 29.6 us (0.23)
  local copies, waits for them, and re-layouts: 43.4 us -> 5.07 us
  starting transfers between devices: 30.6 us -> 8.95 us
  other arithmetic: 19.1 us -> 0 us
  waiting for transfers between devices: 18.5 us -> 3.83 us
  matrix products: 12.3 us -> 0 us
  Pallas kernels: 0 us -> 10.8 us
    another operation x29 -> x0, local copies, waits for them, and re-layouts: 31.4 us -> none  [single_channel_conv(): stacked = jnp.stack(windows, axis=0)]
    ppermute x12 -> x6, starting transfers between devices: 26.8 us -> 8.95 us  [the longest x3 7.01 us: per_device(): lax.ppermute(payload, 'gz', [((i + s) % count_gz, i) for i in range(count...]
    dot_general x30 -> x0, matrix products: 12.3 us -> none  [the longest x27 9.45 us: conv_layer(): jnp.einsum('oc,czyx->ozyx', weights[offset], window, preferred_element_ty...]
    pallas_call x0 -> x4, Pallas kernels: none -> 10.8 us  [the longest x1 9.47 us: per_device(): pl.pallas_call(functools.partial(column_kernel, (count_gz, count_gy, dept...]
    ppermute x12 -> x6, waiting for transfers between devices: 11.6 us -> 3.83 us  [the longest x3 3.83 us: per_device(): lax.ppermute(payload, 'gz', [((i + s) % count_gz, i) for i in range(count...]
    sub x3 -> x0, other arithmetic: 7.56 us -> none  [advance(): carbon_new = carbon + 0.12 * pore * laplace(carbon) + 0.3 * organic - uptake]
    all_to_all x1 -> x0, waiting for transfers between devices: 6.98 us -> none  [per_device(): lax.all_to_all(outgoing, 'gz', split_axis=0, concat_axis=0, tiled=True)]
    slice x23 -> x0, local copies, waits for them, and re-layouts: 6.95 us -> none  [the longest x16 4.31 us: laplace(): jnp.pad(field, [(0, 0)] * (field.ndim - 3) + [(1, 1), (1, 1), (1, 1)], mo...]
  transfers between devices with their start and end apart: 13 -> 6, of which waited for: 5 -> 3; matrix products, arithmetic and copies ran while one was open for 15% -> 0% of each run, Pallas kernels for 0% -> 4%
where the time goes in v2:
time: 29.6 us; the launch traced here: 29.3 us
  Pallas kernels  10.8 us (36%)
  starting transfers between devices  8.95 us (30%)
  local copies, waits for them, and re-layouts  5.07 us (17%)
  waiting for transfers between devices  3.83 us (13%)
  between operations  0.71 us (2%)
    pallas_call x1, Pallas kernels, per_device(): pl.pallas_call(functools.partial(column_kernel, (count_gz, count_gy, dept...  9.47 us
    ppermute x3, starting transfers between devices, per_device(): lax.ppermute(payload, 'gz', [((i + s) % count_gz, i) for i in range(count...  7.01 us
    unnamed x16, local copies, waits for them, and re-layouts  5.07 us
    ppermute x3, waiting for transfers between devices, per_device(): lax.ppermute(payload, 'gz', [((i + s) % count_gz, i) for i in range(count...  3.83 us
    ppermute x1, starting transfers between devices, per_device(): edges.append(lax.ppermute(sent[1 + 2 * k], 'gy', pairs))  1.55 us
    pallas_call x1, Pallas kernels, per_device(): pl.pallas_call(functools.partial(banded_kernel, (window, count_gy)), out_...  1.16 us
  transfers between devices with their start and end apart: 6, of which 3 were waited for; matrix products, arithmetic and copies ran while one was open for 0% of the time, Pallas kernels for 4%

profile of v2, /device:TPU:0, one launch (start us, length us, event | category | flops | bytes accessed | tf_op | source)
XLA Modules:
  0.0 29.3 jit_solution(7623174508493196812)
XLA Ops:
  0.6 0.0 copy-start.1
  0.6 0.6 %copy-done.1 = s32[1,1,1,16,1]{3,4,2,1,0:T(1,128)S(1)} copy-done((s32[1,1,1,16,1]{3,4,2,1,0:T(1,128)S(1)}, s32[1,1,1,16,1]{3,4,2,1,0:T(1,128)}, u32[]{:S(2)}) %copy-start.1) | copy-done | bytes 88
  1.3 0.0 copy-start
  1.3 0.8 %copy-done = bf16[4,32,256]{2,1,0:T(8,128)(2,1)S(1)} copy-done((bf16[4,32,256]{2,1,0:T(8,128)(2,1)S(1)}, bf16[4,32,256]{2,1,0:T(8,128)(2,1)}, u32[]{:S(2)}) %copy-start) | copy-done | bytes 65560
  2.1 0.0 copy-start.2
  2.1 0.1 pack.1.refs_0_
  2.2 3.1 %collective-permute-start.2 = (bf16[144,256]{1,0:T(8,128)(2,1)S(1)}, bf16[144,256]{1,0:T(8,128)(2,1)S(1)}, u32[]{:S(2)}, u32[]{:S(2)}) collective-permute-start(bf16[144,256]{1,0:T(8,128)(2,1)S(1)} %pack.1.refs_0_), channel_id=1, source_target_pairs={{12,0},{0,4},{4,8},{8,12},{13,1},{1,5},{5,9},{9,13},{14,2},{2,6},{... | collective-permute-start | bytes 221192 | tf_op jit(solution)/shard_map/ppermute | solution.py:503
  5.3 2.6 %collective-permute-start.1 = (bf16[144,256]{1,0:T(8,128)(2,1)S(1)}, bf16[144,256]{1,0:T(8,128)(2,1)S(1)}, u32[]{:S(2)}, u32[]{:S(2)}) collective-permute-start(bf16[144,256]{1,0:T(8,128)(2,1)S(1)} %pack.1.refs_0_), channel_id=1, source_target_pairs={{8,0},{12,4},{0,8},{4,12},{9,1},{13,5},{1,9},{5,13},{10,2},{14,6},... | collective-permute-start | bytes 221192 | tf_op jit(solution)/shard_map/ppermute | solution.py:503
  7.9 1.3 %collective-permute-start = (bf16[144,256]{1,0:T(8,128)(2,1)S(1)}, bf16[144,256]{1,0:T(8,128)(2,1)S(1)}, u32[]{:S(2)}, u32[]{:S(2)}) collective-permute-start(bf16[144,256]{1,0:T(8,128)(2,1)S(1)} %pack.1.refs_0_), channel_id=1, source_target_pairs={{4,0},{8,4},{12,8},{0,12},{5,1},{9,5},{13,9},{1,13},{6,2},{10,6},{... | collective-permute-start | bytes 221192 | tf_op jit(solution)/shard_map/ppermute | solution.py:503
  9.2 0.8 %collective-permute-done.2.refs_3_ = bf16[144,256]{1,0:T(8,128)(2,1)S(1)} collective-permute-done((bf16[144,256]{1,0:T(8,128)(2,1)S(1)}, bf16[144,256]{1,0:T(8,128)(2,1)S(1)}, u32[]{:S(2)}, u32[]{:S(2)}) %collective-permute-start.2) | collective-permute-done | bytes 73760 | tf_op jit(solution)/shard_map/ppermute | solution.py:503
  10.0 2.8 %collective-permute-done.1.refs_2_ = bf16[144,256]{1,0:T(8,128)(2,1)S(1)} collective-permute-done((bf16[144,256]{1,0:T(8,128)(2,1)S(1)}, bf16[144,256]{1,0:T(8,128)(2,1)S(1)}, u32[]{:S(2)}, u32[]{:S(2)}) %collective-permute-start.1) | collective-permute-done | bytes 73760 | tf_op jit(solution)/shard_map/ppermute | solution.py:503
  12.8 0.2 collective-permute-done.refs_1_
  13.1 0.1 edges.1
  13.1 0.1 collective-permute-start.3
  13.2 1.6 %collective-permute-start.4 = (bf16[32,256]{1,0:T(8,128)(2,1)S(1)}, bf16[32,256]{1,0:T(8,128)(2,1)S(1)}, u32[]{:S(2)}, u32[]{:S(2)}) collective-permute-start(bf16[32,256]{1,0:T(8,128)(2,1)S(1)} %get-tuple-element.12), channel_id=1, source_target_pairs={{0,2},{2,0},{1,3},{3,1},{4,6},{6,4},{5,7},{7,5},{8,10},{10,8},{9,1... | collective-permute-start | bytes 49160 | tf_op jit(solution)/shard_map/ppermute | solution.py:556
  14.7 0.3 %collective-permute-start.5 = (bf16[32,128]{1,0:T(8,128)(2,1)S(1)}, bf16[32,128]{1,0:T(8,128)(2,1)S(1)}, u32[]{:S(2)}, u32[]{:S(2)}) collective-permute-start(bf16[32,128]{1,0:T(8,128)(2,1)S(1)} %get-tuple-element.13), channel_id=1, source_target_pairs={{0,3},{1,2},{2,1},{3,0},{4,7},{5,6},{6,5},{7,4},{8,11},{9,10},{10,... | collective-permute-start | bytes 24584 | tf_op jit(solution)/shard_map/ppermute | solution.py:557
  15.0 0.0 copy-start.4
  15.1 0.7 %copy-done.4 = bf16[27,2,8]{0,2,1:T(8,128)(2,1)S(1)} copy-done((bf16[27,2,8]{0,2,1:T(8,128)(2,1)S(1)}, bf16[27,2,8]{0,2,1:T(8,128)(2,1)}, u32[]{:S(2)}) %copy-start.4) | copy-done | bytes 888
  15.7 0.0 copy-start.5
  15.7 0.7 %copy-done.5 = bf16[27,8,1]{0,1,2:T(8,128)(2,1)S(1)} copy-done((bf16[27,8,1]{0,1,2:T(8,128)(2,1)S(1)}, bf16[27,8,1]{0,1,2:T(8,128)(2,1)}, u32[]{:S(2)}) %copy-start.5) | copy-done | bytes 456
  16.4 0.0 copy-start.6
  16.4 0.7 %copy-done.6 = f32[8]{0:T(128)S(1)} copy-done((f32[8]{0:T(128)S(1)}, f32[8]{0:T(128)}, u32[]{:S(2)}) %copy-start.6) | copy-done | bytes 56
  17.1 0.0 copy-start.7
  17.1 0.7 %copy-done.7 = f32[2]{0:T(128)S(1)} copy-done((f32[2]{0:T(128)S(1)}, f32[2]{0:T(128)}, u32[]{:S(2)}) %copy-start.7) | copy-done | bytes 32
  17.7 1.2 %banded.1 = (bf16[144,192]{1,0:T(8,128)(2,1)S(1)}, f32[144,768]{1,0:T(8,128)S(1)}, bf16[96,432]{1,0:T(8,128)(2,1)S(1)}, f32[32,768]{1,0:T(8,128)S(1)}) custom-call(bf16[8,27]{1,0:T(8,128)(2,1)S(1)} %bitcast.16, f32[8]{0:T(128)S(1)} %copy-done.6, bf16[16,27]{1,0:T(8,128)(2,1)S(1)} %bitcast.15, f32[2]{0:T(128)S(1)} %copy-done.7), custom_call_target="tpu_custom_call" | custom-call | flops 20971520 | bytes 4194304 | tf_op jit(solution)/shard_map/banded/pallas_call | solution.py:509
  18.9 0.0 collective-permute-done.5.refs_6_
  18.9 0.0 collective-permute-done.4.refs_5_
  18.9 0.0 collective-permute-done.3.refs_4_
  18.9 0.0 copy-done.2
  18.9 0.0 copy-start.3
  19.0 0.9 %copy-done.3 = bf16[1,1,1,32,4,4,128]{6,5,4,3,2,1,0:T(4,128)(2,1)S(1)} copy-done((bf16[1,1,1,32,4,4,128]{6,5,4,3,2,1,0:T(4,128)(2,1)S(1)}, bf16[1,1,1,32,4,4,128]{6,5,4,3,2,1,0:T(4,128)(2,1)}, u32[]{:S(2)}) %copy-start.3) | copy-done | bytes 131096
  19.8 9.5 %column.1 = (bf16[2,4,32,256]{3,2,1,0:T(8,128)(2,1)}, f32[1024,128]{1,0:T(8,128)}) custom-call(bf16[144,256]{1,0:T(8,128)(2,1)S(1)} %pack.1.refs_0_, bf16[144,256]{1,0:T(8,128)(2,1)S(1)} %collective-permute-done.refs_1_, bf16[144,256]{1,0:T(8,128)(2,1)S(1)} %collective-permute-done.1.refs_2_, bf16[144,256]{1,0:T(8,128)(2,1)S(1)} %collective-permute-done.2.refs_3_, ...), custom_call_target="tpu_custom_call" | custom-call | flops 1698693120 | bytes 4194304 | tf_op jit(solution)/shard_map/column/pallas_call | solution.py:560
Async XLA Ops:
  0.6 0.7 %copy-start.1 = (s32[1,1,1,16,1]{3,4,2,1,0:T(1,128)S(1)}, s32[1,1,1,16,1]{3,4,2,1,0:T(1,128)}, u32[]{:S(2)}) copy-start(s32[1,1,1,16,1]{3,4,2,1,0:T(1,128)} %param.13) | copy-start | bytes 196
  1.3 0.8 %copy-start = (bf16[4,32,256]{2,1,0:T(8,128)(2,1)S(1)}, bf16[4,32,256]{2,1,0:T(8,128)(2,1)}, u32[]{:S(2)}) copy-start(bf16[4,32,256]{2,1,0:T(8,128)(2,1)} %param.8) | copy-start | bytes 196612
  2.1 16.8 %copy-start.2 = (f32[1,1,1,32,2,4,4,128]{7,6,5,4,3,2,1,0:T(4,128)S(1)}, f32[1,1,1,32,2,4,4,128]{7,6,5,4,3,2,1,0:T(4,128)}, u32[]{:S(2)}) copy-start(f32[1,1,1,32,2,4,4,128]{7,6,5,4,3,2,1,0:T(4,128)} %param.14) | copy-start | bytes 1572868
  2.2 7.8 %collective-permute-start.2 = (bf16[144,256]{1,0:T(8,128)(2,1)S(1)}, bf16[144,256]{1,0:T(8,128)(2,1)S(1)}, u32[]{:S(2)}, u32[]{:S(2)}) collective-permute-start(bf16[144,256]{1,0:T(8,128)(2,1)S(1)} %pack.1.refs_0_), channel_id=1, source_target_pairs={{12,0},{0,4},{4,8},{8,12},{13,1},{1,5},{5,9},{9,13},{14,2},{2,6},{... | collective-permute-start | bytes 221192 | tf_op jit(solution)/shard_map/ppermute | solution.py:503
  5.3 7.5 %collective-permute-start.1 = (bf16[144,256]{1,0:T(8,128)(2,1)S(1)}, bf16[144,256]{1,0:T(8,128)(2,1)S(1)}, u32[]{:S(2)}, u32[]{:S(2)}) collective-permute-start(bf16[144,256]{1,0:T(8,128)(2,1)S(1)} %pack.1.refs_0_), channel_id=1, source_target_pairs={{8,0},{12,4},{0,8},{4,12},{9,1},{13,5},{1,9},{5,13},{10,2},{14,6},... | collective-permute-start | bytes 221192 | tf_op jit(solution)/shard_map/ppermute | solution.py:503
  7.9 5.2 %collective-permute-start = (bf16[144,256]{1,0:T(8,128)(2,1)S(1)}, bf16[144,256]{1,0:T(8,128)(2,1)S(1)}, u32[]{:S(2)}, u32[]{:S(2)}) collective-permute-start(bf16[144,256]{1,0:T(8,128)(2,1)S(1)} %pack.1.refs_0_), channel_id=1, source_target_pairs={{4,0},{8,4},{12,8},{0,12},{5,1},{9,5},{13,9},{1,13},{6,2},{10,6},{... | collective-permute-start | bytes 221192 | tf_op jit(solution)/shard_map/ppermute | solution.py:503
  13.1 5.8 %collective-permute-start.3 = (bf16[512,128]{1,0:T(8,128)(2,1)S(1)}, bf16[512,128]{1,0:T(8,128)(2,1)S(1)}, u32[]{:S(2)}, u32[]{:S(2)}) collective-permute-start(bf16[512,128]{1,0:T(8,128)(2,1)S(1)} %get-tuple-element.11), channel_id=1, source_target_pairs={{0,1},{1,0},{2,3},{3,2},{4,5},{5,4},{6,7},{7,6},{8,9},{9,8},{10,11... | collective-permute-start | bytes 393224 | tf_op jit(solution)/shard_map/ppermute | solution.py:548
  13.2 5.7 %collective-permute-start.4 = (bf16[32,256]{1,0:T(8,128)(2,1)S(1)}, bf16[32,256]{1,0:T(8,128)(2,1)S(1)}, u32[]{:S(2)}, u32[]{:S(2)}) collective-permute-start(bf16[32,256]{1,0:T(8,128)(2,1)S(1)} %get-tuple-element.12), channel_id=1, source_target_pairs={{0,2},{2,0},{1,3},{3,1},{4,6},{6,4},{5,7},{7,5},{8,10},{10,8},{9,1... | collective-permute-start | bytes 49160 | tf_op jit(solution)/shard_map/ppermute | solution.py:556
  14.7 4.2 %collective-permute-start.5 = (bf16[32,128]{1,0:T(8,128)(2,1)S(1)}, bf16[32,128]{1,0:T(8,128)(2,1)S(1)}, u32[]{:S(2)}, u32[]{:S(2)}) collective-permute-start(bf16[32,128]{1,0:T(8,128)(2,1)S(1)} %get-tuple-element.13), channel_id=1, source_target_pairs={{0,3},{1,2},{2,1},{3,0},{4,7},{5,6},{6,5},{7,4},{8,11},{9,10},{10,... | collective-permute-start | bytes 24584 | tf_op jit(solution)/shard_map/ppermute | solution.py:557
  15.0 0.7 %copy-start.4 = (bf16[27,2,8]{0,2,1:T(8,128)(2,1)S(1)}, bf16[27,2,8]{0,2,1:T(8,128)(2,1)}, u32[]{:S(2)}) copy-start(bf16[27,2,8]{0,2,1:T(8,128)(2,1)} %param.11) | copy-start | bytes 2596
  15.7 0.7 %copy-start.5 = (bf16[27,8,1]{0,1,2:T(8,128)(2,1)S(1)}, bf16[27,8,1]{0,1,2:T(8,128)(2,1)}, u32[]{:S(2)}) copy-start(bf16[27,8,1]{0,1,2:T(8,128)(2,1)} %param.9) | copy-start | bytes 1300
  16.4 0.7 %copy-start.6 = (f32[8]{0:T(128)S(1)}, f32[8]{0:T(128)}, u32[]{:S(2)}) copy-start(f32[8]{0:T(128)} %b1_ref.1) | copy-start | bytes 100
  17.1 0.7 %copy-start.7 = (f32[2]{0:T(128)S(1)}, f32[2]{0:T(128)}, u32[]{:S(2)}) copy-start(f32[2]{0:T(128)} %b2_ref.1) | copy-start | bytes 28
  18.9 0.9 %copy-start.3 = (bf16[1,1,1,32,4,4,128]{6,5,4,3,2,1,0:T(4,128)(2,1)S(1)}, bf16[1,1,1,32,4,4,128]{6,5,4,3,2,1,0:T(4,128)(2,1)}, u32[]{:S(2)}) copy-start(bf16[1,1,1,32,4,4,128]{6,5,4,3,2,1,0:T(4,128)(2,1)} %param.15) | copy-start | bytes 393220

commit v3 on v2

--- a/solution.py
+++ b/solution.py
@@ -23,6 +23,10 @@
 HBM = pl.BlockSpec(memory_space=pltpu.HBM)
 
 
+def in_hbm(array):
+    return pltpu.with_memory_space_constraint(array, pltpu.HBM)
+
+
 def step_index(values, width, count):
     index = jnp.zeros(values.shape, jnp.int32)
     for k in range(1, count):
@@ -47,27 +51,47 @@
     return dz, dy, tap - 9 * dz - 3 * dy
 
 
-def pack_kernel(density_ref, owners_ref, payload_ref, sem):
+def pack_kernel(density_ref, owners_ref, payload_ref, named_ref, sems):
     height, columns = density_ref.shape
-    copy = pltpu.make_async_copy(density_ref, payload_ref.at[0:height], sem)
-    copy.start()
-    named = owners_ref[...].astype(jnp.float32)
+    blocks = columns // BX
+    copies = [pltpu.make_async_copy(owners_ref, named_ref, sems.at[blocks])]
+    for k in range(blocks):
+        copies.append(
+            pltpu.make_async_copy(
+                density_ref.at[:, k * BX : (k + 1) * BX],
+                payload_ref.at[k * height : (k + 1) * height],
+                sems.at[k],
+            )
+        )
+    for copy in copies:
+        copy.start()
+    copies[0].wait()
+    named = named_ref[...].astype(jnp.float32)
     count = named.shape[1]
-    payload_ref[height : height + TILE, 0:BX] = jnp.concatenate(
+    payload_ref[blocks * height : blocks * height + TILE, :] = jnp.concatenate(
         [
             jnp.broadcast_to(named, (TILE, count)),
             jnp.zeros((TILE, BX - count), jnp.float32),
         ],
         axis=1,
     ).astype(jnp.bfloat16)
-    payload_ref[height : height + TILE, BX:columns] = jnp.zeros(
-        (TILE, columns - BX), jnp.bfloat16
-    )
-    copy.wait()
-
-
-def banded_kernel(dims, w1_ref, b1_ref, w2_ref, b2_ref, t1_ref, bias_ref, t2_ref, bias2_ref):
+    for copy in copies[1:]:
+        copy.wait()
+
+
+def banded_kernel(dims, *refs):
     window, count_gy = dims
+    sources, refs = refs[:4], refs[5:]
+    t1_ref, bias_ref, t2_ref, bias2_ref, *local, sems = refs
+    copies = [
+        pltpu.make_async_copy(source, target, sems.at[k])
+        for k, (source, target) in enumerate(zip(sources, local))
+    ]
+    for copy in copies:
+        copy.start()
+    for copy in copies:
+        copy.wait()
+    w1_ref, b1_ref, w2_ref, b2_ref = local
     g = lax.axis_index("gy")
     row, channel = iotas((TALL, CHANNELS))
     spread = one_hot((row & (CHANNELS - 1)) == channel)
@@ -129,45 +153,42 @@
 
 def edges_kernel(dims, *refs):
     count_gy, depth, rows, columns, few, count = dims
-    tiles, outs = refs[:few], refs[few:]
+    tiles, outs = refs[:few], refs[few + 1 :]
     g = lax.axis_index("gy")
     c = lax.axis_index("col")
-    block = pl.multiple_of((1 - c) * BX, BX)
-
-    def take(i, start, size, lanes):
+    height = depth * rows
+    block = (1 - c) * height
+
+    def take(i, start, size):
+        start = pl.ds(pl.multiple_of(start, TILE), size)
         if few > 1:
-            return tiles[i][pl.ds(start, size), lanes]
-        return tiles[0][i, pl.ds(start, size), lanes]
+            return tiles[i][start, :]
+        return tiles[0][i, start, :]
 
     def pair(i):
-        whole = pl.ds(0, columns)
-        some = pl.ds(block, BX)
         for k in range(2):
-            height = depth * rows
-            at = (2 * i + k) * height
-            if not isinstance(at, int):
-                at = pl.multiple_of(at, TILE)
-            outs[0][pl.ds(at, height), :] = take(2 * i + k, 0, height, some)
-        low, high = ([], []), ([], [])
+            at = pl.multiple_of((2 * i + k) * height, TILE)
+            outs[0][pl.ds(at, height), :] = take(2 * i + k, block, height)
+        low, high = [], []
         for k in range(2):
             for zz in range(depth):
-                for n, lanes in enumerate((whole, some)):
-                    first = take(2 * i + k, zz * rows, TILE, lanes).astype(jnp.float32)
-                    last = take(2 * i + k, (zz + 1) * rows - TILE, TILE, lanes).astype(jnp.float32)
-                    low[n].append(first[0:2])
-                    high[n].append(last[TILE - 2 :])
-        at = 2 * i * 2 * depth
-        if not isinstance(at, int):
-            at = pl.multiple_of(at, TILE)
-        for n in range(2):
-            first = jnp.concatenate(low[n], axis=0)
-            last = jnp.concatenate(high[n], axis=0)
-            if count_gy == 2:
-                send = jnp.where(g == 0, last, first)
-                outs[1 + n][pl.ds(at, TILE), :] = send.astype(jnp.bfloat16)
-            else:
-                outs[1 + n][pl.ds(at, TILE), :] = last.astype(jnp.bfloat16)
-                outs[3 + n][pl.ds(at, TILE), :] = first.astype(jnp.bfloat16)
+                first, last = [], []
+                for base in (0, height):
+                    at = base + zz * rows
+                    first.append(take(2 * i + k, at, TILE).astype(jnp.float32)[0:2])
+                    at = at + rows - TILE
+                    last.append(take(2 * i + k, at, TILE).astype(jnp.float32)[TILE - 2 :])
+                low.append(jnp.concatenate(first, axis=1))
+                high.append(jnp.concatenate(last, axis=1))
+        at = pl.multiple_of(2 * i * 2 * depth, TILE)
+        first, last = jnp.concatenate(low, axis=0), jnp.concatenate(high, axis=0)
+        sends = [jnp.where(g == 0, last, first)] if count_gy == 2 else [last, first]
+        for n, send in enumerate(sends):
+            send = send.astype(jnp.bfloat16)
+            outs[1 + 2 * n][pl.ds(at, TILE), :] = send
+            outs[2 + 2 * n][pl.ds(at, TILE), :] = jnp.where(
+                c == 0, send[:, BX:columns], send[:, 0:BX]
+            )
 
     if few > 1:
         for i in range(count // 2):
@@ -220,15 +241,15 @@
     biomass_copy = pltpu.make_async_copy(biomass_ref, biomass, sems.at[1])
     biomass_copy.start()
 
-    def tile_rows(i, start, size, lanes):
+    def tile_rows(i, start, size):
         if not isinstance(start, int):
             start = pl.multiple_of(start, TILE)
         if few > 1:
-            return tiles[i][pl.ds(start, size), lanes]
-        return tiles[0][i, pl.ds(start, size), lanes]
+            return tiles[i][pl.ds(start, size), :]
+        return tiles[0][i, pl.ds(start, size), :]
 
     def read_owners(i):
-        row = tile_rows(i, depth * rows, TILE, pl.ds(0, BX))
+        row = tile_rows(i, brick_columns * depth * rows, TILE)
         owner_rows[i] = row.astype(jnp.float32)[0:8].astype(jnp.int32)
 
     if few > 1:
@@ -239,8 +260,7 @@
     table_copy = pltpu.make_async_copy(owner_rows, owner_table, sems.at[2])
     table_copy.start()
 
-    def arrange(own, other):
-        left, right = own[:, 0:BX], own[:, BX:columns]
+    def arrange(left, right, other):
         return jnp.concatenate(
             [
                 jnp.where(c == 0, left, other),
@@ -252,7 +272,8 @@
 
     for k, pair in enumerate((top_refs, bottom_refs)):
         exists = (g > 0) if k == 0 else (g < count_gy - 1)
-        values = arrange(pair[0][...].astype(jnp.float32), pair[1][...].astype(jnp.float32))
+        own, other = pair[0][...].astype(jnp.float32), pair[1][...].astype(jnp.float32)
+        values = arrange(own[:, 0:BX], own[:, BX:columns], other)
         edge_rows[k] = values * exists.astype(jnp.float32)
 
     def moved(values):
@@ -273,11 +294,12 @@
         z = i * depth + zz
         halves = []
         for h in range(2):
-            own = tile_rows(i, zz * rows + h * HALF, HALF, pl.ds(0, columns))
+            at = zz * rows + h * HALF
+            own = [tile_rows(i, k * depth * rows + at, HALF) for k in range(2)]
             at = z * rows + h * HALF
             if not isinstance(at, int):
                 at = pl.multiple_of(at, TILE)
-            values = arrange(own, x_ref[pl.ds(at, HALF), :]).astype(jnp.float32)
+            values = arrange(*own, x_ref[pl.ds(at, HALF), :]).astype(jnp.float32)
             halves.append(values if valid is None else values * valid)
         top, bottom = edge_pair(0, 2 * z), edge_pair(1, 2 * z)
         if valid is not None:
@@ -447,19 +469,24 @@
             [state[rows_of(2 * size, size + z * BY + y), :] for y in range(BY)]
             for z in range(depth)
         ]
+        pore = [[arrived[rows_of(2 * size, z * 8 + y), :] for y in range(BY)] for z in range(depth)]
+        organic = [
+            [0.3 * arrived[rows_of(2 * size, z * 8 + BY + y), :] for y in range(BY)]
+            for z in range(depth)
+        ]
+        quarter = [[mass[rows_of(size, z * BY + y), :] for y in range(BY)] for z in range(depth)]
+        slow = [[0.12 * p for p in row] for row in pore]
+        fast = [[0.16 * p for p in row] for row in pore]
         for _ in range(STEPS):
             carbon_new = [[None] * BY for _ in range(depth)]
             oxygen_new = [[None] * BY for _ in range(depth)]
             for z, y in grid:
                 doc, oxy = carbon[z][y], oxygen[z][y]
-                pore = arrived[rows_of(2 * size, z * 8 + y), :]
-                organic = arrived[rows_of(2 * size, z * 8 + BY + y), :]
-                quarter = mass[rows_of(size, z * BY + y), :]
-                uptake = (quarter * doc * oxy) / ((0.5 + jnp.abs(doc)) * (0.3 + jnp.abs(oxy)))
-                carbon_new[z][y] = doc + (0.12 * pore) * laplace(carbon, z, y) + (
-                    0.3 * organic - uptake
-                )
-                oxygen_new[z][y] = oxy + (0.16 * pore) * laplace(oxygen, z, y) - uptake
+                uptake = quarter[z][y] * doc * oxy
+                uptake = uptake / ((0.5 + jnp.abs(doc)) * (0.3 + jnp.abs(oxy)))
+                gain = organic[z][y] - uptake
+                carbon_new[z][y] = doc + slow[z][y] * laplace(carbon, z, y) + gain
+                oxygen_new[z][y] = oxy + fast[z][y] * laplace(oxygen, z, y) - uptake
             carbon, oxygen = carbon_new, oxygen_new
         for z, y in grid:
             state[rows_of(2 * size, z * BY + y), :] = carbon[z][y]
@@ -489,13 +516,16 @@
 
     payload = pl.pallas_call(
         pack_kernel,
-        out_shape=shape((height + TILE, columns), bf16),
-        in_specs=[HBM, VMEM],
+        out_shape=shape((columns // BX * height + TILE, BX), bf16),
+        in_specs=[HBM, HBM],
         out_specs=VMEM,
-        scratch_shapes=[pltpu.SemaphoreType.DMA],
+        scratch_shapes=[
+            pltpu.VMEM((1, brick_count), jnp.int32),
+            pltpu.SemaphoreType.DMA((columns // BX + 1,)),
+        ],
         compiler_params=pltpu.CompilerParams(vmem_limit_bytes=4 * 2**20),
         name="pack",
-    )(density.reshape(height, columns), owners.reshape(1, brick_count))
+    )(in_hbm(density.reshape(height, columns)), in_hbm(owners.reshape(1, brick_count)))
 
     few = count_gz if count_gz == segment else 1
     if few > 1:
@@ -514,29 +544,37 @@
             shape((6 * HALF, 3 * TALL), bf16),
             shape((2 * HALF, 2 * window), f32),
         ),
-        in_specs=[VMEM, SMEM, VMEM, SMEM],
+        in_specs=[HBM, HBM, HBM, HBM, pl.BlockSpec(memory_space=pl.ANY)],
         out_specs=(VMEM, VMEM, VMEM, VMEM),
+        scratch_shapes=[
+            pltpu.VMEM((CHANNELS, 27), bf16),
+            pltpu.SMEM((CHANNELS,), f32),
+            pltpu.VMEM((2 * CHANNELS, 27), bf16),
+            pltpu.SMEM((2,), f32),
+            pltpu.SemaphoreType.DMA((4,)),
+        ],
         compiler_params=pltpu.CompilerParams(vmem_limit_bytes=16 * 2**20),
         cost_estimate=pl.CostEstimate(
             flops=20 * 2**20, bytes_accessed=4 * 2**20, transcendentals=0
         ),
         name="banded",
     )(
-        first_kernel.transpose(2, 1, 0).reshape(CHANNELS, 27),
-        first_bias,
-        second_kernel.transpose(1, 2, 0).reshape(2 * CHANNELS, 27),
-        second_bias,
+        in_hbm(first_kernel.transpose(2, 1, 0).reshape(CHANNELS, 27)),
+        in_hbm(first_bias),
+        in_hbm(second_kernel.transpose(1, 2, 0).reshape(2 * CHANNELS, 27)),
+        in_hbm(second_bias),
+        payload,
     )
 
     edge_shapes = [shape((2 * depths, columns), bf16), shape((2 * depths, BX), bf16)]
     sent = pl.pallas_call(
         functools.partial(edges_kernel, (count_gy, depth, rows, columns, few, count_gz)),
         out_shape=[shape((depths * rows, BX), bf16)] + edge_shapes * (1 if count_gy == 2 else 2),
-        in_specs=[VMEM] * few,
+        in_specs=[VMEM] * few + [pl.BlockSpec(memory_space=pl.ANY)],
         out_specs=[VMEM] * (3 if count_gy == 2 else 5),
         compiler_params=pltpu.CompilerParams(vmem_limit_bytes=16 * 2**20),
         name="edges",
-    )(*tiles)
+    )(*tiles, bias2)
 
     def over(pairs):
         return [
@@ -598,8 +636,8 @@
         bias,
         t2,
         bias2,
-        solutes.reshape(slots * 2 * cells, BX),
-        biomass.reshape(slots * cells, BX),
+        in_hbm(solutes.reshape(slots * 2 * cells, BX)),
+        in_hbm(biomass.reshape(slots * cells, BX)),
     )
     return fractions, solutes_next.reshape(solutes.shape)
 

time: 29.6 us -> 26.3 us (0.89)
  local copies, waits for them, and re-layouts: 5.07 us -> 0 us
  waiting for transfers between devices: 3.83 us -> 4.87 us
  Pallas kernels: 10.8 us -> 11.6 us
    unnamed x16 -> x0, local copies, waits for them, and re-layouts: 5.07 us -> none
    ppermute x1, waiting for transfers between devices: 0.01 us -> 2.81 us  [per_device(): edges.append(lax.ppermute(sent[2 + 2 * k], ('gy', 'col'), over(pairs)))]
    ppermute x3, waiting for transfers between devices: 3.83 us -> 2.05 us  [per_device(): lax.ppermute(payload, 'gz', [((i + s) % count_gz, i) for i in range(count...]
    pallas_call x1, Pallas kernels: 0.07 us -> 0.82 us  [per_device(): pl.pallas_call(pack_kernel, out_shape=shape((columns // BX * height + TIL...]
    pallas_call x1, Pallas kernels: 1.16 us -> 1.47 us  [per_device(): pl.pallas_call(functools.partial(banded_kernel, (window, count_gy)), out_...]
  transfers between devices with their start and end apart: 6 -> 6, of which waited for: 3 -> 3; matrix products, arithmetic and copies ran while one was open for 0% -> 0% of each run, Pallas kernels for 4% -> 6%
where the time goes in v3:
time: 26.3 us; the launch traced here: 26 us
  Pallas kernels  11.6 us (44%)
  starting transfers between devices  8.95 us (34%)
  waiting for transfers between devices  4.87 us (19%)
  between operations  0.67 us (3%)
    pallas_call x1, Pallas kernels, per_device(): pl.pallas_call(functools.partial(column_kernel, (count_gz, count_gy, dept...  9.24 us
    ppermute x3, starting transfers between devices, per_device(): lax.ppermute(payload, 'gz', [((i + s) % count_gz, i) for i in range(count...  7.01 us
    ppermute x1, waiting for transfers between devices, per_device(): edges.append(lax.ppermute(sent[2 + 2 * k], ('gy', 'col'), over(pairs)))  2.81 us
    ppermute x3, waiting for transfers between devices, per_device(): lax.ppermute(payload, 'gz', [((i + s) % count_gz, i) for i in range(count...  2.05 us
    ppermute x1, starting transfers between devices, per_device(): edges.append(lax.ppermute(sent[1 + 2 * k], 'gy', pairs))  1.6 us
    pallas_call x1, Pallas kernels, per_device(): pl.pallas_call(functools.partial(banded_kernel, (window, count_gy)), out_...  1.47 us
    pallas_call x1, Pallas kernels, per_device(): pl.pallas_call(pack_kernel, out_shape=shape((columns // BX * height + TIL...  0.82 us
  transfers between devices with their start and end apart: 6, of which 3 were waited for; matrix products, arithmetic and copies ran while one was open for 0% of the time, Pallas kernels for 6%

profile of v3, /device:TPU:0, one launch (start us, length us, event | category | flops | bytes accessed | tf_op | source)
XLA Modules:
  0.0 26.0 jit_solution(8867890104991406236)
XLA Ops:
  0.6 0.8 %pack.1.refs_4_.refs_0_ = bf16[272,128]{1,0:T(8,128)(2,1)S(1)} custom-call(bf16[128,256]{1,0:T(8,128)(2,1)} %bitcast.11, s32[1,16]{1,0:T(1,128)} %bitcast.12), custom_call_target="tpu_custom_call" | custom-call | tf_op jit(solution)/shard_map/pack/pallas_call | solution.py:517
  1.5 3.1 %collective-permute-start.2 = (bf16[272,128]{1,0:T(8,128)(2,1)S(1)}, bf16[272,128]{1,0:T(8,128)(2,1)S(1)}, u32[]{:S(2)}, u32[]{:S(2)}) collective-permute-start(bf16[272,128]{1,0:T(8,128)(2,1)S(1)} %pack.1.refs_4_.refs_0_), channel_id=1, source_target_pairs={{12,0},{0,4},{4,8},{8,12},{13,1},{1,5},{5,9},{9,13},{14,2},{2,6},{... | collective-permute-start | bytes 208904 | tf_op jit(solution)/shard_map/ppermute | solution.py:533
  4.5 2.6 %collective-permute-start.1 = (bf16[272,128]{1,0:T(8,128)(2,1)S(1)}, bf16[272,128]{1,0:T(8,128)(2,1)S(1)}, u32[]{:S(2)}, u32[]{:S(2)}) collective-permute-start(bf16[272,128]{1,0:T(8,128)(2,1)S(1)} %pack.1.refs_4_.refs_0_), channel_id=1, source_target_pairs={{8,0},{12,4},{0,8},{4,12},{9,1},{13,5},{1,9},{5,13},{10,2},{14,6},... | collective-permute-start | bytes 208904 | tf_op jit(solution)/shard_map/ppermute | solution.py:533
  7.1 1.3 %collective-permute-start = (bf16[272,128]{1,0:T(8,128)(2,1)S(1)}, bf16[272,128]{1,0:T(8,128)(2,1)S(1)}, u32[]{:S(2)}, u32[]{:S(2)}) collective-permute-start(bf16[272,128]{1,0:T(8,128)(2,1)S(1)} %pack.1.refs_4_.refs_0_), channel_id=1, source_target_pairs={{4,0},{8,4},{12,8},{0,12},{5,1},{9,5},{13,9},{1,13},{6,2},{10,6},{... | collective-permute-start | bytes 208904 | tf_op jit(solution)/shard_map/ppermute | solution.py:533
  8.5 1.5 %banded.1 = (bf16[144,192]{1,0:T(8,128)(2,1)S(1)}, f32[144,768]{1,0:T(8,128)S(1)}, bf16[96,432]{1,0:T(8,128)(2,1)S(1)}, f32[32,768]{1,0:T(8,128)S(1)}) custom-call(bf16[8,27]{1,0:T(8,128)(2,1)} %bitcast.16, f32[8]{0:T(128)} %refs_1_.1, bf16[16,27]{1,0:T(8,128)(2,1)} %bitcast.15, f32[2]{0:T(128)} %refs_3_.1, bf16[272,128]{1,0:T(8,128)(2,1)S(1)} %pack.1.refs_4_.refs_0_), custom_call_target="tpu_custom_call" | custom-call | flops 20971520 | bytes 4194304 | tf_op jit(solution)/shard_map/banded/pallas_call | solution.py:539
  9.9 0.0 collective-permute-done.2.refs_3_
  10.0 1.9 %collective-permute-done.1.refs_2_ = bf16[272,128]{1,0:T(8,128)(2,1)S(1)} collective-permute-done((bf16[272,128]{1,0:T(8,128)(2,1)S(1)}, bf16[272,128]{1,0:T(8,128)(2,1)S(1)}, u32[]{:S(2)}, u32[]{:S(2)}) %collective-permute-start.1) | collective-permute-done | bytes 69664 | tf_op jit(solution)/shard_map/ppermute | solution.py:533
  11.8 0.2 collective-permute-done.refs_1_
  12.0 0.1 collective-permute-start.3
  12.1 1.6 %collective-permute-start.4 = (bf16[32,256]{1,0:T(8,128)(2,1)S(1)}, bf16[32,256]{1,0:T(8,128)(2,1)S(1)}, u32[]{:S(2)}, u32[]{:S(2)}) collective-permute-start(bf16[32,256]{1,0:T(8,128)(2,1)S(1)} %get-tuple-element.13), channel_id=1, source_target_pairs={{0,2},{2,0},{1,3},{3,1},{4,6},{6,4},{5,7},{7,5},{8,10},{10,8},{9,1... | collective-permute-start | bytes 49160 | tf_op jit(solution)/shard_map/ppermute | solution.py:594
  13.7 0.3 %collective-permute-start.5 = (bf16[32,128]{1,0:T(8,128)(2,1)S(1)}, bf16[32,128]{1,0:T(8,128)(2,1)S(1)}, u32[]{:S(2)}, u32[]{:S(2)}) collective-permute-start(bf16[32,128]{1,0:T(8,128)(2,1)S(1)} %get-tuple-element.14), channel_id=1, source_target_pairs={{0,3},{1,2},{2,1},{3,0},{4,7},{5,6},{6,5},{7,4},{8,11},{9,10},{10,... | collective-permute-start | bytes 24584 | tf_op jit(solution)/shard_map/ppermute | solution.py:595
  14.0 2.8 %collective-permute-done.5.refs_6_ = bf16[32,128]{1,0:T(8,128)(2,1)S(1)} collective-permute-done((bf16[32,128]{1,0:T(8,128)(2,1)S(1)}, bf16[32,128]{1,0:T(8,128)(2,1)S(1)}, u32[]{:S(2)}, u32[]{:S(2)}) %collective-permute-start.5) | collective-permute-done | bytes 8224 | tf_op jit(solution)/shard_map/ppermute | solution.py:595
  16.8 0.0 collective-permute-done.4.refs_5_
  16.8 0.0 collective-permute-done.3.refs_4_
  16.8 9.2 %column.1 = (bf16[2,4,32,256]{3,2,1,0:T(8,128)(2,1)}, f32[1024,128]{1,0:T(8,128)}) custom-call(bf16[272,128]{1,0:T(8,128)(2,1)S(1)} %pack.1.refs_4_.refs_0_, bf16[272,128]{1,0:T(8,128)(2,1)S(1)} %collective-permute-done.refs_1_, bf16[272,128]{1,0:T(8,128)(2,1)S(1)} %collective-permute-done.1.refs_2_, bf16[272,128]{1,0:T(8,128)(2,1)S(1)} %collective-permute-done.2.refs_3_, ...), custom_call_target="tpu_custom_call" | custom-call | flops 1698693120 | bytes 4194304 | tf_op jit(solution)/shard_map/column/pallas_call | solution.py:598
  (1 shorter events, 0.0 us)
Async XLA Ops:
  1.5 8.5 %collective-permute-start.2 = (bf16[272,128]{1,0:T(8,128)(2,1)S(1)}, bf16[272,128]{1,0:T(8,128)(2,1)S(1)}, u32[]{:S(2)}, u32[]{:S(2)}) collective-permute-start(bf16[272,128]{1,0:T(8,128)(2,1)S(1)} %pack.1.refs_4_.refs_0_), channel_id=1, source_target_pairs={{12,0},{0,4},{4,8},{8,12},{13,1},{1,5},{5,9},{9,13},{14,2},{2,6},{... | collective-permute-start | bytes 208904 | tf_op jit(solution)/shard_map/ppermute | solution.py:533
  4.5 7.3 %collective-permute-start.1 = (bf16[272,128]{1,0:T(8,128)(2,1)S(1)}, bf16[272,128]{1,0:T(8,128)(2,1)S(1)}, u32[]{:S(2)}, u32[]{:S(2)}) collective-permute-start(bf16[272,128]{1,0:T(8,128)(2,1)S(1)} %pack.1.refs_4_.refs_0_), channel_id=1, source_target_pairs={{8,0},{12,4},{0,8},{4,12},{9,1},{13,5},{1,9},{5,13},{10,2},{14,6},... | collective-permute-start | bytes 208904 | tf_op jit(solution)/shard_map/ppermute | solution.py:533
  7.1 4.9 %collective-permute-start = (bf16[272,128]{1,0:T(8,128)(2,1)S(1)}, bf16[272,128]{1,0:T(8,128)(2,1)S(1)}, u32[]{:S(2)}, u32[]{:S(2)}) collective-permute-start(bf16[272,128]{1,0:T(8,128)(2,1)S(1)} %pack.1.refs_4_.refs_0_), channel_id=1, source_target_pairs={{4,0},{8,4},{12,8},{0,12},{5,1},{9,5},{13,9},{1,13},{6,2},{10,6},{... | collective-permute-start | bytes 208904 | tf_op jit(solution)/shard_map/ppermute | solution.py:533
  12.0 4.8 %collective-permute-start.3 = (bf16[512,128]{1,0:T(8,128)(2,1)S(1)}, bf16[512,128]{1,0:T(8,128)(2,1)S(1)}, u32[]{:S(2)}, u32[]{:S(2)}) collective-permute-start(bf16[512,128]{1,0:T(8,128)(2,1)S(1)} %get-tuple-element.12), channel_id=1, source_target_pairs={{0,1},{1,0},{2,3},{3,2},{4,5},{5,4},{6,7},{7,6},{8,9},{9,8},{10,11... | collective-permute-start | bytes 393224 | tf_op jit(solution)/shard_map/ppermute | solution.py:586
  12.1 4.7 %collective-permute-start.4 = (bf16[32,256]{1,0:T(8,128)(2,1)S(1)}, bf16[32,256]{1,0:T(8,128)(2,1)S(1)}, u32[]{:S(2)}, u32[]{:S(2)}) collective-permute-start(bf16[32,256]{1,0:T(8,128)(2,1)S(1)} %get-tuple-element.13), channel_id=1, source_target_pairs={{0,2},{2,0},{1,3},{3,1},{4,6},{6,4},{5,7},{7,5},{8,10},{10,8},{9,1... | collective-permute-start | bytes 49160 | tf_op jit(solution)/shard_map/ppermute | solution.py:594
  13.7 3.1 %collective-permute-start.5 = (bf16[32,128]{1,0:T(8,128)(2,1)S(1)}, bf16[32,128]{1,0:T(8,128)(2,1)S(1)}, u32[]{:S(2)}, u32[]{:S(2)}) collective-permute-start(bf16[32,128]{1,0:T(8,128)(2,1)S(1)} %get-tuple-element.14), channel_id=1, source_target_pairs={{0,3},{1,2},{2,1},{3,0},{4,7},{5,6},{6,5},{7,4},{8,11},{9,10},{10,... | collective-permute-start | bytes 24584 | tf_op jit(solution)/shard_map/ppermute | solution.py:595

commit v4 on v3

--- a/solution.py
+++ b/solution.py
@@ -17,6 +17,7 @@
 PART = 3 * HALF + TILE
 TALL = REACH * CHANNELS
 OUTSIDE = -3e38
+OWNER_ROW = 6
 
 VMEM = pl.BlockSpec(memory_space=pltpu.VMEM)
 SMEM = pl.BlockSpec(memory_space=pltpu.SMEM)
@@ -51,7 +52,17 @@
     return dz, dy, tap - 9 * dz - 3 * dy
 
 
-def pack_kernel(density_ref, owners_ref, payload_ref, named_ref, sems):
+def swap_lanes(c, row, lane, first, sender):
+    low = (c != 0) if sender else (c == 0)
+    place = row - first
+    return (place >= 0) & (place < 2) & (lane == jnp.where(low, place, BX - 2 + place))
+
+
+def edges_kernel(dims, density_ref, owners_ref, own_ref, misc_ref, x_ref, *refs):
+    count_gy, depth, rows, directions = dims
+    sends, (named_ref, sems) = refs[: 2 * directions], refs[2 * directions :]
+    g = lax.axis_index("gy")
+    c = lax.axis_index("col")
     height, columns = density_ref.shape
     blocks = columns // BX
     copies = [pltpu.make_async_copy(owners_ref, named_ref, sems.at[blocks])]
@@ -59,24 +70,68 @@
         copies.append(
             pltpu.make_async_copy(
                 density_ref.at[:, k * BX : (k + 1) * BX],
-                payload_ref.at[k * height : (k + 1) * height],
+                own_ref.at[k * height : (k + 1) * height],
                 sems.at[k],
             )
         )
     for copy in copies:
         copy.start()
+    row, lane = iotas((TILE, BX))
     copies[0].wait()
     named = named_ref[...].astype(jnp.float32)
     count = named.shape[1]
-    payload_ref[blocks * height : blocks * height + TILE, :] = jnp.concatenate(
+    named = jnp.concatenate(
         [
             jnp.broadcast_to(named, (TILE, count)),
             jnp.zeros((TILE, BX - count), jnp.float32),
         ],
         axis=1,
-    ).astype(jnp.bfloat16)
+    )
+    misc_ref[...] = jnp.where(row == OWNER_ROW, named, 0.0).astype(jnp.bfloat16)
     for copy in copies[1:]:
         copy.wait()
+
+    def columns_of(first, values):
+        pick = one_hot(swap_lanes(c, row, lane, first, True))
+        return lax.dot_general(
+            pick, values, (((1,), (1,)), ((), ())), preferred_element_type=jnp.float32
+        ).astype(jnp.bfloat16)
+
+    x_ref[...] = columns_of(
+        0, own_ref[pl.ds(pl.multiple_of((1 - c) * height, TILE), height), :]
+    )
+    first, last = [], []
+    for k in range(blocks):
+        ends = ([], [])
+        for zz in range(depth):
+            at = k * height + zz * rows
+            ends[0].append(own_ref[at : at + TILE, :].astype(jnp.float32)[0:2])
+            at = at + rows - TILE
+            ends[1].append(own_ref[at : at + TILE, :].astype(jnp.float32)[TILE - 2 :])
+        first.append(jnp.concatenate(ends[0], axis=0))
+        last.append(jnp.concatenate(ends[1], axis=0))
+    if directions == 1:
+        chosen = [[jnp.where(g == 0, low, high) for low, high in zip(last, first)]]
+    else:
+        chosen = [last, first]
+    for d, pair in enumerate(chosen):
+        sends[2 * d][...] = jnp.concatenate(pair, axis=0).astype(jnp.bfloat16)
+        near = jnp.where(c == 0, pair[1], pair[0])
+        near = jnp.concatenate([near, jnp.zeros((BX - near.shape[0], BX), jnp.float32)], axis=0)
+        sends[2 * d + 1][...] = columns_of(2 + 2 * d, near.astype(jnp.bfloat16))
+
+
+def pack_kernel(directions, own_ref, misc_ref, x_ref, *refs):
+    received, (payload_ref, edge_ref) = refs[: 2 * directions], refs[2 * directions :]
+    height = own_ref.shape[0]
+    payload_ref[0:height, :] = own_ref[...]
+    misc = misc_ref[...] + x_ref[...]
+    for d in range(directions):
+        misc = misc + received[2 * d + 1][...]
+    for d, value in enumerate([received[2 * k][...] for k in range(directions)] + [misc]):
+        at = d * TILE
+        edge_ref[at : at + TILE, :] = value
+        payload_ref[height + at : height + at + TILE, :] = value
 
 
 def banded_kernel(dims, *refs):
@@ -151,65 +206,15 @@
     bias2_ref[...] = jnp.where(((row >> 2) & 1) == 0, b2_ref[0], b2_ref[1])
 
 
-def edges_kernel(dims, *refs):
-    count_gy, depth, rows, columns, few, count = dims
-    tiles, outs = refs[:few], refs[few + 1 :]
-    g = lax.axis_index("gy")
-    c = lax.axis_index("col")
-    height = depth * rows
-    block = (1 - c) * height
-
-    def take(i, start, size):
-        start = pl.ds(pl.multiple_of(start, TILE), size)
-        if few > 1:
-            return tiles[i][start, :]
-        return tiles[0][i, start, :]
-
-    def pair(i):
-        for k in range(2):
-            at = pl.multiple_of((2 * i + k) * height, TILE)
-            outs[0][pl.ds(at, height), :] = take(2 * i + k, block, height)
-        low, high = [], []
-        for k in range(2):
-            for zz in range(depth):
-                first, last = [], []
-                for base in (0, height):
-                    at = base + zz * rows
-                    first.append(take(2 * i + k, at, TILE).astype(jnp.float32)[0:2])
-                    at = at + rows - TILE
-                    last.append(take(2 * i + k, at, TILE).astype(jnp.float32)[TILE - 2 :])
-                low.append(jnp.concatenate(first, axis=1))
-                high.append(jnp.concatenate(last, axis=1))
-        at = pl.multiple_of(2 * i * 2 * depth, TILE)
-        first, last = jnp.concatenate(low, axis=0), jnp.concatenate(high, axis=0)
-        sends = [jnp.where(g == 0, last, first)] if count_gy == 2 else [last, first]
-        for n, send in enumerate(sends):
-            send = send.astype(jnp.bfloat16)
-            outs[1 + 2 * n][pl.ds(at, TILE), :] = send
-            outs[2 + 2 * n][pl.ds(at, TILE), :] = jnp.where(
-                c == 0, send[:, BX:columns], send[:, 0:BX]
-            )
-
-    if few > 1:
-        for i in range(count // 2):
-            pair(i)
-    else:
-        pl.loop(0, count // 2)(pair)
-
-
 def column_kernel(dims, few, *refs):
-    count_gz, count_gy, depth, rows, columns, segment, slots = dims
-    tiles, refs = refs[:few], refs[few:]
-    x_ref, refs = refs[0], refs[1:]
-    top_refs, refs = refs[:2], refs[2:]
-    if count_gy == 2:
-        bottom_refs = top_refs
-    else:
-        bottom_refs, refs = refs[:2], refs[2:]
+    count_gz, count_gy, depth, rows, columns, segment, slots, directions = dims
+    count = few + 1 if few > 1 else 1
+    tiles, refs = refs[:count], refs[count:]
     t1_ref, bias_ref, t2_ref, bias2_ref, solutes_ref, biomass_ref, *refs = refs
     fractions_ref, next_ref, *refs = refs
     (
         edge_rows,
+        beside,
         shifted,
         hidden,
         bricks,
@@ -248,17 +253,11 @@
             return tiles[i][pl.ds(start, size), :]
         return tiles[0][i, pl.ds(start, size), :]
 
-    def read_owners(i):
-        row = tile_rows(i, brick_columns * depth * rows, TILE)
-        owner_rows[i] = row.astype(jnp.float32)[0:8].astype(jnp.int32)
-
-    if few > 1:
-        for i in range(count_gz):
-            read_owners(i)
-    else:
-        pl.loop(0, count_gz)(read_owners)
-    table_copy = pltpu.make_async_copy(owner_rows, owner_table, sems.at[2])
-    table_copy.start()
+    def edge_tile(i, k):
+        at = brick_columns * depth * rows + k * TILE
+        if few > 1 and tiles[i].shape[0] <= at:
+            return tiles[count_gz][k * TILE : (k + 1) * TILE, :]
+        return tile_rows(i, at, TILE)
 
     def arrange(left, right, other):
         return jnp.concatenate(
@@ -270,11 +269,40 @@
             axis=1,
         )
 
-    for k, pair in enumerate((top_refs, bottom_refs)):
-        exists = (g > 0) if k == 0 else (g < count_gy - 1)
-        own, other = pair[0][...].astype(jnp.float32), pair[1][...].astype(jnp.float32)
-        values = arrange(own[:, 0:BX], own[:, BX:columns], other)
-        edge_rows[k] = values * exists.astype(jnp.float32)
+    small_row, small_lane = iotas((TILE, BX))
+
+    def unpack(i):
+        misc = edge_tile(i, directions)
+        owner_rows[i] = misc.astype(jnp.float32)[0:8].astype(jnp.int32)
+
+        def columns_of(first):
+            pick = one_hot(swap_lanes(c, small_row, small_lane, first, False))
+            return lax.dot_general(
+                misc, pick, (((0,), (0,)), ((), ())), preferred_element_type=jnp.float32
+            )
+
+        at = i * (depth * rows)
+        if not isinstance(at, int):
+            at = pl.multiple_of(at, TILE)
+        beside[pl.ds(at, depth * rows), :] = columns_of(0).astype(jnp.bfloat16)
+        at = i * (2 * depth)
+        if not isinstance(at, int):
+            at = pl.multiple_of(at, 8)
+        sides = []
+        for d in range(directions):
+            pair = edge_tile(i, d).astype(jnp.float32)
+            corner = columns_of(2 + 2 * d)[0 : 2 * depth]
+            sides.append(arrange(pair[0 : 2 * depth], pair[2 * depth :], corner))
+        edge_rows[0, pl.ds(at, 2 * depth), :] = jnp.where(g > 0, sides[0], 0.0)
+        edge_rows[1, pl.ds(at, 2 * depth), :] = jnp.where(g < count_gy - 1, sides[-1], 0.0)
+
+    if few > 1:
+        for i in range(count_gz):
+            unpack(i)
+    else:
+        pl.loop(0, count_gz)(unpack)
+    table_copy = pltpu.make_async_copy(owner_rows, owner_table, sems.at[2])
+    table_copy.start()
 
     def moved(values):
         lane = lax.broadcasted_iota(jnp.int32, values.shape, 1)
@@ -299,7 +327,7 @@
             at = z * rows + h * HALF
             if not isinstance(at, int):
                 at = pl.multiple_of(at, TILE)
-            values = arrange(*own, x_ref[pl.ds(at, HALF), :]).astype(jnp.float32)
+            values = arrange(*own, beside[pl.ds(at, HALF), :]).astype(jnp.float32)
             halves.append(values if valid is None else values * valid)
         top, bottom = edge_pair(0, 2 * z), edge_pair(1, 2 * z)
         if valid is not None:
@@ -417,7 +445,7 @@
         tile = lax.rem(first_tile + i, count_gz)
         rank = jnp.int32(0)
         for b in range(brick_count):
-            mine = owner_table[i, 0, b] == z_index
+            mine = owner_table[i, OWNER_ROW, b] == z_index
 
             @pl.when(mine)
             def _():
@@ -514,25 +542,57 @@
     bf16, f32 = jnp.bfloat16, jnp.float32
     shape = jax.ShapeDtypeStruct
 
-    payload = pl.pallas_call(
-        pack_kernel,
-        out_shape=shape((columns // BX * height + TILE, BX), bf16),
+    def over(pairs):
+        return [
+            (gy * count_col + col, to * count_col + 1 - col)
+            for gy, to in pairs
+            for col in range(count_col)
+        ]
+
+    if count_gy == 2:
+        ways = [[(0, 1), (1, 0)]]
+    else:
+        up = [(i, i + 1) for i in range(count_gy - 1)]
+        ways = [up, [(j, i) for i, j in up]]
+    directions = len(ways)
+    blocks = columns // BX
+    own, misc, near, *sent = pl.pallas_call(
+        functools.partial(edges_kernel, (count_gy, depth, rows, directions)),
+        out_shape=[shape((blocks * height, BX), bf16)] + [shape((TILE, BX), bf16)] * (2 + 2 * directions),
         in_specs=[HBM, HBM],
-        out_specs=VMEM,
+        out_specs=[VMEM] * (3 + 2 * directions),
         scratch_shapes=[
             pltpu.VMEM((1, brick_count), jnp.int32),
-            pltpu.SemaphoreType.DMA((columns // BX + 1,)),
+            pltpu.SemaphoreType.DMA((blocks + 1,)),
         ],
         compiler_params=pltpu.CompilerParams(vmem_limit_bytes=4 * 2**20),
+        name="edges",
+    )(in_hbm(density.reshape(height, columns)), in_hbm(owners.reshape(1, brick_count)))
+
+    received = []
+    for d, pairs in enumerate(ways):
+        received.append(lax.ppermute(sent[2 * d], "gy", pairs))
+        received.append(lax.ppermute(sent[2 * d + 1], ("gy", "col"), over(pairs)))
+    near = lax.ppermute(near, "col", [(0, 1), (1, 0)])
+    payload, cells_around = pl.pallas_call(
+        functools.partial(pack_kernel, directions),
+        out_shape=[
+            shape((blocks * height + (directions + 1) * TILE, BX), bf16),
+            shape(((directions + 1) * TILE, BX), bf16),
+        ],
+        in_specs=[VMEM] * (3 + 2 * directions),
+        out_specs=[VMEM] * 2,
+        compiler_params=pltpu.CompilerParams(vmem_limit_bytes=4 * 2**20),
         name="pack",
-    )(in_hbm(density.reshape(height, columns)), in_hbm(owners.reshape(1, brick_count)))
-
-    few = count_gz if count_gz == segment else 1
+    )(own, misc, near, *received)
+
+    def turned(array, s):
+        return lax.ppermute(array, "gz", [((i + s) % count_gz, i) for i in range(count_gz)])
+
+    few = count_gz if count_gz == 4 else 1
     if few > 1:
-        tiles = [payload] + [
-            lax.ppermute(payload, "gz", [((i + s) % count_gz, i) for i in range(count_gz)])
-            for s in range(1, count_gz)
-        ]
+        tiles = [payload, turned(payload, 1), turned(own, 2), turned(payload, 3)]
+        tiles.append(turned(cells_around, 2))
     else:
         tiles = [lax.all_gather(payload, "gz", axis=0, tiled=False)]
 
@@ -566,47 +626,22 @@
         payload,
     )
 
-    edge_shapes = [shape((2 * depths, columns), bf16), shape((2 * depths, BX), bf16)]
-    sent = pl.pallas_call(
-        functools.partial(edges_kernel, (count_gy, depth, rows, columns, few, count_gz)),
-        out_shape=[shape((depths * rows, BX), bf16)] + edge_shapes * (1 if count_gy == 2 else 2),
-        in_specs=[VMEM] * few + [pl.BlockSpec(memory_space=pl.ANY)],
-        out_specs=[VMEM] * (3 if count_gy == 2 else 5),
-        compiler_params=pltpu.CompilerParams(vmem_limit_bytes=16 * 2**20),
-        name="edges",
-    )(*tiles, bias2)
-
-    def over(pairs):
-        return [
-            (gy * count_col + col, to * count_col + 1 - col)
-            for gy, to in pairs
-            for col in range(count_col)
-        ]
-
-    beside = lax.ppermute(sent[0], "col", [(0, 1), (1, 0)])
-    if count_gy == 2:
-        directions = [[(0, 1), (1, 0)]]
-    else:
-        up = [(i, i + 1) for i in range(count_gy - 1)]
-        directions = [up, [(j, i) for i, j in up]]
-    edges = []
-    for k, pairs in enumerate(directions):
-        edges.append(lax.ppermute(sent[1 + 2 * k], "gy", pairs))
-        edges.append(lax.ppermute(sent[2 + 2 * k], ("gy", "col"), over(pairs)))
-
     cells = depth * BY
     fractions, solutes_next = pl.pallas_call(
         functools.partial(
-            column_kernel, (count_gz, count_gy, depth, rows, columns, segment, slots), few
+            column_kernel,
+            (count_gz, count_gy, depth, rows, columns, segment, slots, directions),
+            few,
         ),
         out_shape=(
             shape((2, depth, rows, columns), bf16),
             shape((slots * 2 * cells, BX), f32),
         ),
-        in_specs=[VMEM] * (few + 1 + len(edges) + 4) + [HBM, HBM],
+        in_specs=[VMEM] * (len(tiles) + 4) + [HBM, HBM],
         out_specs=(HBM, HBM),
         scratch_shapes=[
             pltpu.VMEM((2, 2 * depths, window), f32),
+            pltpu.VMEM((depths * rows, BX), bf16),
             pltpu.VMEM((segment * depth + 4, PART, 2 * window), bf16),
             pltpu.VMEM((segment * depth + 2, TALL, 2 * window), bf16),
             pltpu.VMEM((count_gz, brick_count, depth, 8, BX), f32),
@@ -630,8 +665,6 @@
         name="column",
     )(
         *tiles,
-        beside,
-        *edges,
         t1,
         bias,
         t2,

time: 26.3 us -> 28.3 us (1.076)
  starting transfers between devices: 8.95 us -> 9.95 us
  waiting for transfers between devices: 4.87 us -> 5.68 us
    ppermute x6 -> x7, starting transfers between devices: 8.95 us -> 9.95 us  [the longest x4 6.8 us: turned(): lax.ppermute(array, 'gz', [((i + s) % count_gz, i) for i in range(count_g...]
    ppermute x6 -> x7, waiting for transfers between devices: 4.87 us -> 5.68 us  [the longest x4 2.72 us: turned(): lax.ppermute(array, 'gz', [((i + s) % count_gz, i) for i in range(count_g...]
  transfers between devices with their start and end apart: 6 -> 7, of which waited for: 3 -> 3; matrix products, arithmetic and copies ran while one was open for 0% -> 0% of each run, Pallas kernels for 6% -> 5%
where the time goes in v4:
time: 28.3 us; the launch traced here: 28.1 us
  Pallas kernels  11.8 us (42%)
  starting transfers between devices  9.95 us (35%)
  waiting for transfers between devices  5.68 us (20%)
  between operations  0.66 us (2%)
    pallas_call x1, Pallas kernels, per_device(): pl.pallas_call(functools.partial(column_kernel, (count_gz, count_gy, dept...  9.36 us
    ppermute x4, starting transfers between devices, turned(): lax.ppermute(array, 'gz', [((i + s) % count_gz, i) for i in range(count_g...  6.8 us
    ppermute x4, waiting for transfers between devices, turned(): lax.ppermute(array, 'gz', [((i + s) % count_gz, i) for i in range(count_g...  2.72 us
    ppermute x1, starting transfers between devices, per_device(): received.append(lax.ppermute(sent[2 * d], 'gy', pairs))  2.56 us
    ppermute x1, waiting for transfers between devices, per_device(): received.append(lax.ppermute(sent[2 * d], 'gy', pairs))  1.51 us
    pallas_call x1, Pallas kernels, per_device(): pl.pallas_call(functools.partial(banded_kernel, (window, count_gy)), out_...  1.47 us
    ppermute x1, waiting for transfers between devices, per_device(): received.append(lax.ppermute(sent[2 * d + 1], ('gy', 'col'), over(pairs)))  1.45 us
    pallas_call x1, Pallas kernels, per_device(): pl.pallas_call(functools.partial(edges_kernel, (count_gy, depth, rows, di...  0.97 us
  transfers between devices with their start and end apart: 7, of which 3 were waited for; matrix products, arithmetic and copies ran while one was open for 0% of the time, Pallas kernels for 5%

profile of v4, /device:TPU:0, one launch (start us, length us, event | category | flops | bytes accessed | tf_op | source)
XLA Modules:
  0.0 28.1 jit_solution(14161538696132148885)
XLA Ops:
  0.6 1.0 %edges.1 = (bf16[256,128]{1,0:T(8,128)(2,1)S(1)}, bf16[16,128]{1,0:T(8,128)(2,1)S(1)}, bf16[16,128]{1,0:T(8,128)(2,1)S(1)}, bf16[16,128]{1,0:T(8,128)(2,1)S(1)}, bf16[16,128]{1,0:T(8,128)(2,1)S(1)}) custom-call(bf16[128,256]{1,0:T(8,128)(2,1)} %bitcast.11, s32[1,16]{1,0:T(1,128)} %bitcast.14), custom_call_target="tpu_custom_call" | custom-call | tf_op jit(solution)/shard_map/edges/pallas_call | solution.py:559
  1.6 0.5 %collective-permute-start = (bf16[16,128]{1,0:T(8,128)(2,1)S(1)}, bf16[16,128]{1,0:T(8,128)(2,1)S(1)}, u32[]{:S(2)}, u32[]{:S(2)}) collective-permute-start(bf16[16,128]{1,0:T(8,128)(2,1)S(1)} %get-tuple-element.17), channel_id=1, source_target_pairs={{0,1},{1,0},{2,3},{3,2},{4,5},{5,4},{6,7},{7,6},{8,9},{9,8},{10,11... | collective-permute-start | bytes 12296 | tf_op jit(solution)/shard_map/ppermute | solution.py:576
  2.1 2.6 %collective-permute-start.1 = (bf16[16,128]{1,0:T(8,128)(2,1)S(1)}, bf16[16,128]{1,0:T(8,128)(2,1)S(1)}, u32[]{:S(2)}, u32[]{:S(2)}) collective-permute-start(bf16[16,128]{1,0:T(8,128)(2,1)S(1)} %get-tuple-element.18), channel_id=1, source_target_pairs={{0,2},{2,0},{1,3},{3,1},{4,6},{6,4},{5,7},{7,5},{8,10},{10,8},{9,1... | collective-permute-start | bytes 12296 | tf_op jit(solution)/shard_map/ppermute | solution.py:574
  4.7 0.1 collective-permute-start.2
  4.8 0.0 collective-permute-done.x_ref
  4.8 1.5 %collective-permute-done.1.refs_0_ = bf16[16,128]{1,0:T(8,128)(2,1)S(1)} collective-permute-done((bf16[16,128]{1,0:T(8,128)(2,1)S(1)}, bf16[16,128]{1,0:T(8,128)(2,1)S(1)}, u32[]{:S(2)}, u32[]{:S(2)}) %collective-permute-start.1) | collective-permute-done | bytes 4128 | tf_op jit(solution)/shard_map/ppermute | solution.py:574
  6.3 1.4 %collective-permute-done.2.refs_1_ = bf16[16,128]{1,0:T(8,128)(2,1)S(1)} collective-permute-done((bf16[16,128]{1,0:T(8,128)(2,1)S(1)}, bf16[16,128]{1,0:T(8,128)(2,1)S(1)}, u32[]{:S(2)}, u32[]{:S(2)}) %collective-permute-start.2) | collective-permute-done | bytes 4128 | tf_op jit(solution)/shard_map/ppermute | solution.py:575
  7.7 1.6 %collective-permute-start.5 = (bf16[288,128]{1,0:T(8,128)(2,1)S(1)}, bf16[288,128]{1,0:T(8,128)(2,1)S(1)}, u32[]{:S(2)}, u32[]{:S(2)}) collective-permute-start(bf16[288,128]{1,0:T(8,128)(2,1)S(1)} %get-tuple-element.20.refs_4_.refs_0_), channel_id=1, source_target_pairs={{12,0},{0,4},{4,8},{8,12},{13,1},{1,5},{5,9},{9,13},{14,2},{2,6},{... | collective-permute-start | bytes 221192 | tf_op jit(solution)/shard_map/ppermute | solution.py:590
  9.4 2.2 %collective-permute-start.3 = (bf16[288,128]{1,0:T(8,128)(2,1)S(1)}, bf16[288,128]{1,0:T(8,128)(2,1)S(1)}, u32[]{:S(2)}, u32[]{:S(2)}) collective-permute-start(bf16[288,128]{1,0:T(8,128)(2,1)S(1)} %get-tuple-element.20.refs_4_.refs_0_), channel_id=1, source_target_pairs={{4,0},{8,4},{12,8},{0,12},{5,1},{9,5},{13,9},{1,13},{6,2},{10,6},{... | collective-permute-start | bytes 221192 | tf_op jit(solution)/shard_map/ppermute | solution.py:590
  11.6 0.8 %collective-permute-start.4 = (bf16[256,128]{1,0:T(8,128)(2,1)S(1)}, bf16[256,128]{1,0:T(8,128)(2,1)S(1)}, u32[]{:S(2)}, u32[]{:S(2)}) collective-permute-start(bf16[256,128]{1,0:T(8,128)(2,1)S(1)} %get-tuple-element.15.own_ref), channel_id=1, source_target_pairs={{8,0},{12,4},{0,8},{4,12},{9,1},{13,5},{1,9},{5,13},{10,2},{14,6},... | collective-permute-start | bytes 196616 | tf_op jit(solution)/shard_map/ppermute | solution.py:590
  12.4 2.1 %collective-permute-start.6 = (bf16[32,128]{1,0:T(8,128)(2,1)S(1)}, bf16[32,128]{1,0:T(8,128)(2,1)S(1)}, u32[]{:S(2)}, u32[]{:S(2)}) collective-permute-start(bf16[32,128]{1,0:T(8,128)(2,1)S(1)} %get-tuple-element.21), channel_id=1, source_target_pairs={{8,0},{12,4},{0,8},{4,12},{9,1},{13,5},{1,9},{5,13},{10,2},{14,6},... | collective-permute-start | bytes 24584 | tf_op jit(solution)/shard_map/ppermute | solution.py:590
  14.5 1.5 %banded.1 = (bf16[144,192]{1,0:T(8,128)(2,1)S(1)}, f32[144,768]{1,0:T(8,128)S(1)}, bf16[96,432]{1,0:T(8,128)(2,1)S(1)}, f32[32,768]{1,0:T(8,128)S(1)}) custom-call(bf16[8,27]{1,0:T(8,128)(2,1)} %bitcast.13, f32[8]{0:T(128)} %refs_1_.1, bf16[16,27]{1,0:T(8,128)(2,1)} %bitcast.12, f32[2]{0:T(128)} %refs_3_.1, ...), custom_call_target="tpu_custom_call" | custom-call | flops 20971520 | bytes 4194304 | tf_op jit(solution)/shard_map/banded/pallas_call | solution.py:599
  16.0 2.7 %collective-permute-done.6.refs_4_ = bf16[32,128]{1,0:T(8,128)(2,1)S(1)} collective-permute-done((bf16[32,128]{1,0:T(8,128)(2,1)S(1)}, bf16[32,128]{1,0:T(8,128)(2,1)S(1)}, u32[]{:S(2)}, u32[]{:S(2)}) %collective-permute-start.6) | collective-permute-done | bytes 8224 | tf_op jit(solution)/shard_map/ppermute | solution.py:590
  18.7 0.0 collective-permute-done.4.refs_2_
  18.7 0.0 collective-permute-done.5.refs_3_
  18.7 0.0 collective-permute-done.3.refs_1_
  18.7 9.4 %column.1 = (bf16[2,4,32,256]{3,2,1,0:T(8,128)(2,1)}, f32[1024,128]{1,0:T(8,128)}) custom-call(bf16[288,128]{1,0:T(8,128)(2,1)S(1)} %get-tuple-element.20.refs_4_.refs_0_, bf16[288,128]{1,0:T(8,128)(2,1)S(1)} %collective-permute-done.3.refs_1_, bf16[256,128]{1,0:T(8,128)(2,1)S(1)} %collective-permute-done.4.refs_2_, ...), custom_call_target="tpu_custom_call" | custom-call | flops 1698693120 | bytes 4194304 | tf_op jit(solution)/shard_map/column/pallas_call | solution.py:630
  (1 shorter events, 0.0 us)
Async XLA Ops:
  1.6 3.2 %collective-permute-start = (bf16[16,128]{1,0:T(8,128)(2,1)S(1)}, bf16[16,128]{1,0:T(8,128)(2,1)S(1)}, u32[]{:S(2)}, u32[]{:S(2)}) collective-permute-start(bf16[16,128]{1,0:T(8,128)(2,1)S(1)} %get-tuple-element.17), channel_id=1, source_target_pairs={{0,1},{1,0},{2,3},{3,2},{4,5},{5,4},{6,7},{7,6},{8,9},{9,8},{10,11... | collective-permute-start | bytes 12296 | tf_op jit(solution)/shard_map/ppermute | solution.py:576
  2.1 4.2 %collective-permute-start.1 = (bf16[16,128]{1,0:T(8,128)(2,1)S(1)}, bf16[16,128]{1,0:T(8,128)(2,1)S(1)}, u32[]{:S(2)}, u32[]{:S(2)}) collective-permute-start(bf16[16,128]{1,0:T(8,128)(2,1)S(1)} %get-tuple-element.18), channel_id=1, source_target_pairs={{0,2},{2,0},{1,3},{3,1},{4,6},{6,4},{5,7},{7,5},{8,10},{10,8},{9,1... | collective-permute-start | bytes 12296 | tf_op jit(solution)/shard_map/ppermute | solution.py:574
  4.7 3.0 %collective-permute-start.2 = (bf16[16,128]{1,0:T(8,128)(2,1)S(1)}, bf16[16,128]{1,0:T(8,128)(2,1)S(1)}, u32[]{:S(2)}, u32[]{:S(2)}) collective-permute-start(bf16[16,128]{1,0:T(8,128)(2,1)S(1)} %get-tuple-element.19), channel_id=1, source_target_pairs={{0,3},{1,2},{2,1},{3,0},{4,7},{5,6},{6,5},{7,4},{8,11},{9,10},{10,... | collective-permute-start | bytes 12296 | tf_op jit(solution)/shard_map/ppermute | solution.py:575
  7.7 11.0 %collective-permute-start.5 = (bf16[288,128]{1,0:T(8,128)(2,1)S(1)}, bf16[288,128]{1,0:T(8,128)(2,1)S(1)}, u32[]{:S(2)}, u32[]{:S(2)}) collective-permute-start(bf16[288,128]{1,0:T(8,128)(2,1)S(1)} %get-tuple-element.20.refs_4_.refs_0_), channel_id=1, source_target_pairs={{12,0},{0,4},{4,8},{8,12},{13,1},{1,5},{5,9},{9,13},{14,2},{2,6},{... | collective-permute-start | bytes 221192 | tf_op jit(solution)/shard_map/ppermute | solution.py:590
  9.4 9.4 %collective-permute-start.3 = (bf16[288,128]{1,0:T(8,128)(2,1)S(1)}, bf16[288,128]{1,0:T(8,128)(2,1)S(1)}, u32[]{:S(2)}, u32[]{:S(2)}) collective-permute-start(bf16[288,128]{1,0:T(8,128)(2,1)S(1)} %get-tuple-element.20.refs_4_.refs_0_), channel_id=1, source_target_pairs={{4,0},{8,4},{12,8},{0,12},{5,1},{9,5},{13,9},{1,13},{6,2},{10,6},{... | collective-permute-start | bytes 221192 | tf_op jit(solution)/shard_map/ppermute | solution.py:590
  11.6 7.1 %collective-permute-start.4 = (bf16[256,128]{1,0:T(8,128)(2,1)S(1)}, bf16[256,128]{1,0:T(8,128)(2,1)S(1)}, u32[]{:S(2)}, u32[]{:S(2)}) collective-permute-start(bf16[256,128]{1,0:T(8,128)(2,1)S(1)} %get-tuple-element.15.own_ref), channel_id=1, source_target_pairs={{8,0},{12,4},{0,8},{4,12},{9,1},{13,5},{1,9},{5,13},{10,2},{14,6},... | collective-permute-start | bytes 196616 | tf_op jit(solution)/shard_map/ppermute | solution.py:590
  12.4 6.3 %collective-permute-start.6 = (bf16[32,128]{1,0:T(8,128)(2,1)S(1)}, bf16[32,128]{1,0:T(8,128)(2,1)S(1)}, u32[]{:S(2)}, u32[]{:S(2)}) collective-permute-start(bf16[32,128]{1,0:T(8,128)(2,1)S(1)} %get-tuple-element.21), channel_id=1, source_target_pairs={{8,0},{12,4},{0,8},{4,12},{9,1},{13,5},{1,9},{5,13},{10,2},{14,6},... | collective-permute-start | bytes 24584 | tf_op jit(solution)/shard_map/ppermute | solution.py:590

commit v5 on v4

--- a/solution.py
+++ b/solution.py
@@ -21,6 +21,7 @@
 
 VMEM = pl.BlockSpec(memory_space=pltpu.VMEM)
 SMEM = pl.BlockSpec(memory_space=pltpu.SMEM)
+ANY = pl.BlockSpec(memory_space=pl.ANY)
 HBM = pl.BlockSpec(memory_space=pltpu.HBM)
 
 
@@ -121,7 +122,7 @@
         sends[2 * d + 1][...] = columns_of(2 + 2 * d, near.astype(jnp.bfloat16))
 
 
-def pack_kernel(directions, own_ref, misc_ref, x_ref, *refs):
+def pack_kernel(directions, own_ref, misc_ref, x_ref, _, *refs):
     received, (payload_ref, edge_ref) = refs[: 2 * directions], refs[2 * directions :]
     height = own_ref.shape[0]
     payload_ref[0:height, :] = own_ref[...]
@@ -206,11 +207,77 @@
     bias2_ref[...] = jnp.where(((row >> 2) & 1) == 0, b2_ref[0], b2_ref[1])
 
 
+def laplace(field, z, y):
+    centre = field[z][y]
+    last = lax.broadcasted_iota(jnp.int32, centre.shape, 1) == BX - 1
+    ahead = jnp.where(last, 0.0, pltpu.roll(centre, BX - 1, 1) - centre)
+    result = ahead - pltpu.roll(ahead, 1, 1)
+    beside = [
+        field[zz][yy]
+        for zz, yy in ((z - 1, y), (z + 1, y), (z, y - 1), (z, y + 1))
+        if 0 <= zz < len(field) and 0 <= yy < BY
+    ]
+    return result + (functools.reduce(jnp.add, beside) - float(len(beside)) * centre)
+
+
+def uptake_of(quarter, doc, oxy):
+    return quarter * doc * oxy / ((0.5 + jnp.abs(doc)) * (0.3 + jnp.abs(oxy)))
+
+
+def prepare_kernel(dims, solutes_ref, biomass_ref, _, *refs):
+    depth, slots = dims
+    outs, (state, biomass, mass, sems) = refs[:5], refs[5:]
+    size = depth * BY
+    copies = []
+    for group in range(slots // 8):
+        for k, (source, target) in enumerate(((solutes_ref, state), (biomass_ref, biomass))):
+            rows = (2 - k) * 8 * size
+            at = pl.ds(group * rows, rows)
+            copies.append(
+                pltpu.make_async_copy(source.at[at], target.at[at], sems.at[group, k])
+            )
+    for copy in copies:
+        copy.start()
+    for group in range(slots // 8):
+        copies[2 * group].wait()
+        copies[2 * group + 1].wait()
+        at = slice(group * 8 * size, (group + 1) * 8 * size)
+        mass[at, :] = biomass[at, :].astype(jnp.float32)
+
+        def rows_of(pitch, offset):
+            return pl.ds(group * 8 * pitch + offset, 8, stride=pitch)
+
+        grid = [(z, y) for z in range(depth) for y in range(BY)]
+        carbon, oxygen = [
+            [
+                [state[rows_of(2 * size, k * size + z * BY + y), :] for y in range(BY)]
+                for z in range(depth)
+            ]
+            for k in range(2)
+        ]
+        for z, y in grid:
+            at = group * 8 * size + (z * BY + y) * 8
+            at = slice(at, at + 8)
+            doc, oxy = carbon[z][y], oxygen[z][y]
+            quarter = 0.25 * mass[rows_of(size, z * BY + y), :]
+            uptake = uptake_of(quarter, doc, oxy)
+            values = (
+                doc - uptake,
+                oxy - uptake,
+                laplace(carbon, z, y),
+                laplace(oxygen, z, y),
+                quarter,
+            )
+            for out, value in zip(outs, values):
+                out[at, :] = value
+
+
 def column_kernel(dims, few, *refs):
     count_gz, count_gy, depth, rows, columns, segment, slots, directions = dims
     count = few + 1 if few > 1 else 1
     tiles, refs = refs[:count], refs[count:]
-    t1_ref, bias_ref, t2_ref, bias2_ref, solutes_ref, biomass_ref, *refs = refs
+    t1_ref, bias_ref, t2_ref, bias2_ref, *refs = refs
+    carbon_ref, oxygen_ref, carbon_around_ref, oxygen_around_ref, quarter_ref, *refs = refs
     fractions_ref, next_ref, *refs = refs
     (
         edge_rows,
@@ -220,8 +287,6 @@
         bricks,
         arrived,
         state,
-        biomass,
-        mass,
         fractions,
         owner_rows,
         owner_table,
@@ -241,11 +306,6 @@
     first_tile = z_index if few > 1 else 0
     size = depth * BY
 
-    state_copy = pltpu.make_async_copy(solutes_ref, state, sems.at[0])
-    state_copy.start()
-    biomass_copy = pltpu.make_async_copy(biomass_ref, biomass, sems.at[1])
-    biomass_copy.start()
-
     def tile_rows(i, start, size):
         if not isinstance(start, int):
             start = pl.multiple_of(start, TILE)
@@ -301,7 +361,7 @@
             unpack(i)
     else:
         pl.loop(0, count_gz)(unpack)
-    table_copy = pltpu.make_async_copy(owner_rows, owner_table, sems.at[2])
+    table_copy = pltpu.make_async_copy(owner_rows, owner_table, sems.at[0])
     table_copy.start()
 
     def moved(values):
@@ -431,54 +491,29 @@
             for o in range(2):
                 values = jnp.concatenate([v[o * BY : o * BY + BY] for v in own], axis=0)
                 fractions[o, zz, :, xb * BX : (xb + 1) * BX] = values.astype(jnp.bfloat16)
-    fractions_copy = pltpu.make_async_copy(fractions, fractions_ref, sems.at[3])
+    fractions_copy = pltpu.make_async_copy(fractions, fractions_ref, sems.at[1])
     fractions_copy.start()
 
     table_copy.wait()
-
-    @pl.loop(0, slots)
-    def _(j):
+    for j in range(slots):
         brick_of_slot[j] = -1
 
     @pl.loop(0, count_gz)
     def _(i):
-        tile = lax.rem(first_tile + i, count_gz)
+        first = lax.rem(first_tile + i, count_gz) * capacity
         rank = jnp.int32(0)
         for b in range(brick_count):
             mine = owner_table[i, OWNER_ROW, b] == z_index
-
-            @pl.when(mine)
-            def _():
-                brick_of_slot[tile * capacity + rank] = b
-
+            brick_of_slot[jnp.where(mine, first + rank, slots)] = b
             rank = rank + mine.astype(jnp.int32)
 
-    biomass_copy.wait()
-
-    @pl.loop(0, slots)
+    @pl.loop(0, slots, unroll=8)
     def _(j):
         brick = brick_of_slot[j]
         values = bricks[j // capacity, jnp.maximum(brick, 0)]
         values = jnp.where(brick >= 0, values, 0.0)
         at = pl.multiple_of(j * (2 * size), 8)
         arrived[pl.ds(at, 2 * size), :] = values.reshape(2 * size, BX)
-        at = pl.multiple_of(j * size, size)
-        mass[pl.ds(at, size), :] = 0.25 * biomass[pl.ds(at, size), :].astype(jnp.float32)
-
-    last = lax.broadcasted_iota(jnp.int32, (8, BX), 1) == BX - 1
-
-    def laplace(field, z, y):
-        centre = field[z][y]
-        ahead = jnp.where(last, 0.0, pltpu.roll(centre, BX - 1, 1) - centre)
-        result = ahead - pltpu.roll(ahead, 1, 1)
-        beside = [
-            field[zz][yy]
-            for zz, yy in ((z - 1, y), (z + 1, y), (z, y - 1), (z, y + 1))
-            if 0 <= zz < depth and 0 <= yy < BY
-        ]
-        return result + (functools.reduce(jnp.add, beside) - float(len(beside)) * centre)
-
-    state_copy.wait()
 
     def next_copy(group):
         at = pl.ds(pl.multiple_of(group * 16 * size, 16 * size), 16 * size)
@@ -486,39 +521,46 @@
 
     @pl.loop(0, slots // 8)
     def _(group):
-        def rows_of(pitch, offset):
-            return pl.ds(group * 8 * pitch + offset, 8, stride=pitch)
-
         grid = [(z, y) for z in range(depth) for y in range(BY)]
-        carbon = [
-            [state[rows_of(2 * size, z * BY + y), :] for y in range(BY)] for z in range(depth)
+
+        def load(ref):
+            base = group * (8 * size)
+            return [
+                [
+                    ref[pl.ds(pl.multiple_of(base + (z * BY + y) * 8, 8), 8), :]
+                    for y in range(BY)
+                ]
+                for z in range(depth)
+            ]
+
+        def rows_of(offset):
+            return pl.ds(group * 16 * size + offset, 8, stride=2 * size)
+
+        quarter = load(quarter_ref)
+        pore = [[arrived[rows_of(z * 8 + y), :] for y in range(BY)] for z in range(depth)]
+        organic = [
+            [0.3 * arrived[rows_of(z * 8 + BY + y), :] for y in range(BY)] for z in range(depth)
         ]
-        oxygen = [
-            [state[rows_of(2 * size, size + z * BY + y), :] for y in range(BY)]
-            for z in range(depth)
-        ]
-        pore = [[arrived[rows_of(2 * size, z * 8 + y), :] for y in range(BY)] for z in range(depth)]
-        organic = [
-            [0.3 * arrived[rows_of(2 * size, z * 8 + BY + y), :] for y in range(BY)]
-            for z in range(depth)
-        ]
-        quarter = [[mass[rows_of(size, z * BY + y), :] for y in range(BY)] for z in range(depth)]
         slow = [[0.12 * p for p in row] for row in pore]
         fast = [[0.16 * p for p in row] for row in pore]
-        for _ in range(STEPS):
+        carbon, oxygen = load(carbon_ref), load(oxygen_ref)
+        around = load(carbon_around_ref), load(oxygen_around_ref)
+        for z, y in grid:
+            carbon[z][y] += slow[z][y] * around[0][z][y] + organic[z][y]
+            oxygen[z][y] += fast[z][y] * around[1][z][y]
+        for _ in range(STEPS - 1):
             carbon_new = [[None] * BY for _ in range(depth)]
             oxygen_new = [[None] * BY for _ in range(depth)]
             for z, y in grid:
                 doc, oxy = carbon[z][y], oxygen[z][y]
-                uptake = quarter[z][y] * doc * oxy
-                uptake = uptake / ((0.5 + jnp.abs(doc)) * (0.3 + jnp.abs(oxy)))
+                uptake = uptake_of(quarter[z][y], doc, oxy)
                 gain = organic[z][y] - uptake
                 carbon_new[z][y] = doc + slow[z][y] * laplace(carbon, z, y) + gain
                 oxygen_new[z][y] = oxy + fast[z][y] * laplace(oxygen, z, y) - uptake
             carbon, oxygen = carbon_new, oxygen_new
         for z, y in grid:
-            state[rows_of(2 * size, z * BY + y), :] = carbon[z][y]
-            state[rows_of(2 * size, size + z * BY + y), :] = oxygen[z][y]
+            state[rows_of(z * BY + y), :] = carbon[z][y]
+            state[rows_of(size + z * BY + y), :] = oxygen[z][y]
         next_copy(group).start()
 
     @pl.loop(0, slots // 8)
@@ -574,24 +616,48 @@
         received.append(lax.ppermute(sent[2 * d], "gy", pairs))
         received.append(lax.ppermute(sent[2 * d + 1], ("gy", "col"), over(pairs)))
     near = lax.ppermute(near, "col", [(0, 1), (1, 0)])
+    cells = depth * BY
+    prepared = pl.pallas_call(
+        functools.partial(prepare_kernel, (depth, slots)),
+        out_shape=[shape((slots * cells, BX), f32)] * 5,
+        in_specs=[HBM, HBM, ANY],
+        out_specs=[VMEM] * 5,
+        scratch_shapes=[
+            pltpu.VMEM((slots * 2 * cells, BX), f32),
+            pltpu.VMEM((slots * cells, BX), bf16),
+            pltpu.VMEM((slots * cells, BX), f32),
+            pltpu.SemaphoreType.DMA((slots // 8, 2)),
+        ],
+        compiler_params=pltpu.CompilerParams(vmem_limit_bytes=12 * 2**20),
+        cost_estimate=pl.CostEstimate(
+            flops=60 * slots * cells * BX, bytes_accessed=2**20, transcendentals=0
+        ),
+        name="prepare",
+    )(
+        in_hbm(solutes.reshape(slots * 2 * cells, BX)),
+        in_hbm(biomass.reshape(slots * cells, BX)),
+        misc,
+    )
     payload, cells_around = pl.pallas_call(
         functools.partial(pack_kernel, directions),
         out_shape=[
             shape((blocks * height + (directions + 1) * TILE, BX), bf16),
             shape(((directions + 1) * TILE, BX), bf16),
         ],
-        in_specs=[VMEM] * (3 + 2 * directions),
+        in_specs=[VMEM] * 3 + [ANY] + [VMEM] * (2 * directions),
         out_specs=[VMEM] * 2,
         compiler_params=pltpu.CompilerParams(vmem_limit_bytes=4 * 2**20),
         name="pack",
-    )(own, misc, near, *received)
+    )(own, misc, near, prepared[-1], *received)
 
     def turned(array, s):
         return lax.ppermute(array, "gz", [((i + s) % count_gz, i) for i in range(count_gz)])
 
     few = count_gz if count_gz == 4 else 1
     if few > 1:
-        tiles = [payload, turned(payload, 1), turned(own, 2), turned(payload, 3)]
+        opposite = turned(own, 2)
+        tiles = [payload, turned(payload, 1), opposite, turned(payload, 3)]
+        cells_around, _ = lax.optimization_barrier((cells_around, opposite))
         tiles.append(turned(cells_around, 2))
     else:
         tiles = [lax.all_gather(payload, "gz", axis=0, tiled=False)]
@@ -604,7 +670,7 @@
             shape((6 * HALF, 3 * TALL), bf16),
             shape((2 * HALF, 2 * window), f32),
         ),
-        in_specs=[HBM, HBM, HBM, HBM, pl.BlockSpec(memory_space=pl.ANY)],
+        in_specs=[HBM, HBM, HBM, HBM, ANY],
         out_specs=(VMEM, VMEM, VMEM, VMEM),
         scratch_shapes=[
             pltpu.VMEM((CHANNELS, 27), bf16),
@@ -626,7 +692,6 @@
         payload,
     )
 
-    cells = depth * BY
     fractions, solutes_next = pl.pallas_call(
         functools.partial(
             column_kernel,
@@ -637,7 +702,7 @@
             shape((2, depth, rows, columns), bf16),
             shape((slots * 2 * cells, BX), f32),
         ),
-        in_specs=[VMEM] * (len(tiles) + 4) + [HBM, HBM],
+        in_specs=[VMEM] * (len(tiles) + 9),
         out_specs=(HBM, HBM),
         scratch_shapes=[
             pltpu.VMEM((2, 2 * depths, window), f32),
@@ -647,13 +712,11 @@
             pltpu.VMEM((count_gz, brick_count, depth, 8, BX), f32),
             pltpu.VMEM((slots * 2 * cells, BX), f32),
             pltpu.VMEM((slots * 2 * cells, BX), f32),
-            pltpu.VMEM((slots * cells, BX), bf16),
-            pltpu.VMEM((slots * cells, BX), f32),
             pltpu.VMEM((2, depth, rows, columns), bf16),
             pltpu.VMEM((count_gz, 8, BX), jnp.int32),
             pltpu.SMEM((count_gz, 8, BX), jnp.int32),
-            pltpu.SMEM((slots,), jnp.int32),
-            pltpu.SemaphoreType.DMA((4,)),
+            pltpu.SMEM((slots + 1,), jnp.int32),
+            pltpu.SemaphoreType.DMA((2,)),
             pltpu.SemaphoreType.DMA((slots // 8,)),
         ],
         compiler_params=pltpu.CompilerParams(vmem_limit_bytes=40 * 2**20),
@@ -669,8 +732,7 @@
         bias,
         t2,
         bias2,
-        in_hbm(solutes.reshape(slots * 2 * cells, BX)),
-        in_hbm(biomass.reshape(slots * cells, BX)),
+        *prepared,
     )
     return fractions, solutes_next.reshape(solutes.shape)
 

time: 28.3 us -> 26.7 us (0.943)
  waiting for transfers between devices: 5.68 us -> 3.09 us
  Pallas kernels: 11.8 us -> 12.8 us
    pallas_call x0 -> x1, Pallas kernels: none -> 2 us  [per_device(): pl.pallas_call(functools.partial(prepare_kernel, (depth, slots)), out_sha...]
    ppermute x1, waiting for transfers between devices: 1.51 us -> 0.01 us  [per_device(): received.append(lax.ppermute(sent[2 * d], 'gy', pairs))]
    ppermute x1, waiting for transfers between devices: 1.45 us -> 0.01 us  [per_device(): received.append(lax.ppermute(sent[2 * d + 1], ('gy', 'col'), over(pairs)))]
    pallas_call x1, Pallas kernels: 9.36 us -> 8.34 us  [per_device(): pl.pallas_call(functools.partial(column_kernel, (count_gz, count_gy, dept...]
    ppermute x4, waiting for transfers between devices: 2.72 us -> 3.08 us  [turned(): lax.ppermute(array, 'gz', [((i + s) % count_gz, i) for i in range(count_g...]
  transfers between devices with their start and end apart: 7 -> 7, of which waited for: 3 -> 1; matrix products, arithmetic and copies ran while one was open for 0% -> 0% of each run, Pallas kernels for 5% -> 13%
where the time goes in v5:
time: 26.7 us; the launch traced here: 26.4 us
  Pallas kernels  12.8 us (48%)
  starting transfers between devices  9.86 us (37%)
  waiting for transfers between devices  3.09 us (12%)
  between operations  0.69 us (3%)
    pallas_call x1, Pallas kernels, per_device(): pl.pallas_call(functools.partial(column_kernel, (count_gz, count_gy, dept...  8.34 us
    ppermute x4, starting transfers between devices, turned(): lax.ppermute(array, 'gz', [((i + s) % count_gz, i) for i in range(count_g...  6.7 us
    ppermute x4, waiting for transfers between devices, turned(): lax.ppermute(array, 'gz', [((i + s) % count_gz, i) for i in range(count_g...  3.08 us
    ppermute x1, starting transfers between devices, per_device(): received.append(lax.ppermute(sent[2 * d], 'gy', pairs))  2.56 us
    pallas_call x1, Pallas kernels, per_device(): pl.pallas_call(functools.partial(prepare_kernel, (depth, slots)), out_sha...  2 us
    pallas_call x1, Pallas kernels, per_device(): pl.pallas_call(functools.partial(banded_kernel, (window, count_gy)), out_...  1.46 us
    pallas_call x1, Pallas kernels, per_device(): pl.pallas_call(functools.partial(edges_kernel, (count_gy, depth, rows, di...  0.97 us
  transfers between devices with their start and end apart: 7, of which 1 were waited for; matrix products, arithmetic and copies ran while one was open for 0% of the time, Pallas kernels for 13%

profile of v5, /device:TPU:0, one launch (start us, length us, event | category | flops | bytes accessed | tf_op | source)
XLA Modules:
  0.0 26.4 jit_solution(14810358329950560384)
XLA Ops:
  0.6 1.0 %edges.1 = (bf16[256,128]{1,0:T(8,128)(2,1)S(1)}, bf16[16,128]{1,0:T(8,128)(2,1)S(1)}, bf16[16,128]{1,0:T(8,128)(2,1)S(1)}, bf16[16,128]{1,0:T(8,128)(2,1)S(1)}, bf16[16,128]{1,0:T(8,128)(2,1)S(1)}) custom-call(bf16[128,256]{1,0:T(8,128)(2,1)} %bitcast.13, s32[1,16]{1,0:T(1,128)} %bitcast.16), custom_call_target="tpu_custom_call" | custom-call | tf_op jit(solution)/shard_map/edges/pallas_call | solution.py:601
  1.6 0.5 %collective-permute-start = (bf16[16,128]{1,0:T(8,128)(2,1)S(1)}, bf16[16,128]{1,0:T(8,128)(2,1)S(1)}, u32[]{:S(2)}, u32[]{:S(2)}) collective-permute-start(bf16[16,128]{1,0:T(8,128)(2,1)S(1)} %get-tuple-element.23), channel_id=1, source_target_pairs={{0,1},{1,0},{2,3},{3,2},{4,5},{5,4},{6,7},{7,6},{8,9},{9,8},{10,11... | collective-permute-start | bytes 12296 | tf_op jit(solution)/shard_map/ppermute | solution.py:618
  2.1 2.6 %collective-permute-start.1 = (bf16[16,128]{1,0:T(8,128)(2,1)S(1)}, bf16[16,128]{1,0:T(8,128)(2,1)S(1)}, u32[]{:S(2)}, u32[]{:S(2)}) collective-permute-start(bf16[16,128]{1,0:T(8,128)(2,1)S(1)} %get-tuple-element.25), channel_id=1, source_target_pairs={{0,2},{2,0},{1,3},{3,1},{4,6},{6,4},{5,7},{7,5},{8,10},{10,8},{9,1... | collective-permute-start | bytes 12296 | tf_op jit(solution)/shard_map/ppermute | solution.py:616
  4.7 0.1 collective-permute-start.2
  4.8 2.8 %collective-permute-start.4 = (bf16[256,128]{1,0:T(8,128)(2,1)S(1)}, bf16[256,128]{1,0:T(8,128)(2,1)S(1)}, u32[]{:S(2)}, u32[]{:S(2)}) collective-permute-start(bf16[256,128]{1,0:T(8,128)(2,1)S(1)} %get-tuple-element.21.own_ref), channel_id=1, source_target_pairs={{8,0},{12,4},{0,8},{4,12},{9,1},{13,5},{1,9},{5,13},{10,2},{14,6},... | collective-permute-start | bytes 196616 | tf_op jit(solution)/shard_map/ppermute | solution.py:654
  7.6 2.0 %prepare.1 = (f32[512,128]{1,0:T(8,128)S(1)}, f32[512,128]{1,0:T(8,128)S(1)}, f32[512,128]{1,0:T(8,128)S(1)}, f32[512,128]{1,0:T(8,128)S(1)}, f32[512,128]{1,0:T(8,128)S(1)}) custom-call(f32[1024,128]{1,0:T(8,128)} %bitcast.11, bf16[512,128]{1,0:T(8,128)(2,1)} %bitcast.12, bf16[16,128]{1,0:T(8,128)(2,1)S(1)} %get-tuple-element.22._.misc_ref), custom_call_target="tpu_custom_call" | custom-call | flops 3932160 | bytes 1048576 | tf_op jit(solution)/shard_map/prepare/pallas_call | solution.py:620
  9.6 0.0 collective-permute-done.x_ref
  9.6 0.0 collective-permute-done.1.refs_0_
  9.6 0.0 collective-permute-done.2.refs_1_
  9.6 1.6 %collective-permute-start.5 = (bf16[288,128]{1,0:T(8,128)(2,1)S(1)}, bf16[288,128]{1,0:T(8,128)(2,1)S(1)}, u32[]{:S(2)}, u32[]{:S(2)}) collective-permute-start(bf16[288,128]{1,0:T(8,128)(2,1)S(1)} %get-tuple-element.27.refs_4_.refs_0_), channel_id=1, source_target_pairs={{12,0},{0,4},{4,8},{8,12},{13,1},{1,5},{5,9},{9,13},{14,2},{2,6},{... | collective-permute-start | bytes 221192 | tf_op jit(solution)/shard_map/ppermute | solution.py:654
  11.3 2.2 %collective-permute-start.3 = (bf16[288,128]{1,0:T(8,128)(2,1)S(1)}, bf16[288,128]{1,0:T(8,128)(2,1)S(1)}, u32[]{:S(2)}, u32[]{:S(2)}) collective-permute-start(bf16[288,128]{1,0:T(8,128)(2,1)S(1)} %get-tuple-element.27.refs_4_.refs_0_), channel_id=1, source_target_pairs={{4,0},{8,4},{12,8},{0,12},{5,1},{9,5},{13,9},{1,13},{6,2},{10,6},{... | collective-permute-start | bytes 221192 | tf_op jit(solution)/shard_map/ppermute | solution.py:654
  13.5 0.0 collective-permute-done.4.refs_2_
  13.5 0.0 collective-permute-start.6
  13.5 1.5 %banded.1 = (bf16[144,192]{1,0:T(8,128)(2,1)S(1)}, f32[144,768]{1,0:T(8,128)S(1)}, bf16[96,432]{1,0:T(8,128)(2,1)S(1)}, f32[32,768]{1,0:T(8,128)S(1)}) custom-call(bf16[8,27]{1,0:T(8,128)(2,1)} %bitcast.15, f32[8]{0:T(128)} %refs_1_.1, bf16[16,27]{1,0:T(8,128)(2,1)} %bitcast.14, f32[2]{0:T(128)} %refs_3_.1, ...), custom_call_target="tpu_custom_call" | custom-call | flops 20971520 | bytes 4194304 | tf_op jit(solution)/shard_map/banded/pallas_call | solution.py:665
  15.0 3.1 %collective-permute-done.6.refs_4_ = bf16[32,128]{1,0:T(8,128)(2,1)S(1)} collective-permute-done((bf16[32,128]{1,0:T(8,128)(2,1)S(1)}, bf16[32,128]{1,0:T(8,128)(2,1)S(1)}, u32[]{:S(2)}, u32[]{:S(2)}) %collective-permute-start.6) | collective-permute-done | bytes 8224 | tf_op jit(solution)/shard_map/ppermute | solution.py:654
  18.1 0.0 collective-permute-done.5.refs_3_
  18.1 0.0 collective-permute-done.3.refs_1_
  18.1 8.3 %column.1 = (bf16[2,4,32,256]{3,2,1,0:T(8,128)(2,1)}, f32[1024,128]{1,0:T(8,128)}) custom-call(bf16[288,128]{1,0:T(8,128)(2,1)S(1)} %get-tuple-element.27.refs_4_.refs_0_, bf16[288,128]{1,0:T(8,128)(2,1)S(1)} %collective-permute-done.3.refs_1_, bf16[256,128]{1,0:T(8,128)(2,1)S(1)} %collective-permute-done.4.refs_2_, ...), custom_call_target="tpu_custom_call" | custom-call | flops 1698693120 | bytes 4194304 | tf_op jit(solution)/shard_map/column/pallas_call | solution.py:695
  (1 shorter events, 0.0 us)
Async XLA Ops:
  1.6 8.0 %collective-permute-start = (bf16[16,128]{1,0:T(8,128)(2,1)S(1)}, bf16[16,128]{1,0:T(8,128)(2,1)S(1)}, u32[]{:S(2)}, u32[]{:S(2)}) collective-permute-start(bf16[16,128]{1,0:T(8,128)(2,1)S(1)} %get-tuple-element.23), channel_id=1, source_target_pairs={{0,1},{1,0},{2,3},{3,2},{4,5},{5,4},{6,7},{7,6},{8,9},{9,8},{10,11... | collective-permute-start | bytes 12296 | tf_op jit(solution)/shard_map/ppermute | solution.py:618
  2.1 7.5 %collective-permute-start.1 = (bf16[16,128]{1,0:T(8,128)(2,1)S(1)}, bf16[16,128]{1,0:T(8,128)(2,1)S(1)}, u32[]{:S(2)}, u32[]{:S(2)}) collective-permute-start(bf16[16,128]{1,0:T(8,128)(2,1)S(1)} %get-tuple-element.25), channel_id=1, source_target_pairs={{0,2},{2,0},{1,3},{3,1},{4,6},{6,4},{5,7},{7,5},{8,10},{10,8},{9,1... | collective-permute-start | bytes 12296 | tf_op jit(solution)/shard_map/ppermute | solution.py:616
  4.7 4.9 %collective-permute-start.2 = (bf16[16,128]{1,0:T(8,128)(2,1)S(1)}, bf16[16,128]{1,0:T(8,128)(2,1)S(1)}, u32[]{:S(2)}, u32[]{:S(2)}) collective-permute-start(bf16[16,128]{1,0:T(8,128)(2,1)S(1)} %get-tuple-element.26), channel_id=1, source_target_pairs={{0,3},{1,2},{2,1},{3,0},{4,7},{5,6},{6,5},{7,4},{8,11},{9,10},{10,... | collective-permute-start | bytes 12296 | tf_op jit(solution)/shard_map/ppermute | solution.py:617
  4.8 8.8 %collective-permute-start.4 = (bf16[256,128]{1,0:T(8,128)(2,1)S(1)}, bf16[256,128]{1,0:T(8,128)(2,1)S(1)}, u32[]{:S(2)}, u32[]{:S(2)}) collective-permute-start(bf16[256,128]{1,0:T(8,128)(2,1)S(1)} %get-tuple-element.21.own_ref), channel_id=1, source_target_pairs={{8,0},{12,4},{0,8},{4,12},{9,1},{13,5},{1,9},{5,13},{10,2},{14,6},... | collective-permute-start | bytes 196616 | tf_op jit(solution)/shard_map/ppermute | solution.py:654
  9.6 8.4 %collective-permute-start.5 = (bf16[288,128]{1,0:T(8,128)(2,1)S(1)}, bf16[288,128]{1,0:T(8,128)(2,1)S(1)}, u32[]{:S(2)}, u32[]{:S(2)}) collective-permute-start(bf16[288,128]{1,0:T(8,128)(2,1)S(1)} %get-tuple-element.27.refs_4_.refs_0_), channel_id=1, source_target_pairs={{12,0},{0,4},{4,8},{8,12},{13,1},{1,5},{5,9},{9,13},{14,2},{2,6},{... | collective-permute-start | bytes 221192 | tf_op jit(solution)/shard_map/ppermute | solution.py:654
  11.3 6.8 %collective-permute-start.3 = (bf16[288,128]{1,0:T(8,128)(2,1)S(1)}, bf16[288,128]{1,0:T(8,128)(2,1)S(1)}, u32[]{:S(2)}, u32[]{:S(2)}) collective-permute-start(bf16[288,128]{1,0:T(8,128)(2,1)S(1)} %get-tuple-element.27.refs_4_.refs_0_), channel_id=1, source_target_pairs={{4,0},{8,4},{12,8},{0,12},{5,1},{9,5},{13,9},{1,13},{6,2},{10,6},{... | collective-permute-start | bytes 221192 | tf_op jit(solution)/shard_map/ppermute | solution.py:654
  13.5 4.6 %collective-permute-start.6 = (bf16[32,128]{1,0:T(8,128)(2,1)S(1)}, bf16[32,128]{1,0:T(8,128)(2,1)S(1)}, u32[]{:S(2)}, u32[]{:S(2)}) collective-permute-start(bf16[32,128]{1,0:T(8,128)(2,1)S(1)} %get-tuple-element.29), channel_id=1, source_target_pairs={{8,0},{12,4},{0,8},{4,12},{9,1},{13,5},{1,9},{5,13},{10,2},{14,6},... | collective-permute-start | bytes 24584 | tf_op jit(solution)/shard_map/ppermute | solution.py:654

commit v6 on v3

--- a/solution.py
+++ b/solution.py
@@ -20,6 +20,7 @@
 
 VMEM = pl.BlockSpec(memory_space=pltpu.VMEM)
 SMEM = pl.BlockSpec(memory_space=pltpu.SMEM)
+ANY = pl.BlockSpec(memory_space=pl.ANY)
 HBM = pl.BlockSpec(memory_space=pltpu.HBM)
 
 
@@ -153,7 +154,7 @@
 
 def edges_kernel(dims, *refs):
     count_gy, depth, rows, columns, few, count = dims
-    tiles, outs = refs[:few], refs[few + 1 :]
+    tiles, outs = refs[:few], refs[few + 2 :]
     g = lax.axis_index("gy")
     c = lax.axis_index("col")
     height = depth * rows
@@ -185,10 +186,7 @@
         sends = [jnp.where(g == 0, last, first)] if count_gy == 2 else [last, first]
         for n, send in enumerate(sends):
             send = send.astype(jnp.bfloat16)
-            outs[1 + 2 * n][pl.ds(at, TILE), :] = send
-            outs[2 + 2 * n][pl.ds(at, TILE), :] = jnp.where(
-                c == 0, send[:, BX:columns], send[:, 0:BX]
-            )
+            outs[1 + n][pl.ds(at, TILE), :] = send
 
     if few > 1:
         for i in range(count // 2):
@@ -197,16 +195,87 @@
         pl.loop(0, count // 2)(pair)
 
 
+def corner_kernel(edge_ref, corner_ref):
+    c = lax.axis_index("col")
+    corner_ref[...] = jnp.where(c == 0, edge_ref[:, BX:], edge_ref[:, 0:BX])
+
+
+def laplace(field, z, y):
+    centre = field[z][y]
+    last = lax.broadcasted_iota(jnp.int32, centre.shape, 1) == BX - 1
+    ahead = jnp.where(last, 0.0, pltpu.roll(centre, BX - 1, 1) - centre)
+    result = ahead - pltpu.roll(ahead, 1, 1)
+    beside = [
+        field[zz][yy]
+        for zz, yy in ((z - 1, y), (z + 1, y), (z, y - 1), (z, y + 1))
+        if 0 <= zz < len(field) and 0 <= yy < BY
+    ]
+    return result + (functools.reduce(jnp.add, beside) - float(len(beside)) * centre)
+
+
+def uptake_of(quarter, doc, oxy):
+    return quarter * doc * oxy / ((0.5 + jnp.abs(doc)) * (0.3 + jnp.abs(oxy)))
+
+
+def prepare_kernel(dims, solutes_ref, biomass_ref, _, *refs):
+    depth, slots = dims
+    outs, (state, biomass, mass, sems) = refs[:5], refs[5:]
+    size = depth * BY
+    copies = []
+    for group in range(slots // 8):
+        for k, (source, target) in enumerate(((solutes_ref, state), (biomass_ref, biomass))):
+            rows = (2 - k) * 8 * size
+            at = pl.ds(group * rows, rows)
+            copies.append(
+                pltpu.make_async_copy(source.at[at], target.at[at], sems.at[group, k])
+            )
+    for copy in copies:
+        copy.start()
+    for group in range(slots // 8):
+        copies[2 * group].wait()
+        copies[2 * group + 1].wait()
+        at = slice(group * 8 * size, (group + 1) * 8 * size)
+        mass[at, :] = biomass[at, :].astype(jnp.float32)
+
+        def rows_of(pitch, offset):
+            return pl.ds(group * 8 * pitch + offset, 8, stride=pitch)
+
+        grid = [(z, y) for z in range(depth) for y in range(BY)]
+        carbon, oxygen = [
+            [
+                [state[rows_of(2 * size, k * size + z * BY + y), :] for y in range(BY)]
+                for z in range(depth)
+            ]
+            for k in range(2)
+        ]
+        for z, y in grid:
+            at = group * 8 * size + (z * BY + y) * 8
+            at = slice(at, at + 8)
+            doc, oxy = carbon[z][y], oxygen[z][y]
+            quarter = 0.25 * mass[rows_of(size, z * BY + y), :]
+            uptake = uptake_of(quarter, doc, oxy)
+            values = (
+                doc - uptake,
+                oxy - uptake,
+                laplace(carbon, z, y),
+                laplace(oxygen, z, y),
+                quarter,
+            )
+            for out, value in zip(outs, values):
+                out[at, :] = value
+
+
 def column_kernel(dims, few, *refs):
-    count_gz, count_gy, depth, rows, columns, segment, slots = dims
+    count_gz, count_gy, depth, rows, columns, segment, slots, directions = dims
     tiles, refs = refs[:few], refs[few:]
     x_ref, refs = refs[0], refs[1:]
     top_refs, refs = refs[:2], refs[2:]
-    if count_gy == 2:
+    if directions == 1:
         bottom_refs = top_refs
     else:
         bottom_refs, refs = refs[:2], refs[2:]
-    t1_ref, bias_ref, t2_ref, bias2_ref, solutes_ref, biomass_ref, *refs = refs
+    t1_ref, bias_ref, t2_ref, bias2_ref, *refs = refs
+    carbon_ref, oxygen_ref, carbon_around_ref, oxygen_around_ref, quarter_ref, *refs = refs
     fractions_ref, next_ref, *refs = refs
     (
         edge_rows,
@@ -215,8 +284,6 @@
         bricks,
         arrived,
         state,
-        biomass,
-        mass,
         fractions,
         owner_rows,
         owner_table,
@@ -236,11 +303,6 @@
     first_tile = z_index if few > 1 else 0
     size = depth * BY
 
-    state_copy = pltpu.make_async_copy(solutes_ref, state, sems.at[0])
-    state_copy.start()
-    biomass_copy = pltpu.make_async_copy(biomass_ref, biomass, sems.at[1])
-    biomass_copy.start()
-
     def tile_rows(i, start, size):
         if not isinstance(start, int):
             start = pl.multiple_of(start, TILE)
@@ -257,7 +319,7 @@
             read_owners(i)
     else:
         pl.loop(0, count_gz)(read_owners)
-    table_copy = pltpu.make_async_copy(owner_rows, owner_table, sems.at[2])
+    table_copy = pltpu.make_async_copy(owner_rows, owner_table, sems.at[0])
     table_copy.start()
 
     def arrange(left, right, other):
@@ -370,12 +432,10 @@
             for zz in range(depth):
                 shifts(i, zz, tile * depth + zz + 2, None)
 
-        @pl.loop(0, depths, unroll=4)
-        def _(z):
-            first(z, None)
-
-        @pl.loop(0, depths, unroll=4)
-        def _(z):
+        first(0, None)
+        for z in range(depths):
+            if z + 1 < depths:
+                first(z + 1, None)
             second(z, z // depth, z % depth)
     else:
 
@@ -403,54 +463,29 @@
             for o in range(2):
                 values = jnp.concatenate([v[o * BY : o * BY + BY] for v in own], axis=0)
                 fractions[o, zz, :, xb * BX : (xb + 1) * BX] = values.astype(jnp.bfloat16)
-    fractions_copy = pltpu.make_async_copy(fractions, fractions_ref, sems.at[3])
+    fractions_copy = pltpu.make_async_copy(fractions, fractions_ref, sems.at[1])
     fractions_copy.start()
 
     table_copy.wait()
-
-    @pl.loop(0, slots)
-    def _(j):
+    for j in range(slots):
         brick_of_slot[j] = -1
 
     @pl.loop(0, count_gz)
     def _(i):
-        tile = lax.rem(first_tile + i, count_gz)
+        first = lax.rem(first_tile + i, count_gz) * capacity
         rank = jnp.int32(0)
         for b in range(brick_count):
             mine = owner_table[i, 0, b] == z_index
-
-            @pl.when(mine)
-            def _():
-                brick_of_slot[tile * capacity + rank] = b
-
+            brick_of_slot[jnp.where(mine, first + rank, slots)] = b
             rank = rank + mine.astype(jnp.int32)
 
-    biomass_copy.wait()
-
-    @pl.loop(0, slots)
+    @pl.loop(0, slots, unroll=8)
     def _(j):
         brick = brick_of_slot[j]
         values = bricks[j // capacity, jnp.maximum(brick, 0)]
         values = jnp.where(brick >= 0, values, 0.0)
         at = pl.multiple_of(j * (2 * size), 8)
         arrived[pl.ds(at, 2 * size), :] = values.reshape(2 * size, BX)
-        at = pl.multiple_of(j * size, size)
-        mass[pl.ds(at, size), :] = 0.25 * biomass[pl.ds(at, size), :].astype(jnp.float32)
-
-    last = lax.broadcasted_iota(jnp.int32, (8, BX), 1) == BX - 1
-
-    def laplace(field, z, y):
-        centre = field[z][y]
-        ahead = jnp.where(last, 0.0, pltpu.roll(centre, BX - 1, 1) - centre)
-        result = ahead - pltpu.roll(ahead, 1, 1)
-        beside = [
-            field[zz][yy]
-            for zz, yy in ((z - 1, y), (z + 1, y), (z, y - 1), (z, y + 1))
-            if 0 <= zz < depth and 0 <= yy < BY
-        ]
-        return result + (functools.reduce(jnp.add, beside) - float(len(beside)) * centre)
-
-    state_copy.wait()
 
     def next_copy(group):
         at = pl.ds(pl.multiple_of(group * 16 * size, 16 * size), 16 * size)
@@ -458,39 +493,46 @@
 
     @pl.loop(0, slots // 8)
     def _(group):
-        def rows_of(pitch, offset):
-            return pl.ds(group * 8 * pitch + offset, 8, stride=pitch)
-
         grid = [(z, y) for z in range(depth) for y in range(BY)]
-        carbon = [
-            [state[rows_of(2 * size, z * BY + y), :] for y in range(BY)] for z in range(depth)
+
+        def load(ref):
+            base = group * (8 * size)
+            return [
+                [
+                    ref[pl.ds(pl.multiple_of(base + (z * BY + y) * 8, 8), 8), :]
+                    for y in range(BY)
+                ]
+                for z in range(depth)
+            ]
+
+        def rows_of(offset):
+            return pl.ds(group * 16 * size + offset, 8, stride=2 * size)
+
+        quarter = load(quarter_ref)
+        pore = [[arrived[rows_of(z * 8 + y), :] for y in range(BY)] for z in range(depth)]
+        organic = [
+            [0.3 * arrived[rows_of(z * 8 + BY + y), :] for y in range(BY)] for z in range(depth)
         ]
-        oxygen = [
-            [state[rows_of(2 * size, size + z * BY + y), :] for y in range(BY)]
-            for z in range(depth)
-        ]
-        pore = [[arrived[rows_of(2 * size, z * 8 + y), :] for y in range(BY)] for z in range(depth)]
-        organic = [
-            [0.3 * arrived[rows_of(2 * size, z * 8 + BY + y), :] for y in range(BY)]
-            for z in range(depth)
-        ]
-        quarter = [[mass[rows_of(size, z * BY + y), :] for y in range(BY)] for z in range(depth)]
         slow = [[0.12 * p for p in row] for row in pore]
         fast = [[0.16 * p for p in row] for row in pore]
-        for _ in range(STEPS):
+        carbon, oxygen = load(carbon_ref), load(oxygen_ref)
+        around = load(carbon_around_ref), load(oxygen_around_ref)
+        for z, y in grid:
+            carbon[z][y] += slow[z][y] * around[0][z][y] + organic[z][y]
+            oxygen[z][y] += fast[z][y] * around[1][z][y]
+        for _ in range(STEPS - 1):
             carbon_new = [[None] * BY for _ in range(depth)]
             oxygen_new = [[None] * BY for _ in range(depth)]
             for z, y in grid:
                 doc, oxy = carbon[z][y], oxygen[z][y]
-                uptake = quarter[z][y] * doc * oxy
-                uptake = uptake / ((0.5 + jnp.abs(doc)) * (0.3 + jnp.abs(oxy)))
+                uptake = uptake_of(quarter[z][y], doc, oxy)
                 gain = organic[z][y] - uptake
                 carbon_new[z][y] = doc + slow[z][y] * laplace(carbon, z, y) + gain
                 oxygen_new[z][y] = oxy + fast[z][y] * laplace(oxygen, z, y) - uptake
             carbon, oxygen = carbon_new, oxygen_new
         for z, y in grid:
-            state[rows_of(2 * size, z * BY + y), :] = carbon[z][y]
-            state[rows_of(2 * size, size + z * BY + y), :] = oxygen[z][y]
+            state[rows_of(z * BY + y), :] = carbon[z][y]
+            state[rows_of(size + z * BY + y), :] = oxygen[z][y]
         next_copy(group).start()
 
     @pl.loop(0, slots // 8)
@@ -536,6 +578,28 @@
     else:
         tiles = [lax.all_gather(payload, "gz", axis=0, tiled=False)]
 
+    cells = depth * BY
+    prepared = pl.pallas_call(
+        functools.partial(prepare_kernel, (depth, slots)),
+        out_shape=[shape((slots * cells, BX), f32)] * 5,
+        in_specs=[HBM, HBM, ANY],
+        out_specs=[VMEM] * 5,
+        scratch_shapes=[
+            pltpu.VMEM((slots * 2 * cells, BX), f32),
+            pltpu.VMEM((slots * cells, BX), bf16),
+            pltpu.VMEM((slots * cells, BX), f32),
+            pltpu.SemaphoreType.DMA((slots // 8, 2)),
+        ],
+        compiler_params=pltpu.CompilerParams(vmem_limit_bytes=12 * 2**20),
+        cost_estimate=pl.CostEstimate(
+            flops=60 * slots * cells * BX, bytes_accessed=2**20, transcendentals=0
+        ),
+        name="prepare",
+    )(
+        in_hbm(solutes.reshape(slots * 2 * cells, BX)),
+        in_hbm(biomass.reshape(slots * cells, BX)),
+        payload,
+    )
     t1, bias, t2, bias2 = pl.pallas_call(
         functools.partial(banded_kernel, (window, count_gy)),
         out_shape=(
@@ -544,7 +608,7 @@
             shape((6 * HALF, 3 * TALL), bf16),
             shape((2 * HALF, 2 * window), f32),
         ),
-        in_specs=[HBM, HBM, HBM, HBM, pl.BlockSpec(memory_space=pl.ANY)],
+        in_specs=[HBM, HBM, HBM, HBM, ANY],
         out_specs=(VMEM, VMEM, VMEM, VMEM),
         scratch_shapes=[
             pltpu.VMEM((CHANNELS, 27), bf16),
@@ -566,44 +630,47 @@
         payload,
     )
 
-    edge_shapes = [shape((2 * depths, columns), bf16), shape((2 * depths, BX), bf16)]
-    sent = pl.pallas_call(
+    if count_gy == 2:
+        ways = [[(0, 1), (1, 0)]]
+    else:
+        up = [(i, i + 1) for i in range(count_gy - 1)]
+        ways = [up, [(j, i) for i, j in up]]
+    directions = len(ways)
+    swap = [(0, 1), (1, 0)]
+    near, *sent = pl.pallas_call(
         functools.partial(edges_kernel, (count_gy, depth, rows, columns, few, count_gz)),
-        out_shape=[shape((depths * rows, BX), bf16)] + edge_shapes * (1 if count_gy == 2 else 2),
-        in_specs=[VMEM] * few + [pl.BlockSpec(memory_space=pl.ANY)],
-        out_specs=[VMEM] * (3 if count_gy == 2 else 5),
+        out_shape=[shape((depths * rows, BX), bf16)]
+        + [shape((2 * depths, columns), bf16)] * directions,
+        in_specs=[VMEM] * few + [ANY, ANY],
+        out_specs=[VMEM] * (1 + directions),
         compiler_params=pltpu.CompilerParams(vmem_limit_bytes=16 * 2**20),
         name="edges",
-    )(*tiles, bias2)
-
-    def over(pairs):
-        return [
-            (gy * count_col + col, to * count_col + 1 - col)
-            for gy, to in pairs
-            for col in range(count_col)
-        ]
-
-    beside = lax.ppermute(sent[0], "col", [(0, 1), (1, 0)])
-    if count_gy == 2:
-        directions = [[(0, 1), (1, 0)]]
-    else:
-        up = [(i, i + 1) for i in range(count_gy - 1)]
-        directions = [up, [(j, i) for i, j in up]]
+    )(*tiles, bias2, prepared[-1])
     edges = []
-    for k, pairs in enumerate(directions):
-        edges.append(lax.ppermute(sent[1 + 2 * k], "gy", pairs))
-        edges.append(lax.ppermute(sent[2 + 2 * k], ("gy", "col"), over(pairs)))
-
-    cells = depth * BY
+    for pairs, edge in zip(ways, sent):
+        edge = lax.ppermute(edge, "gy", pairs)
+        corner = pl.pallas_call(
+            corner_kernel,
+            out_shape=shape((2 * depths, BX), bf16),
+            in_specs=[VMEM],
+            out_specs=VMEM,
+            compiler_params=pltpu.CompilerParams(vmem_limit_bytes=4 * 2**20),
+            name="corner",
+        )(edge)
+        edges += [edge, lax.ppermute(corner, "col", swap)]
+    near = lax.ppermute(near, "col", swap)
+
     fractions, solutes_next = pl.pallas_call(
         functools.partial(
-            column_kernel, (count_gz, count_gy, depth, rows, columns, segment, slots), few
+            column_kernel,
+            (count_gz, count_gy, depth, rows, columns, segment, slots, directions),
+            few,
         ),
         out_shape=(
             shape((2, depth, rows, columns), bf16),
             shape((slots * 2 * cells, BX), f32),
         ),
-        in_specs=[VMEM] * (few + 1 + len(edges) + 4) + [HBM, HBM],
+        in_specs=[VMEM] * (few + 1 + len(edges) + 9),
         out_specs=(HBM, HBM),
         scratch_shapes=[
             pltpu.VMEM((2, 2 * depths, window), f32),
@@ -612,13 +679,11 @@
             pltpu.VMEM((count_gz, brick_count, depth, 8, BX), f32),
             pltpu.VMEM((slots * 2 * cells, BX), f32),
             pltpu.VMEM((slots * 2 * cells, BX), f32),
-            pltpu.VMEM((slots * cells, BX), bf16),
-            pltpu.VMEM((slots * cells, BX), f32),
             pltpu.VMEM((2, depth, rows, columns), bf16),
             pltpu.VMEM((count_gz, 8, BX), jnp.int32),
             pltpu.SMEM((count_gz, 8, BX), jnp.int32),
-            pltpu.SMEM((slots,), jnp.int32),
-            pltpu.SemaphoreType.DMA((4,)),
+            pltpu.SMEM((slots + 1,), jnp.int32),
+            pltpu.SemaphoreType.DMA((2,)),
             pltpu.SemaphoreType.DMA((slots // 8,)),
         ],
         compiler_params=pltpu.CompilerParams(vmem_limit_bytes=40 * 2**20),
@@ -630,14 +695,13 @@
         name="column",
     )(
         *tiles,
-        beside,
+        near,
         *edges,
         t1,
         bias,
         t2,
         bias2,
-        in_hbm(solutes.reshape(slots * 2 * cells, BX)),
-        in_hbm(biomass.reshape(slots * cells, BX)),
+        *prepared,
     )
     return fractions, solutes_next.reshape(solutes.shape)
 

time: 26.3 us -> 26.1 us (level)
  waiting for transfers between devices: 4.87 us -> 3.41 us
  Pallas kernels: 11.6 us -> 13 us
    ppermute x3, waiting for transfers between devices: 2.05 us -> 0.03 us  [per_device(): lax.ppermute(payload, 'gz', [((i + s) % count_gz, i) for i in range(count...]
    pallas_call x0 -> x2, Pallas kernels: none -> 2 us  [the longest x1 2 us: per_device(): pl.pallas_call(functools.partial(prepare_kernel, (depth, slots)), out_sha...]
    ppermute x3, waiting for transfers between devices: 2.82 us -> 3.37 us  [the longest x1 2.2 us: per_device(): edge = lax.ppermute(edge, 'gy', pairs)]
    pallas_call x1, Pallas kernels: 9.24 us -> 8.73 us  [per_device(): pl.pallas_call(functools.partial(column_kernel, (count_gz, count_gy, dept...]
  transfers between devices with their start and end apart: 6 -> 6, of which waited for: 3 -> 2; matrix products, arithmetic and copies ran while one was open for 0% -> 0% of each run, Pallas kernels for 6% -> 13%
where the time goes in v6:
time: 26.1 us; the launch traced here: 25.8 us
  Pallas kernels  13 us (50%)
  starting transfers between devices  8.69 us (33%)
  waiting for transfers between devices  3.41 us (13%)
  between operations  0.69 us (3%)
    pallas_call x1, Pallas kernels, per_device(): pl.pallas_call(functools.partial(column_kernel, (count_gz, count_gy, dept...  8.73 us
    ppermute x3, starting transfers between devices, per_device(): lax.ppermute(payload, 'gz', [((i + s) % count_gz, i) for i in range(count...  7.01 us
    ppermute x1, waiting for transfers between devices, per_device(): edge = lax.ppermute(edge, 'gy', pairs)  2.2 us
    pallas_call x1, Pallas kernels, per_device(): pl.pallas_call(functools.partial(prepare_kernel, (depth, slots)), out_sha...  2 us
    ppermute x1, starting transfers between devices, per_device(): edge = lax.ppermute(edge, 'gy', pairs)  1.6 us
    pallas_call x1, Pallas kernels, per_device(): pl.pallas_call(functools.partial(banded_kernel, (window, count_gy)), out_...  1.47 us
    ppermute x1, waiting for transfers between devices, per_device(): edges += [edge, lax.ppermute(corner, 'col', swap)]  1.17 us
    pallas_call x1, Pallas kernels, per_device(): pl.pallas_call(pack_kernel, out_shape=shape((columns // BX * height + TIL...  0.82 us
  transfers between devices with their start and end apart: 6, of which 2 were waited for; matrix products, arithmetic and copies ran while one was open for 0% of the time, Pallas kernels for 13%

profile of v6, /device:TPU:0, one launch (start us, length us, event | category | flops | bytes accessed | tf_op | source)
XLA Modules:
  0.0 25.8 jit_solution(7613762912929726922)
XLA Ops:
  0.6 0.8 %pack.1.refs_4_._.refs_0_ = bf16[272,128]{1,0:T(8,128)(2,1)S(1)} custom-call(bf16[128,256]{1,0:T(8,128)(2,1)} %bitcast.13, s32[1,16]{1,0:T(1,128)} %bitcast.14), custom_call_target="tpu_custom_call" | custom-call | tf_op jit(solution)/shard_map/pack/pallas_call | solution.py:559
  1.5 3.1 %collective-permute-start.2 = (bf16[272,128]{1,0:T(8,128)(2,1)S(1)}, bf16[272,128]{1,0:T(8,128)(2,1)S(1)}, u32[]{:S(2)}, u32[]{:S(2)}) collective-permute-start(bf16[272,128]{1,0:T(8,128)(2,1)S(1)} %pack.1.refs_4_._.refs_0_), channel_id=1, source_target_pairs={{12,0},{0,4},{4,8},{8,12},{13,1},{1,5},{5,9},{9,13},{14,2},{2,6},{... | collective-permute-start | bytes 208904 | tf_op jit(solution)/shard_map/ppermute | solution.py:575
  4.5 2.6 %collective-permute-start.1 = (bf16[272,128]{1,0:T(8,128)(2,1)S(1)}, bf16[272,128]{1,0:T(8,128)(2,1)S(1)}, u32[]{:S(2)}, u32[]{:S(2)}) collective-permute-start(bf16[272,128]{1,0:T(8,128)(2,1)S(1)} %pack.1.refs_4_._.refs_0_), channel_id=1, source_target_pairs={{8,0},{12,4},{0,8},{4,12},{9,1},{13,5},{1,9},{5,13},{10,2},{14,6},... | collective-permute-start | bytes 208904 | tf_op jit(solution)/shard_map/ppermute | solution.py:575
  7.1 1.3 %collective-permute-start = (bf16[272,128]{1,0:T(8,128)(2,1)S(1)}, bf16[272,128]{1,0:T(8,128)(2,1)S(1)}, u32[]{:S(2)}, u32[]{:S(2)}) collective-permute-start(bf16[272,128]{1,0:T(8,128)(2,1)S(1)} %pack.1.refs_4_._.refs_0_), channel_id=1, source_target_pairs={{4,0},{8,4},{12,8},{0,12},{5,1},{9,5},{13,9},{1,13},{6,2},{10,6},{... | collective-permute-start | bytes 208904 | tf_op jit(solution)/shard_map/ppermute | solution.py:575
  8.5 2.0 %prepare.1 = (f32[512,128]{1,0:T(8,128)S(1)}, f32[512,128]{1,0:T(8,128)S(1)}, f32[512,128]{1,0:T(8,128)S(1)}, f32[512,128]{1,0:T(8,128)S(1)}, f32[512,128]{1,0:T(8,128)S(1)}) custom-call(f32[1024,128]{1,0:T(8,128)} %bitcast.11, bf16[512,128]{1,0:T(8,128)(2,1)} %bitcast.12, bf16[272,128]{1,0:T(8,128)(2,1)S(1)} %pack.1.refs_4_._.refs_0_), custom_call_target="tpu_custom_call" | custom-call | flops 3932160 | bytes 1048576 | tf_op jit(solution)/shard_map/prepare/pallas_call | solution.py:582
  10.5 1.5 %banded.1 = (bf16[144,192]{1,0:T(8,128)(2,1)S(1)}, f32[144,768]{1,0:T(8,128)S(1)}, bf16[96,432]{1,0:T(8,128)(2,1)S(1)}, f32[32,768]{1,0:T(8,128)S(1)}) custom-call(bf16[8,27]{1,0:T(8,128)(2,1)} %bitcast.16, f32[8]{0:T(128)} %refs_1_.1, bf16[16,27]{1,0:T(8,128)(2,1)} %bitcast.15, f32[2]{0:T(128)} %refs_3_.1, bf16[272,128]{1,0:T(8,128)(2,1)S(1)} %pack.1.refs_4_._.refs_0_), custom_call_target="tpu_custom_call" | custom-call | flops 20971520 | bytes 4194304 | tf_op jit(solution)/shard_map/banded/pallas_call | solution.py:603
  12.0 0.0 collective-permute-done.2.refs_3_
  12.0 0.0 collective-permute-done.1.refs_2_
  12.0 0.0 collective-permute-done.refs_1_
  12.0 0.1 collective-permute-start.3
  12.1 1.6 %collective-permute-start.4 = (bf16[32,256]{1,0:T(8,128)(2,1)S(1)}, bf16[32,256]{1,0:T(8,128)(2,1)S(1)}, u32[]{:S(2)}, u32[]{:S(2)}) collective-permute-start(bf16[32,256]{1,0:T(8,128)(2,1)S(1)} %get-tuple-element.18), channel_id=1, source_target_pairs={{0,2},{2,0},{1,3},{3,1},{4,6},{6,4},{5,7},{7,5},{8,10},{10,8},{9,1... | collective-permute-start | bytes 49160 | tf_op jit(solution)/shard_map/ppermute | solution.py:651
  13.7 2.2 %collective-permute-done.4.edge_ref.refs_5_ = bf16[32,256]{1,0:T(8,128)(2,1)S(1)} collective-permute-done((bf16[32,256]{1,0:T(8,128)(2,1)S(1)}, bf16[32,256]{1,0:T(8,128)(2,1)S(1)}, u32[]{:S(2)}, u32[]{:S(2)}) %collective-permute-start.4) | collective-permute-done | bytes 16416 | tf_op jit(solution)/shard_map/ppermute | solution.py:651
  15.9 0.0 collective-permute-start.5
  15.9 1.2 %collective-permute-done.5.refs_6_ = bf16[32,128]{1,0:T(8,128)(2,1)S(1)} collective-permute-done((bf16[32,128]{1,0:T(8,128)(2,1)S(1)}, bf16[32,128]{1,0:T(8,128)(2,1)S(1)}, u32[]{:S(2)}, u32[]{:S(2)}) %collective-permute-start.5) | collective-permute-done | bytes 8224 | tf_op jit(solution)/shard_map/ppermute | solution.py:660
  17.1 0.0 collective-permute-done.3.refs_4_
  17.1 8.7 %column.1 = (bf16[2,4,32,256]{3,2,1,0:T(8,128)(2,1)}, f32[1024,128]{1,0:T(8,128)}) custom-call(bf16[272,128]{1,0:T(8,128)(2,1)S(1)} %pack.1.refs_4_._.refs_0_, bf16[272,128]{1,0:T(8,128)(2,1)S(1)} %collective-permute-done.refs_1_, bf16[272,128]{1,0:T(8,128)(2,1)S(1)} %collective-permute-done.1.refs_2_, bf16[272,128]{1,0:T(8,128)(2,1)S(1)} %collective-permute-done.2.refs_3_, ...), custom_call_target="tpu_custom_call" | custom-call | flops 1698693120 | bytes 4194304 | tf_op jit(solution)/shard_map/column/pallas_call | solution.py:663
  (2 shorter events, 0.0 us)
Async XLA Ops:
  1.5 10.5 %collective-permute-start.2 = (bf16[272,128]{1,0:T(8,128)(2,1)S(1)}, bf16[272,128]{1,0:T(8,128)(2,1)S(1)}, u32[]{:S(2)}, u32[]{:S(2)}) collective-permute-start(bf16[272,128]{1,0:T(8,128)(2,1)S(1)} %pack.1.refs_4_._.refs_0_), channel_id=1, source_target_pairs={{12,0},{0,4},{4,8},{8,12},{13,1},{1,5},{5,9},{9,13},{14,2},{2,6},{... | collective-permute-start | bytes 208904 | tf_op jit(solution)/shard_map/ppermute | solution.py:575
  4.5 7.4 %collective-permute-start.1 = (bf16[272,128]{1,0:T(8,128)(2,1)S(1)}, bf16[272,128]{1,0:T(8,128)(2,1)S(1)}, u32[]{:S(2)}, u32[]{:S(2)}) collective-permute-start(bf16[272,128]{1,0:T(8,128)(2,1)S(1)} %pack.1.refs_4_._.refs_0_), channel_id=1, source_target_pairs={{8,0},{12,4},{0,8},{4,12},{9,1},{13,5},{1,9},{5,13},{10,2},{14,6},... | collective-permute-start | bytes 208904 | tf_op jit(solution)/shard_map/ppermute | solution.py:575
  7.1 4.9 %collective-permute-start = (bf16[272,128]{1,0:T(8,128)(2,1)S(1)}, bf16[272,128]{1,0:T(8,128)(2,1)S(1)}, u32[]{:S(2)}, u32[]{:S(2)}) collective-permute-start(bf16[272,128]{1,0:T(8,128)(2,1)S(1)} %pack.1.refs_4_._.refs_0_), channel_id=1, source_target_pairs={{4,0},{8,4},{12,8},{0,12},{5,1},{9,5},{13,9},{1,13},{6,2},{10,6},{... | collective-permute-start | bytes 208904 | tf_op jit(solution)/shard_map/ppermute | solution.py:575
  12.0 5.1 %collective-permute-start.3 = (bf16[512,128]{1,0:T(8,128)(2,1)S(1)}, bf16[512,128]{1,0:T(8,128)(2,1)S(1)}, u32[]{:S(2)}, u32[]{:S(2)}) collective-permute-start(bf16[512,128]{1,0:T(8,128)(2,1)S(1)} %get-tuple-element.17), channel_id=1, source_target_pairs={{0,1},{1,0},{2,3},{3,2},{4,5},{5,4},{6,7},{7,6},{8,9},{9,8},{10,11... | collective-permute-start | bytes 393224 | tf_op jit(solution)/shard_map/ppermute | solution.py:661
  12.1 3.8 %collective-permute-start.4 = (bf16[32,256]{1,0:T(8,128)(2,1)S(1)}, bf16[32,256]{1,0:T(8,128)(2,1)S(1)}, u32[]{:S(2)}, u32[]{:S(2)}) collective-permute-start(bf16[32,256]{1,0:T(8,128)(2,1)S(1)} %get-tuple-element.18), channel_id=1, source_target_pairs={{0,2},{2,0},{1,3},{3,1},{4,6},{6,4},{5,7},{7,5},{8,10},{10,8},{9,1... | collective-permute-start | bytes 49160 | tf_op jit(solution)/shard_map/ppermute | solution.py:651
  15.9 1.2 %collective-permute-start.5 = (bf16[32,128]{1,0:T(8,128)(2,1)S(1)}, bf16[32,128]{1,0:T(8,128)(2,1)S(1)}, u32[]{:S(2)}, u32[]{:S(2)}) collective-permute-start(bf16[32,128]{1,0:T(8,128)(2,1)S(1)} %corner.1), channel_id=1, source_target_pairs={{0,1},{1,0},{2,3},{3,2},{4,5},{5,4},{6,7},{7,6},{8,9},{9,8},{10,11... | collective-permute-start | bytes 24584 | tf_op jit(solution)/shard_map/ppermute | solution.py:660

commit v7 on v6

--- a/solution.py
+++ b/solution.py
@@ -80,8 +80,15 @@
         copy.wait()
 
 
+def upper_lanes(first):
+    half = BX // 2
+    start = first + jnp.where(lax.axis_index("col") == 0, 0, half)
+    return start, start + half
+
+
 def banded_kernel(dims, *refs):
-    window, count_gy = dims
+    columns, count_gy = dims
+    lanes = 2 * columns + BX
     sources, refs = refs[:4], refs[5:]
     t1_ref, bias_ref, t2_ref, bias2_ref, *local, sems = refs
     copies = [
@@ -113,12 +120,14 @@
         values = jnp.dot(w1, one_hot(tap == base + 3 * dy), preferred_element_type=jnp.float32)
         total = jnp.where(distance == dy, values, total)
     t1_ref[...] = total.astype(jnp.bfloat16)
-    row, column = iotas((TALL, 2 * window))
-    bias = jnp.zeros((TALL, 2 * window), jnp.float32)
+    row, column = iotas((TALL, lanes))
+    bias = jnp.zeros((TALL, lanes), jnp.float32)
     for k in range(CHANNELS):
         bias = jnp.where((row & (CHANNELS - 1)) == k, b1_ref[k], bias)
-    outside = ((row < CHANNELS) & (column < window) & (g == 0)) | (
-        (row >= TALL - CHANNELS) & (column >= window) & (g == count_gy - 1)
+    start, stop = upper_lanes(2 * columns)
+    upper = (column < columns) | ((column >= start) & (column < stop))
+    outside = ((row < CHANNELS) & upper & (g == 0)) | (
+        (row >= TALL - CHANNELS) & jnp.logical_not(upper) & (g == count_gy - 1)
     )
     bias_ref[...] = jnp.where(outside, OUTSIDE, bias)
     channel, column = iotas((CHANNELS, 3 * TALL))
@@ -148,7 +157,7 @@
             values = values + jnp.dot(pick, wide[o], preferred_element_type=jnp.float32)
         total = jnp.where(hidden_row - y == dy, values, total)
     t2_ref[...] = total.astype(jnp.bfloat16)
-    row, _ = iotas((2 * HALF, 2 * window))
+    row, _ = iotas((2 * HALF, columns))
     bias2_ref[...] = jnp.where(((row >> 2) & 1) == 0, b2_ref[0], b2_ref[1])
 
 
@@ -214,7 +223,9 @@
 
 
 def uptake_of(quarter, doc, oxy):
-    return quarter * doc * oxy / ((0.5 + jnp.abs(doc)) * (0.3 + jnp.abs(oxy)))
+    divisor = (0.5 + jnp.abs(doc)) * (0.3 + jnp.abs(oxy))
+    inverse = pl.reciprocal(divisor, approx=True)
+    return quarter * doc * oxy * (inverse * (2.0 - divisor * inverse))
 
 
 def prepare_kernel(dims, solutes_ref, biomass_ref, _, *refs):
@@ -295,6 +306,7 @@
     g = lax.axis_index("gy")
     c = lax.axis_index("col")
     window = columns + BX
+    lanes = 2 * columns + BX
     brick_rows = HALF // BY
     brick_columns = columns // BX
     brick_count = rows // BY * brick_columns
@@ -323,14 +335,10 @@
     table_copy.start()
 
     def arrange(left, right, other):
-        return jnp.concatenate(
-            [
-                jnp.where(c == 0, left, other),
-                jnp.where(c == 0, right, left),
-                jnp.where(c == 0, other, right),
-            ],
-            axis=1,
-        )
+        lane = lax.broadcasted_iota(jnp.int32, other.shape, 1)
+        near = jnp.where(c == 0, 0, BX - 2)
+        other = jnp.where((lane >= near) & (lane < near + 2), other, 0.0).astype(other.dtype)
+        return jnp.concatenate([left, right, other], axis=1)
 
     for k, pair in enumerate((top_refs, bottom_refs)):
         exists = (g > 0) if k == 0 else (g < count_gy - 1)
@@ -339,12 +347,21 @@
         edge_rows[k] = values * exists.astype(jnp.float32)
 
     def moved(values):
-        lane = lax.broadcasted_iota(jnp.int32, values.shape, 1)
-        return (
-            jnp.where(lane == 0, 0.0, pltpu.roll(values, 1, 1)),
-            values,
-            jnp.where(lane == window - 1, 0.0, pltpu.roll(values, window - 1, 1)),
+        return pltpu.roll(values, 1, 1), values, pltpu.roll(values, window - 1, 1)
+
+    def shared(upper, lower):
+        lane = lax.broadcasted_iota(jnp.int32, upper.shape, 1)
+        start, stop = upper_lanes(0)
+        return jnp.where(
+            (lane >= start) & (lane < stop), upper, pltpu.roll(lower, BX // 2, 1)
         )
+
+    def keep(slot, rows_at, upper, lower):
+        parts = (upper[:, 0:columns], lower[:, 0:columns])
+        for h, part in enumerate(parts):
+            shifted[slot, rows_at, h * columns : (h + 1) * columns] = part.astype(jnp.bfloat16)
+        part = shared(upper[:, columns:], lower[:, columns:])
+        shifted[slot, rows_at, 2 * columns : lanes] = part.astype(jnp.bfloat16)
 
     def edge_pair(k, at):
         if isinstance(at, int):
@@ -370,19 +387,16 @@
             jnp.concatenate([top, halves[1][0:2]], axis=0),
             jnp.concatenate([halves[0][HALF - 2 :], bottom], axis=0),
         ]
-        for h in range(2):
-            lanes = slice(h * window, (h + 1) * window)
-            for dx, values in enumerate(moved(halves[h])):
-                shifted[slot, dx * HALF : (dx + 1) * HALF, lanes] = values.astype(jnp.bfloat16)
-            values = jnp.concatenate(
-                [*moved(seams[h]), jnp.zeros((4, window), jnp.float32)], axis=0
-            )
-            shifted[slot, 3 * HALF : PART, lanes] = values.astype(jnp.bfloat16)
+        for dx, (upper, lower) in enumerate(zip(moved(halves[0]), moved(halves[1]))):
+            keep(slot, slice(dx * HALF, (dx + 1) * HALF), upper, lower)
+        rest = jnp.zeros((4, window), jnp.float32)
+        upper, lower = [jnp.concatenate([*moved(seam), rest], axis=0) for seam in seams]
+        keep(slot, slice(3 * HALF, PART), upper, lower)
 
     def first(z, valid):
         total = jnp.dot(
             t1_ref[...],
-            shifted[pl.ds(z + 1, 3)].reshape(3 * PART, 2 * window),
+            shifted[pl.ds(z + 1, 3)].reshape(3 * PART, lanes),
             preferred_element_type=jnp.float32,
         )
         values = jnp.maximum(total + bias_ref[...], 0.0)
@@ -391,26 +405,29 @@
         hidden[z + 1] = values.astype(jnp.bfloat16)
 
     height = 2 * HALF
-    lane = lax.broadcasted_iota(jnp.int32, (height, 2 * window), 1)
-    left_edge = (lane == 0) | (lane == window)
-    right_edge = (lane == window - 1) | (lane == 2 * window - 1)
+    lane = lax.broadcasted_iota(jnp.int32, (height, columns), 1)
 
     def second(z, t, zz):
         total = jnp.dot(
             t2_ref[...],
-            hidden[pl.ds(z, 3)].reshape(3 * TALL, 2 * window),
+            hidden[pl.ds(z, 3)].reshape(3 * TALL, lanes),
             preferred_element_type=jnp.float32,
         )
-        before = pltpu.roll(total[0:height], 1, 1)
-        after = pltpu.roll(total[2 * height :], 2 * window - 1, 1)
-        total = total[height : 2 * height] + bias2_ref[...]
-        total = total + jnp.where(left_edge, 0.0, before)
-        total = total + jnp.where(right_edge, 0.0, after)
+        before = jnp.where(c == 0, 0.0, total[0:height, 2 * columns :])
+        after = jnp.where(c == 0, total[2 * height :, 2 * columns :], 0.0)
         for h in range(2):
-            at = h * window
-            own = jnp.where(
-                c == 0, total[:, at : at + columns], total[:, at + BX : at + window]
+            at = slice(h * columns, (h + 1) * columns)
+            left = pltpu.roll(before, 1 + h * BX // 2, 1)
+            left = jnp.concatenate([left] * brick_columns, axis=1)
+            left = jnp.where(lane == 0, left, pltpu.roll(total[0:height, at], 1, 1))
+            right = pltpu.roll(after, BX - 1 - h * BX // 2, 1)
+            right = jnp.concatenate([right] * brick_columns, axis=1)
+            right = jnp.where(
+                lane == columns - 1,
+                right,
+                pltpu.roll(total[2 * height :, at], columns - 1, 1),
             )
+            own = total[height : 2 * height, at] + bias2_ref[...] + (left + right)
             values = 0.5 + 0.5 * jnp.tanh(0.5 * own)
             values = values.astype(jnp.bfloat16).astype(jnp.float32)
             for yb in range(brick_rows):
@@ -423,20 +440,23 @@
 
     depths = segment * depth
     if single:
-        shifted[1] = jnp.zeros((PART, 2 * window), jnp.bfloat16)
-        shifted[depths + 2] = jnp.zeros((PART, 2 * window), jnp.bfloat16)
-        hidden[0] = jnp.zeros((TALL, 2 * window), jnp.bfloat16)
-        hidden[depths + 1] = jnp.zeros((TALL, 2 * window), jnp.bfloat16)
+        shifted[1] = jnp.zeros((PART, lanes), jnp.bfloat16)
+        shifted[depths + 2] = jnp.zeros((PART, lanes), jnp.bfloat16)
+        hidden[0] = jnp.zeros((TALL, lanes), jnp.bfloat16)
+        hidden[depths + 1] = jnp.zeros((TALL, lanes), jnp.bfloat16)
         for i in range(count_gz):
             tile = lax.rem(first_tile + i, count_gz)
             for zz in range(depth):
                 shifts(i, zz, tile * depth + zz + 2, None)
 
-        first(0, None)
-        for z in range(depths):
-            if z + 1 < depths:
-                first(z + 1, None)
+        @pl.loop(0, depths, unroll=4)
+        def _(z):
+            first(z, None)
+
+        @pl.loop(0, depths, unroll=4)
+        def _(z):
             second(z, z // depth, z % depth)
+
     else:
 
         @pl.loop(0, count_gz // segment)
@@ -549,6 +569,7 @@
     depth, rows, columns = density.shape
     slots = solutes.shape[3]
     window = columns + BX
+    lanes = 2 * columns + BX
     segment = min(count_gz, 4)
     brick_count = (rows // BY) * (columns // BX)
     height = depth * rows
@@ -601,12 +622,12 @@
         payload,
     )
     t1, bias, t2, bias2 = pl.pallas_call(
-        functools.partial(banded_kernel, (window, count_gy)),
+        functools.partial(banded_kernel, (columns, count_gy)),
         out_shape=(
             shape((TALL, 3 * PART), bf16),
-            shape((TALL, 2 * window), f32),
+            shape((TALL, lanes), f32),
             shape((6 * HALF, 3 * TALL), bf16),
-            shape((2 * HALF, 2 * window), f32),
+            shape((2 * HALF, columns), f32),
         ),
         in_specs=[HBM, HBM, HBM, HBM, ANY],
         out_specs=(VMEM, VMEM, VMEM, VMEM),
@@ -674,8 +695,8 @@
         out_specs=(HBM, HBM),
         scratch_shapes=[
             pltpu.VMEM((2, 2 * depths, window), f32),
-            pltpu.VMEM((segment * depth + 4, PART, 2 * window), bf16),
-            pltpu.VMEM((segment * depth + 2, TALL, 2 * window), bf16),
+            pltpu.VMEM((segment * depth + 4, PART, lanes), bf16),
+            pltpu.VMEM((segment * depth + 2, TALL, lanes), bf16),
             pltpu.VMEM((count_gz, brick_count, depth, 8, BX), f32),
             pltpu.VMEM((slots * 2 * cells, BX), f32),
             pltpu.VMEM((slots * 2 * cells, BX), f32),
@@ -688,7 +709,7 @@
         ],
         compiler_params=pltpu.CompilerParams(vmem_limit_bytes=40 * 2**20),
         cost_estimate=pl.CostEstimate(
-            flops=2 * depths * 2 * window * TALL * (3 * PART + 3 * 6 * HALF),
+            flops=2 * depths * lanes * TALL * (3 * PART + 3 * 6 * HALF),
             bytes_accessed=4 * 2**20,
             transcendentals=0,
         ),

time: 26.1 us -> 27 us (1.034)
  Pallas kernels: 13 us -> 14 us
    pallas_call x1, Pallas kernels: 8.73 us -> 9.7 us  [per_device(): pl.pallas_call(functools.partial(column_kernel, (count_gz, count_gy, dept...]
where the time goes in v7:
time: 27 us; the launch traced here: 26.8 us
  Pallas kernels  14 us (52%)
  starting transfers between devices  8.69 us (32%)
  waiting for transfers between devices  3.41 us (13%)
  between operations  0.69 us (3%)
    pallas_call x1, Pallas kernels, per_device(): pl.pallas_call(functools.partial(column_kernel, (count_gz, count_gy, dept...  9.7 us
    ppermute x3, starting transfers between devices, per_device(): lax.ppermute(payload, 'gz', [((i + s) % count_gz, i) for i in range(count...  7.01 us
    ppermute x1, waiting for transfers between devices, per_device(): edge = lax.ppermute(edge, 'gy', pairs)  2.2 us
    pallas_call x1, Pallas kernels, per_device(): pl.pallas_call(functools.partial(prepare_kernel, (depth, slots)), out_sha...  2 us
    ppermute x1, starting transfers between devices, per_device(): edge = lax.ppermute(edge, 'gy', pairs)  1.6 us
    pallas_call x1, Pallas kernels, per_device(): pl.pallas_call(functools.partial(banded_kernel, (columns, count_gy)), out...  1.47 us
    ppermute x1, waiting for transfers between devices, per_device(): edges += [edge, lax.ppermute(corner, 'col', swap)]  1.17 us
    pallas_call x1, Pallas kernels, per_device(): pl.pallas_call(pack_kernel, out_shape=shape((columns // BX * height + TIL...  0.82 us
  transfers between devices with their start and end apart: 6, of which 2 were waited for; matrix products, arithmetic and copies ran while one was open for 0% of the time, Pallas kernels for 13%

profile of v7, /device:TPU:0, one launch (start us, length us, event | category | flops | bytes accessed | tf_op | source)
XLA Modules:
  0.0 26.8 jit_solution(4257486827931223139)
XLA Ops:
  0.6 0.8 %pack.1.refs_4_._.refs_0_ = bf16[272,128]{1,0:T(8,128)(2,1)S(1)} custom-call(bf16[128,256]{1,0:T(8,128)(2,1)} %bitcast.13, s32[1,16]{1,0:T(1,128)} %bitcast.14), custom_call_target="tpu_custom_call" | custom-call | tf_op jit(solution)/shard_map/pack/pallas_call | solution.py:580
  1.5 3.1 %collective-permute-start.2 = (bf16[272,128]{1,0:T(8,128)(2,1)S(1)}, bf16[272,128]{1,0:T(8,128)(2,1)S(1)}, u32[]{:S(2)}, u32[]{:S(2)}) collective-permute-start(bf16[272,128]{1,0:T(8,128)(2,1)S(1)} %pack.1.refs_4_._.refs_0_), channel_id=1, source_target_pairs={{12,0},{0,4},{4,8},{8,12},{13,1},{1,5},{5,9},{9,13},{14,2},{2,6},{... | collective-permute-start | bytes 208904 | tf_op jit(solution)/shard_map/ppermute | solution.py:596
  4.5 2.6 %collective-permute-start.1 = (bf16[272,128]{1,0:T(8,128)(2,1)S(1)}, bf16[272,128]{1,0:T(8,128)(2,1)S(1)}, u32[]{:S(2)}, u32[]{:S(2)}) collective-permute-start(bf16[272,128]{1,0:T(8,128)(2,1)S(1)} %pack.1.refs_4_._.refs_0_), channel_id=1, source_target_pairs={{8,0},{12,4},{0,8},{4,12},{9,1},{13,5},{1,9},{5,13},{10,2},{14,6},... | collective-permute-start | bytes 208904 | tf_op jit(solution)/shard_map/ppermute | solution.py:596
  7.1 1.3 %collective-permute-start = (bf16[272,128]{1,0:T(8,128)(2,1)S(1)}, bf16[272,128]{1,0:T(8,128)(2,1)S(1)}, u32[]{:S(2)}, u32[]{:S(2)}) collective-permute-start(bf16[272,128]{1,0:T(8,128)(2,1)S(1)} %pack.1.refs_4_._.refs_0_), channel_id=1, source_target_pairs={{4,0},{8,4},{12,8},{0,12},{5,1},{9,5},{13,9},{1,13},{6,2},{10,6},{... | collective-permute-start | bytes 208904 | tf_op jit(solution)/shard_map/ppermute | solution.py:596
  8.5 2.0 %prepare.1 = (f32[512,128]{1,0:T(8,128)S(1)}, f32[512,128]{1,0:T(8,128)S(1)}, f32[512,128]{1,0:T(8,128)S(1)}, f32[512,128]{1,0:T(8,128)S(1)}, f32[512,128]{1,0:T(8,128)S(1)}) custom-call(f32[1024,128]{1,0:T(8,128)} %bitcast.11, bf16[512,128]{1,0:T(8,128)(2,1)} %bitcast.12, bf16[272,128]{1,0:T(8,128)(2,1)S(1)} %pack.1.refs_4_._.refs_0_), custom_call_target="tpu_custom_call" | custom-call | flops 3932160 | bytes 1048576 | tf_op jit(solution)/shard_map/prepare/pallas_call | solution.py:603
  10.5 1.5 %banded.1 = (bf16[144,192]{1,0:T(8,128)(2,1)S(1)}, f32[144,640]{1,0:T(8,128)S(1)}, bf16[96,432]{1,0:T(8,128)(2,1)S(1)}, f32[32,256]{1,0:T(8,128)S(1)}) custom-call(bf16[8,27]{1,0:T(8,128)(2,1)} %bitcast.16, f32[8]{0:T(128)} %refs_1_.1, bf16[16,27]{1,0:T(8,128)(2,1)} %bitcast.15, f32[2]{0:T(128)} %refs_3_.1, bf16[272,128]{1,0:T(8,128)(2,1)S(1)} %pack.1.refs_4_._.refs_0_), custom_call_target="tpu_custom_call" | custom-call | flops 20971520 | bytes 4194304 | tf_op jit(solution)/shard_map/banded/pallas_call | solution.py:624
  12.0 0.0 collective-permute-done.2.refs_3_
  12.0 0.0 collective-permute-done.1.refs_2_
  12.0 0.0 collective-permute-done.refs_1_
  12.0 0.1 collective-permute-start.3
  12.1 1.6 %collective-permute-start.4 = (bf16[32,256]{1,0:T(8,128)(2,1)S(1)}, bf16[32,256]{1,0:T(8,128)(2,1)S(1)}, u32[]{:S(2)}, u32[]{:S(2)}) collective-permute-start(bf16[32,256]{1,0:T(8,128)(2,1)S(1)} %get-tuple-element.18), channel_id=1, source_target_pairs={{0,2},{2,0},{1,3},{3,1},{4,6},{6,4},{5,7},{7,5},{8,10},{10,8},{9,1... | collective-permute-start | bytes 49160 | tf_op jit(solution)/shard_map/ppermute | solution.py:672
  13.7 2.2 %collective-permute-done.4.edge_ref.refs_5_ = bf16[32,256]{1,0:T(8,128)(2,1)S(1)} collective-permute-done((bf16[32,256]{1,0:T(8,128)(2,1)S(1)}, bf16[32,256]{1,0:T(8,128)(2,1)S(1)}, u32[]{:S(2)}, u32[]{:S(2)}) %collective-permute-start.4) | collective-permute-done | bytes 16416 | tf_op jit(solution)/shard_map/ppermute | solution.py:672
  15.9 0.0 collective-permute-start.5
  15.9 1.2 %collective-permute-done.5.refs_6_ = bf16[32,128]{1,0:T(8,128)(2,1)S(1)} collective-permute-done((bf16[32,128]{1,0:T(8,128)(2,1)S(1)}, bf16[32,128]{1,0:T(8,128)(2,1)S(1)}, u32[]{:S(2)}, u32[]{:S(2)}) %collective-permute-start.5) | collective-permute-done | bytes 8224 | tf_op jit(solution)/shard_map/ppermute | solution.py:681
  17.1 0.0 collective-permute-done.3.refs_4_
  17.1 9.7 %column.1 = (bf16[2,4,32,256]{3,2,1,0:T(8,128)(2,1)}, f32[1024,128]{1,0:T(8,128)}) custom-call(bf16[272,128]{1,0:T(8,128)(2,1)S(1)} %pack.1.refs_4_._.refs_0_, bf16[272,128]{1,0:T(8,128)(2,1)S(1)} %collective-permute-done.refs_1_, bf16[272,128]{1,0:T(8,128)(2,1)S(1)} %collective-permute-done.1.refs_2_, bf16[272,128]{1,0:T(8,128)(2,1)S(1)} %collective-permute-done.2.refs_3_, ...), custom_call_target="tpu_custom_call" | custom-call | flops 1415577600 | bytes 4194304 | tf_op jit(solution)/shard_map/column/pallas_call | solution.py:684
  (2 shorter events, 0.0 us)
Async XLA Ops:
  1.5 10.5 %collective-permute-start.2 = (bf16[272,128]{1,0:T(8,128)(2,1)S(1)}, bf16[272,128]{1,0:T(8,128)(2,1)S(1)}, u32[]{:S(2)}, u32[]{:S(2)}) collective-permute-start(bf16[272,128]{1,0:T(8,128)(2,1)S(1)} %pack.1.refs_4_._.refs_0_), channel_id=1, source_target_pairs={{12,0},{0,4},{4,8},{8,12},{13,1},{1,5},{5,9},{9,13},{14,2},{2,6},{... | collective-permute-start | bytes 208904 | tf_op jit(solution)/shard_map/ppermute | solution.py:596
  4.5 7.4 %collective-permute-start.1 = (bf16[272,128]{1,0:T(8,128)(2,1)S(1)}, bf16[272,128]{1,0:T(8,128)(2,1)S(1)}, u32[]{:S(2)}, u32[]{:S(2)}) collective-permute-start(bf16[272,128]{1,0:T(8,128)(2,1)S(1)} %pack.1.refs_4_._.refs_0_), channel_id=1, source_target_pairs={{8,0},{12,4},{0,8},{4,12},{9,1},{13,5},{1,9},{5,13},{10,2},{14,6},... | collective-permute-start | bytes 208904 | tf_op jit(solution)/shard_map/ppermute | solution.py:596
  7.1 4.9 %collective-permute-start = (bf16[272,128]{1,0:T(8,128)(2,1)S(1)}, bf16[272,128]{1,0:T(8,128)(2,1)S(1)}, u32[]{:S(2)}, u32[]{:S(2)}) collective-permute-start(bf16[272,128]{1,0:T(8,128)(2,1)S(1)} %pack.1.refs_4_._.refs_0_), channel_id=1, source_target_pairs={{4,0},{8,4},{12,8},{0,12},{5,1},{9,5},{13,9},{1,13},{6,2},{10,6},{... | collective-permute-start | bytes 208904 | tf_op jit(solution)/shard_map/ppermute | solution.py:596
  12.0 5.1 %collective-permute-start.3 = (bf16[512,128]{1,0:T(8,128)(2,1)S(1)}, bf16[512,128]{1,0:T(8,128)(2,1)S(1)}, u32[]{:S(2)}, u32[]{:S(2)}) collective-permute-start(bf16[512,128]{1,0:T(8,128)(2,1)S(1)} %get-tuple-element.17), channel_id=1, source_target_pairs={{0,1},{1,0},{2,3},{3,2},{4,5},{5,4},{6,7},{7,6},{8,9},{9,8},{10,11... | collective-permute-start | bytes 393224 | tf_op jit(solution)/shard_map/ppermute | solution.py:682
  12.1 3.8 %collective-permute-start.4 = (bf16[32,256]{1,0:T(8,128)(2,1)S(1)}, bf16[32,256]{1,0:T(8,128)(2,1)S(1)}, u32[]{:S(2)}, u32[]{:S(2)}) collective-permute-start(bf16[32,256]{1,0:T(8,128)(2,1)S(1)} %get-tuple-element.18), channel_id=1, source_target_pairs={{0,2},{2,0},{1,3},{3,1},{4,6},{6,4},{5,7},{7,5},{8,10},{10,8},{9,1... | collective-permute-start | bytes 49160 | tf_op jit(solution)/shard_map/ppermute | solution.py:672
  15.9 1.2 %collective-permute-start.5 = (bf16[32,128]{1,0:T(8,128)(2,1)S(1)}, bf16[32,128]{1,0:T(8,128)(2,1)S(1)}, u32[]{:S(2)}, u32[]{:S(2)}) collective-permute-start(bf16[32,128]{1,0:T(8,128)(2,1)S(1)} %corner.1), channel_id=1, source_target_pairs={{0,1},{1,0},{2,3},{3,2},{4,5},{5,4},{6,7},{7,6},{8,9},{9,8},{10,11... | collective-permute-start | bytes 24584 | tf_op jit(solution)/shard_map/ppermute | solution.py:681

commit v8 on v6

--- a/solution.py
+++ b/solution.py
@@ -97,22 +97,24 @@
     row, channel = iotas((TALL, CHANNELS))
     spread = one_hot((row & (CHANNELS - 1)) == channel)
     w1 = jnp.dot(spread, w1_ref[...], preferred_element_type=jnp.float32).astype(jnp.bfloat16)
-    tap, column = iotas((27, 3 * PART))
-    dz = step_index(column, PART, 3)
-    place = column - PART * dz
+    tap, column = iotas((27, 4 * PART))
+    dz = column >> 6
+    place = column & (PART - 1)
     dx = jnp.where(place < 3 * HALF, place >> 4, (place - 3 * HALF) >> 2)
     base = 9 * dz + dx
-    row, column = iotas((TALL, 3 * PART))
+    row, column = iotas((TALL, 4 * PART))
     place = column & (PART - 1)
     seam = (place - 3 * HALF) & 3
     seam_row = jnp.where(seam < 2, seam - 2, seam + HALF - 2)
     input_row = jnp.where(place < 3 * HALF, place & (HALF - 1), seam_row)
     distance = jnp.where(place < 3 * HALF + 12, input_row - (row >> 3) + 2, -1)
-    total = jnp.zeros((TALL, 3 * PART), jnp.float32)
-    for dy in range(3):
-        values = jnp.dot(w1, one_hot(tap == base + 3 * dy), preferred_element_type=jnp.float32)
-        total = jnp.where(distance == dy, values, total)
-    t1_ref[...] = total.astype(jnp.bfloat16)
+    for out in range(2):
+        total = jnp.zeros((TALL, 4 * PART), jnp.float32)
+        for dy in range(3):
+            pick = one_hot(tap == base - 9 * out + 3 * dy)
+            values = jnp.dot(w1, pick, preferred_element_type=jnp.float32)
+            total = jnp.where(distance == dy, values, total)
+        t1_ref[out * TALL : (out + 1) * TALL, :] = total.astype(jnp.bfloat16)
     row, column = iotas((TALL, 2 * window))
     bias = jnp.zeros((TALL, 2 * window), jnp.float32)
     for k in range(CHANNELS):
@@ -121,40 +123,48 @@
         (row >= TALL - CHANNELS) & (column >= window) & (g == count_gy - 1)
     )
     bias_ref[...] = jnp.where(outside, OUTSIDE, bias)
-    channel, column = iotas((CHANNELS, 3 * TALL))
+    channel, column = iotas((CHANNELS, 4 * TALL))
     spread = one_hot((column & (CHANNELS - 1)) == channel)
-    tap, column = iotas((27, 3 * TALL))
-    same_z = tap_parts(tap)[0] == step_index(column, TALL, 3)
+    tap, column = iotas((27, 4 * TALL))
+    tap_z, slice_z = tap_parts(tap)[0], step_index(column, TALL, 4)
     row, tap = iotas((6 * HALF, 27))
     _, tap_y, tap_x = tap_parts(tap)
     same_x = (row >> 5) == tap_x
-    wide = []
-    for o in range(2):
-        values = lax.dot_general(
+    wide = [
+        lax.dot_general(
             w2_ref[o * CHANNELS : (o + 1) * CHANNELS, :],
             spread,
             (((0,), (0,)), ((), ())),
             preferred_element_type=jnp.float32,
         )
-        wide.append(jnp.where(same_z, values, 0.0).astype(jnp.bfloat16))
-    out_row, column = iotas((6 * HALF, 3 * TALL))
+        for o in range(2)
+    ]
+    picks = [
+        [one_hot(same_x & (tap_y == dy) & (((row >> 2) & 1) == o)) for o in range(2)]
+        for dy in range(3)
+    ]
+    out_row, column = iotas((6 * HALF, 4 * TALL))
     y = ((out_row >> 3) & 3) * BY + (out_row & 3)
-    hidden_row = (column - TALL * step_index(column, TALL, 3)) >> 3
-    total = jnp.zeros((6 * HALF, 3 * TALL), jnp.float32)
-    for dy in range(3):
-        values = 0.0
-        for o in range(2):
-            pick = one_hot(same_x & (tap_y == dy) & (((row >> 2) & 1) == o))
-            values = values + jnp.dot(pick, wide[o], preferred_element_type=jnp.float32)
-        total = jnp.where(hidden_row - y == dy, values, total)
-    t2_ref[...] = total.astype(jnp.bfloat16)
+    distance = ((column - TALL * step_index(column, TALL, 4)) >> 3) - y
+    for out in range(2):
+        same_z = tap_z == slice_z - out
+        terms = [jnp.where(same_z, values, 0.0).astype(jnp.bfloat16) for values in wide]
+        total = jnp.zeros((6 * HALF, 4 * TALL), jnp.float32)
+        for dy in range(3):
+            values = 0.0
+            for o in range(2):
+                values = values + jnp.dot(
+                    picks[dy][o], terms[o], preferred_element_type=jnp.float32
+                )
+            total = jnp.where(distance == dy, values, total)
+        t2_ref[out * 6 * HALF : (out + 1) * 6 * HALF, :] = total.astype(jnp.bfloat16)
     row, _ = iotas((2 * HALF, 2 * window))
     bias2_ref[...] = jnp.where(((row >> 2) & 1) == 0, b2_ref[0], b2_ref[1])
 
 
 def edges_kernel(dims, *refs):
     count_gy, depth, rows, columns, few, count = dims
-    tiles, outs = refs[:few], refs[few + 2 :]
+    tiles, outs = refs[:few], refs[few + 1 :]
     g = lax.axis_index("gy")
     c = lax.axis_index("col")
     height = depth * rows
@@ -195,7 +205,7 @@
         pl.loop(0, count // 2)(pair)
 
 
-def corner_kernel(edge_ref, corner_ref):
+def corner_kernel(edge_ref, _, corner_ref):
     c = lax.axis_index("col")
     corner_ref[...] = jnp.where(c == 0, edge_ref[:, BX:], edge_ref[:, 0:BX])
 
@@ -340,11 +350,9 @@
 
     def moved(values):
         lane = lax.broadcasted_iota(jnp.int32, values.shape, 1)
-        return (
-            jnp.where(lane == 0, 0.0, pltpu.roll(values, 1, 1)),
-            values,
-            jnp.where(lane == window - 1, 0.0, pltpu.roll(values, window - 1, 1)),
-        )
+        left = jnp.where(lane == 0, 0.0, pltpu.roll(values, 1, 1))
+        right = jnp.where(lane == window - 1, 0.0, pltpu.roll(values, window - 1, 1))
+        return left.astype(values.dtype), values, right.astype(values.dtype)
 
     def edge_pair(k, at):
         if isinstance(at, int):
@@ -382,25 +390,31 @@
     def first(z, valid):
         total = jnp.dot(
             t1_ref[...],
-            shifted[pl.ds(z + 1, 3)].reshape(3 * PART, 2 * window),
+            shifted[pl.ds(z + 1, 4)].reshape(4 * PART, 2 * window),
             preferred_element_type=jnp.float32,
         )
-        values = jnp.maximum(total + bias_ref[...], 0.0)
-        if valid is not None:
-            values = values * valid
-        hidden[z + 1] = values.astype(jnp.bfloat16)
+        for out in range(2):
+            values = jnp.maximum(total[out * TALL : (out + 1) * TALL] + bias_ref[...], 0.0)
+            if valid is not None:
+                values = values * valid(z + out)
+            hidden[z + 1 + out] = values.astype(jnp.bfloat16)
 
     height = 2 * HALF
     lane = lax.broadcasted_iota(jnp.int32, (height, 2 * window), 1)
     left_edge = (lane == 0) | (lane == window)
     right_edge = (lane == window - 1) | (lane == 2 * window - 1)
 
-    def second(z, t, zz):
+    def second(z, tile):
         total = jnp.dot(
             t2_ref[...],
-            hidden[pl.ds(z, 3)].reshape(3 * TALL, 2 * window),
+            hidden[pl.ds(z, 4)].reshape(4 * TALL, 2 * window),
             preferred_element_type=jnp.float32,
         )
+        for out in range(2):
+            at = z + out
+            place(total[3 * height * out : 3 * height * (out + 1)], tile + at // depth, at % depth)
+
+    def place(total, t, zz):
         before = pltpu.roll(total[0:height], 1, 1)
         after = pltpu.roll(total[2 * height :], 2 * window - 1, 1)
         total = total[height : 2 * height] + bias2_ref[...]
@@ -432,11 +446,14 @@
             for zz in range(depth):
                 shifts(i, zz, tile * depth + zz + 2, None)
 
-        first(0, None)
-        for z in range(depths):
-            if z + 1 < depths:
-                first(z + 1, None)
-            second(z, z // depth, z % depth)
+        @pl.loop(0, depths // 2, unroll=2)
+        def _(k):
+            first(2 * k, None)
+
+        @pl.loop(0, depths // 2, unroll=2)
+        def _(k):
+            second(2 * k, 0)
+
     else:
 
         @pl.loop(0, count_gz // segment)
@@ -447,13 +464,13 @@
                 inside = jnp.clip(at, 0, count_gz * depth - 1)
                 shifts(inside // depth, inside % depth, z + 2, valid_slice(at))
 
-            @pl.loop(-1, depths + 1)
-            def _(z):
-                first(z, valid_slice(q * depths + z))
-
-            @pl.loop(0, depths)
-            def _(z):
-                second(z, q * segment + z // depth, z % depth)
+            @pl.loop(0, depths // 2 + 1)
+            def _(k):
+                first(2 * k - 1, lambda z: valid_slice(q * depths + z))
+
+            @pl.loop(0, depths // 2)
+            def _(k):
+                second(2 * k, q * segment)
 
     for zz in range(depth):
         for xb in range(brick_columns):
@@ -579,33 +596,12 @@
         tiles = [lax.all_gather(payload, "gz", axis=0, tiled=False)]
 
     cells = depth * BY
-    prepared = pl.pallas_call(
-        functools.partial(prepare_kernel, (depth, slots)),
-        out_shape=[shape((slots * cells, BX), f32)] * 5,
-        in_specs=[HBM, HBM, ANY],
-        out_specs=[VMEM] * 5,
-        scratch_shapes=[
-            pltpu.VMEM((slots * 2 * cells, BX), f32),
-            pltpu.VMEM((slots * cells, BX), bf16),
-            pltpu.VMEM((slots * cells, BX), f32),
-            pltpu.SemaphoreType.DMA((slots // 8, 2)),
-        ],
-        compiler_params=pltpu.CompilerParams(vmem_limit_bytes=12 * 2**20),
-        cost_estimate=pl.CostEstimate(
-            flops=60 * slots * cells * BX, bytes_accessed=2**20, transcendentals=0
-        ),
-        name="prepare",
-    )(
-        in_hbm(solutes.reshape(slots * 2 * cells, BX)),
-        in_hbm(biomass.reshape(slots * cells, BX)),
-        payload,
-    )
     t1, bias, t2, bias2 = pl.pallas_call(
         functools.partial(banded_kernel, (window, count_gy)),
         out_shape=(
-            shape((TALL, 3 * PART), bf16),
+            shape((2 * TALL, 4 * PART), bf16),
             shape((TALL, 2 * window), f32),
-            shape((6 * HALF, 3 * TALL), bf16),
+            shape((12 * HALF, 4 * TALL), bf16),
             shape((2 * HALF, 2 * window), f32),
         ),
         in_specs=[HBM, HBM, HBM, HBM, ANY],
@@ -641,22 +637,43 @@
         functools.partial(edges_kernel, (count_gy, depth, rows, columns, few, count_gz)),
         out_shape=[shape((depths * rows, BX), bf16)]
         + [shape((2 * depths, columns), bf16)] * directions,
-        in_specs=[VMEM] * few + [ANY, ANY],
+        in_specs=[VMEM] * few + [ANY],
         out_specs=[VMEM] * (1 + directions),
         compiler_params=pltpu.CompilerParams(vmem_limit_bytes=16 * 2**20),
         name="edges",
-    )(*tiles, bias2, prepared[-1])
+    )(*tiles, bias2)
+    prepared = pl.pallas_call(
+        functools.partial(prepare_kernel, (depth, slots)),
+        out_shape=[shape((slots * cells, BX), f32)] * 5,
+        in_specs=[HBM, HBM, ANY],
+        out_specs=[VMEM] * 5,
+        scratch_shapes=[
+            pltpu.VMEM((slots * 2 * cells, BX), f32),
+            pltpu.VMEM((slots * cells, BX), bf16),
+            pltpu.VMEM((slots * cells, BX), f32),
+            pltpu.SemaphoreType.DMA((slots // 8, 2)),
+        ],
+        compiler_params=pltpu.CompilerParams(vmem_limit_bytes=12 * 2**20),
+        cost_estimate=pl.CostEstimate(
+            flops=60 * slots * cells * BX, bytes_accessed=2**20, transcendentals=0
+        ),
+        name="prepare",
+    )(
+        in_hbm(solutes.reshape(slots * 2 * cells, BX)),
+        in_hbm(biomass.reshape(slots * cells, BX)),
+        near,
+    )
     edges = []
     for pairs, edge in zip(ways, sent):
         edge = lax.ppermute(edge, "gy", pairs)
         corner = pl.pallas_call(
             corner_kernel,
             out_shape=shape((2 * depths, BX), bf16),
-            in_specs=[VMEM],
+            in_specs=[VMEM, ANY],
             out_specs=VMEM,
             compiler_params=pltpu.CompilerParams(vmem_limit_bytes=4 * 2**20),
             name="corner",
-        )(edge)
+        )(edge, prepared[-1])
         edges += [edge, lax.ppermute(corner, "col", swap)]
     near = lax.ppermute(near, "col", swap)
 
@@ -688,7 +705,7 @@
         ],
         compiler_params=pltpu.CompilerParams(vmem_limit_bytes=40 * 2**20),
         cost_estimate=pl.CostEstimate(
-            flops=2 * depths * 2 * window * TALL * (3 * PART + 3 * 6 * HALF),
+            flops=2 * depths * 2 * window * TALL * (4 * PART + 4 * 6 * HALF),
             bytes_accessed=4 * 2**20,
             transcendentals=0,
         ),

time: 26.1 us -> 25.8 us (0.989)
  waiting for transfers between devices: 3.41 us -> 3.07 us
    ppermute x1, waiting for transfers between devices: 2.2 us -> 0.2 us  [per_device(): edge = lax.ppermute(edge, 'gy', pairs)]
    ppermute x3, waiting for transfers between devices: 0.03 us -> 1.75 us  [per_device(): lax.ppermute(payload, 'gz', [((i + s) % count_gz, i) for i in range(count...]
    pallas_call x1, Pallas kernels: 1.47 us -> 1.77 us  [per_device(): pl.pallas_call(functools.partial(banded_kernel, (window, count_gy)), out_...]
  transfers between devices with their start and end apart: 6 -> 6, of which waited for: 2 -> 4; matrix products, arithmetic and copies ran while one was open for 0% -> 0% of each run, Pallas kernels for 13% -> 15%
where the time goes in v8:
time: 25.8 us; the launch traced here: 25.6 us
  Pallas kernels  13.1 us (51%)
  starting transfers between devices  8.74 us (34%)
  waiting for transfers between devices  3.07 us (12%)
  between operations  0.68 us (3%)
    pallas_call x1, Pallas kernels, per_device(): pl.pallas_call(functools.partial(column_kernel, (count_gz, count_gy, dept...  8.48 us
    ppermute x3, starting transfers between devices, per_device(): lax.ppermute(payload, 'gz', [((i + s) % count_gz, i) for i in range(count...  7.01 us
    pallas_call x1, Pallas kernels, per_device(): pl.pallas_call(functools.partial(prepare_kernel, (depth, slots)), out_sha...  2 us
    pallas_call x1, Pallas kernels, per_device(): pl.pallas_call(functools.partial(banded_kernel, (window, count_gy)), out_...  1.77 us
    ppermute x3, waiting for transfers between devices, per_device(): lax.ppermute(payload, 'gz', [((i + s) % count_gz, i) for i in range(count...  1.75 us
    ppermute x1, starting transfers between devices, per_device(): edge = lax.ppermute(edge, 'gy', pairs)  1.6 us
    ppermute x1, waiting for transfers between devices, per_device(): edges += [edge, lax.ppermute(corner, 'col', swap)]  1.12 us
    pallas_call x1, Pallas kernels, per_device(): pl.pallas_call(pack_kernel, out_shape=shape((columns // BX * height + TIL...  0.82 us
  transfers between devices with their start and end apart: 6, of which 4 were waited for; matrix products, arithmetic and copies ran while one was open for 0% of the time, Pallas kernels for 15%

profile of v8, /device:TPU:0, one launch (start us, length us, event | category | flops | bytes accessed | tf_op | source)
XLA Modules:
  0.0 25.6 jit_solution(11786215643668580079)
XLA Ops:
  0.6 0.8 %pack.1.refs_4_.refs_0_ = bf16[272,128]{1,0:T(8,128)(2,1)S(1)} custom-call(bf16[128,256]{1,0:T(8,128)(2,1)} %bitcast.13, s32[1,16]{1,0:T(1,128)} %bitcast.14), custom_call_target="tpu_custom_call" | custom-call | tf_op jit(solution)/shard_map/pack/pallas_call | solution.py:576
  1.5 3.1 %collective-permute-start.2 = (bf16[272,128]{1,0:T(8,128)(2,1)S(1)}, bf16[272,128]{1,0:T(8,128)(2,1)S(1)}, u32[]{:S(2)}, u32[]{:S(2)}) collective-permute-start(bf16[272,128]{1,0:T(8,128)(2,1)S(1)} %pack.1.refs_4_.refs_0_), channel_id=1, source_target_pairs={{12,0},{0,4},{4,8},{8,12},{13,1},{1,5},{5,9},{9,13},{14,2},{2,6},{... | collective-permute-start | bytes 208904 | tf_op jit(solution)/shard_map/ppermute | solution.py:592
  4.5 2.6 %collective-permute-start.1 = (bf16[272,128]{1,0:T(8,128)(2,1)S(1)}, bf16[272,128]{1,0:T(8,128)(2,1)S(1)}, u32[]{:S(2)}, u32[]{:S(2)}) collective-permute-start(bf16[272,128]{1,0:T(8,128)(2,1)S(1)} %pack.1.refs_4_.refs_0_), channel_id=1, source_target_pairs={{8,0},{12,4},{0,8},{4,12},{9,1},{13,5},{1,9},{5,13},{10,2},{14,6},... | collective-permute-start | bytes 208904 | tf_op jit(solution)/shard_map/ppermute | solution.py:592
  7.1 1.3 %collective-permute-start = (bf16[272,128]{1,0:T(8,128)(2,1)S(1)}, bf16[272,128]{1,0:T(8,128)(2,1)S(1)}, u32[]{:S(2)}, u32[]{:S(2)}) collective-permute-start(bf16[272,128]{1,0:T(8,128)(2,1)S(1)} %pack.1.refs_4_.refs_0_), channel_id=1, source_target_pairs={{4,0},{8,4},{12,8},{0,12},{5,1},{9,5},{13,9},{1,13},{6,2},{10,6},{... | collective-permute-start | bytes 208904 | tf_op jit(solution)/shard_map/ppermute | solution.py:592
  8.5 1.8 %banded.1 = (bf16[288,256]{1,0:T(8,128)(2,1)S(1)}, f32[144,768]{1,0:T(8,128)S(1)}, bf16[192,576]{1,0:T(8,128)(2,1)S(1)}, f32[32,768]{1,0:T(8,128)S(1)}) custom-call(bf16[8,27]{1,0:T(8,128)(2,1)} %bitcast.16, f32[8]{0:T(128)} %refs_1_.1, bf16[16,27]{1,0:T(8,128)(2,1)} %bitcast.15, f32[2]{0:T(128)} %refs_3_.1, bf16[272,128]{1,0:T(8,128)(2,1)S(1)} %pack.1.refs_4_.refs_0_), custom_call_target="tpu_custom_call" | custom-call | flops 20971520 | bytes 4194304 | tf_op jit(solution)/shard_map/banded/pallas_call | solution.py:599
  10.2 0.0 collective-permute-done.2.refs_3_
  10.3 1.6 %collective-permute-done.1.refs_2_ = bf16[272,128]{1,0:T(8,128)(2,1)S(1)} collective-permute-done((bf16[272,128]{1,0:T(8,128)(2,1)S(1)}, bf16[272,128]{1,0:T(8,128)(2,1)S(1)}, u32[]{:S(2)}, u32[]{:S(2)}) %collective-permute-start.1) | collective-permute-done | bytes 69664 | tf_op jit(solution)/shard_map/ppermute | solution.py:592
  11.8 0.2 collective-permute-done.refs_1_
  12.0 0.1 collective-permute-start.3
  12.1 1.6 %collective-permute-start.4 = (bf16[32,256]{1,0:T(8,128)(2,1)S(1)}, bf16[32,256]{1,0:T(8,128)(2,1)S(1)}, u32[]{:S(2)}, u32[]{:S(2)}) collective-permute-start(bf16[32,256]{1,0:T(8,128)(2,1)S(1)} %get-tuple-element.17), channel_id=1, source_target_pairs={{0,2},{2,0},{1,3},{3,1},{4,6},{6,4},{5,7},{7,5},{8,10},{10,8},{9,1... | collective-permute-start | bytes 49160 | tf_op jit(solution)/shard_map/ppermute | solution.py:668
  13.7 2.0 %prepare.1 = (f32[512,128]{1,0:T(8,128)S(1)}, f32[512,128]{1,0:T(8,128)S(1)}, f32[512,128]{1,0:T(8,128)S(1)}, f32[512,128]{1,0:T(8,128)S(1)}, f32[512,128]{1,0:T(8,128)S(1)}) custom-call(f32[1024,128]{1,0:T(8,128)} %bitcast.11, bf16[512,128]{1,0:T(8,128)(2,1)} %bitcast.12, bf16[512,128]{1,0:T(8,128)(2,1)S(1)} %get-tuple-element.16._), custom_call_target="tpu_custom_call" | custom-call | flops 3932160 | bytes 1048576 | tf_op jit(solution)/shard_map/prepare/pallas_call | solution.py:645
  15.7 0.2 collective-permute-done.4.edge_ref.refs_5_
  15.9 0.1 collective-permute-start.5
  16.0 1.1 %collective-permute-done.5.refs_6_ = bf16[32,128]{1,0:T(8,128)(2,1)S(1)} collective-permute-done((bf16[32,128]{1,0:T(8,128)(2,1)S(1)}, bf16[32,128]{1,0:T(8,128)(2,1)S(1)}, u32[]{:S(2)}, u32[]{:S(2)}) %collective-permute-start.5) | collective-permute-done | bytes 8224 | tf_op jit(solution)/shard_map/ppermute | solution.py:677
  17.1 0.0 collective-permute-done.3.refs_4_
  17.1 8.5 %column.1 = (bf16[2,4,32,256]{3,2,1,0:T(8,128)(2,1)}, f32[1024,128]{1,0:T(8,128)}) custom-call(bf16[272,128]{1,0:T(8,128)(2,1)S(1)} %pack.1.refs_4_.refs_0_, bf16[272,128]{1,0:T(8,128)(2,1)S(1)} %collective-permute-done.refs_1_, bf16[272,128]{1,0:T(8,128)(2,1)S(1)} %collective-permute-done.1.refs_2_, bf16[272,128]{1,0:T(8,128)(2,1)S(1)} %collective-permute-done.2.refs_3_, ...), custom_call_target="tpu_custom_call" | custom-call | flops 2264924160 | bytes 4194304 | tf_op jit(solution)/shard_map/column/pallas_call | solution.py:680
  (2 shorter events, 0.0 us)
Async XLA Ops:
  1.5 8.8 %collective-permute-start.2 = (bf16[272,128]{1,0:T(8,128)(2,1)S(1)}, bf16[272,128]{1,0:T(8,128)(2,1)S(1)}, u32[]{:S(2)}, u32[]{:S(2)}) collective-permute-start(bf16[272,128]{1,0:T(8,128)(2,1)S(1)} %pack.1.refs_4_.refs_0_), channel_id=1, source_target_pairs={{12,0},{0,4},{4,8},{8,12},{13,1},{1,5},{5,9},{9,13},{14,2},{2,6},{... | collective-permute-start | bytes 208904 | tf_op jit(solution)/shard_map/ppermute | solution.py:592
  4.5 7.3 %collective-permute-start.1 = (bf16[272,128]{1,0:T(8,128)(2,1)S(1)}, bf16[272,128]{1,0:T(8,128)(2,1)S(1)}, u32[]{:S(2)}, u32[]{:S(2)}) collective-permute-start(bf16[272,128]{1,0:T(8,128)(2,1)S(1)} %pack.1.refs_4_.refs_0_), channel_id=1, source_target_pairs={{8,0},{12,4},{0,8},{4,12},{9,1},{13,5},{1,9},{5,13},{10,2},{14,6},... | collective-permute-start | bytes 208904 | tf_op jit(solution)/shard_map/ppermute | solution.py:592
  7.1 4.9 %collective-permute-start = (bf16[272,128]{1,0:T(8,128)(2,1)S(1)}, bf16[272,128]{1,0:T(8,128)(2,1)S(1)}, u32[]{:S(2)}, u32[]{:S(2)}) collective-permute-start(bf16[272,128]{1,0:T(8,128)(2,1)S(1)} %pack.1.refs_4_.refs_0_), channel_id=1, source_target_pairs={{4,0},{8,4},{12,8},{0,12},{5,1},{9,5},{13,9},{1,13},{6,2},{10,6},{... | collective-permute-start | bytes 208904 | tf_op jit(solution)/shard_map/ppermute | solution.py:592
  12.0 5.1 %collective-permute-start.3 = (bf16[512,128]{1,0:T(8,128)(2,1)S(1)}, bf16[512,128]{1,0:T(8,128)(2,1)S(1)}, u32[]{:S(2)}, u32[]{:S(2)}) collective-permute-start(bf16[512,128]{1,0:T(8,128)(2,1)S(1)} %get-tuple-element.16._), channel_id=1, source_target_pairs={{0,1},{1,0},{2,3},{3,2},{4,5},{5,4},{6,7},{7,6},{8,9},{9,8},{10,11... | collective-permute-start | bytes 393224 | tf_op jit(solution)/shard_map/ppermute | solution.py:678
  12.1 3.8 %collective-permute-start.4 = (bf16[32,256]{1,0:T(8,128)(2,1)S(1)}, bf16[32,256]{1,0:T(8,128)(2,1)S(1)}, u32[]{:S(2)}, u32[]{:S(2)}) collective-permute-start(bf16[32,256]{1,0:T(8,128)(2,1)S(1)} %get-tuple-element.17), channel_id=1, source_target_pairs={{0,2},{2,0},{1,3},{3,1},{4,6},{6,4},{5,7},{7,5},{8,10},{10,8},{9,1... | collective-permute-start | bytes 49160 | tf_op jit(solution)/shard_map/ppermute | solution.py:668
  15.9 1.2 %collective-permute-start.5 = (bf16[32,128]{1,0:T(8,128)(2,1)S(1)}, bf16[32,128]{1,0:T(8,128)(2,1)S(1)}, u32[]{:S(2)}, u32[]{:S(2)}) collective-permute-start(bf16[32,128]{1,0:T(8,128)(2,1)S(1)} %corner.1), channel_id=1, source_target_pairs={{0,1},{1,0},{2,3},{3,2},{4,5},{5,4},{6,7},{7,6},{8,9},{9,8},{10,11... | collective-permute-start | bytes 24584 | tf_op jit(solution)/shard_map/ppermute | solution.py:677

commit v9 on v8

--- a/solution.py
+++ b/solution.py
@@ -16,7 +16,8 @@
 REACH = HALF + 2
 PART = 3 * HALF + TILE
 TALL = REACH * CHANNELS
-OUTSIDE = -3e38
+ONE_ROW = 3 * HALF + 12
+OUTSIDE = -1e30
 
 VMEM = pl.BlockSpec(memory_space=pltpu.VMEM)
 SMEM = pl.BlockSpec(memory_space=pltpu.SMEM)
@@ -80,10 +81,9 @@
         copy.wait()
 
 
-def banded_kernel(dims, *refs):
-    window, count_gy = dims
+def banded_kernel(*refs):
     sources, refs = refs[:4], refs[5:]
-    t1_ref, bias_ref, t2_ref, bias2_ref, *local, sems = refs
+    t1_ref, t2_ref, bias2_ref, *local, sems = refs
     copies = [
         pltpu.make_async_copy(source, target, sems.at[k])
         for k, (source, target) in enumerate(zip(sources, local))
@@ -93,7 +93,6 @@
     for copy in copies:
         copy.wait()
     w1_ref, b1_ref, w2_ref, b2_ref = local
-    g = lax.axis_index("gy")
     row, channel = iotas((TALL, CHANNELS))
     spread = one_hot((row & (CHANNELS - 1)) == channel)
     w1 = jnp.dot(spread, w1_ref[...], preferred_element_type=jnp.float32).astype(jnp.bfloat16)
@@ -108,21 +107,25 @@
     seam_row = jnp.where(seam < 2, seam - 2, seam + HALF - 2)
     input_row = jnp.where(place < 3 * HALF, place & (HALF - 1), seam_row)
     distance = jnp.where(place < 3 * HALF + 12, input_row - (row >> 3) + 2, -1)
+    bias = jnp.zeros((TALL, 4 * PART), jnp.float32)
+    for k in range(CHANNELS):
+        bias = jnp.where((row & (CHANNELS - 1)) == k, b1_ref[k], bias)
+    high = bias.astype(jnp.bfloat16).astype(jnp.float32)
+    middle = (bias - high).astype(jnp.bfloat16).astype(jnp.float32)
+    constant = jnp.where(column == PART + ONE_ROW, high, 0.0)
+    constant = jnp.where(column == 2 * PART + ONE_ROW, middle, constant)
+    constant = jnp.where(column == 2 * PART - 1, bias - high - middle, constant)
+    outside = ((column == PART + ONE_ROW + 1) & (row < CHANNELS)) | (
+        (column == PART + ONE_ROW + 2) & (row >= TALL - CHANNELS)
+    )
+    constant = jnp.where(outside, OUTSIDE, constant)
     for out in range(2):
-        total = jnp.zeros((TALL, 4 * PART), jnp.float32)
+        total = constant
         for dy in range(3):
             pick = one_hot(tap == base - 9 * out + 3 * dy)
             values = jnp.dot(w1, pick, preferred_element_type=jnp.float32)
             total = jnp.where(distance == dy, values, total)
         t1_ref[out * TALL : (out + 1) * TALL, :] = total.astype(jnp.bfloat16)
-    row, column = iotas((TALL, 2 * window))
-    bias = jnp.zeros((TALL, 2 * window), jnp.float32)
-    for k in range(CHANNELS):
-        bias = jnp.where((row & (CHANNELS - 1)) == k, b1_ref[k], bias)
-    outside = ((row < CHANNELS) & (column < window) & (g == 0)) | (
-        (row >= TALL - CHANNELS) & (column >= window) & (g == count_gy - 1)
-    )
-    bias_ref[...] = jnp.where(outside, OUTSIDE, bias)
     channel, column = iotas((CHANNELS, 4 * TALL))
     spread = one_hot((column & (CHANNELS - 1)) == channel)
     tap, column = iotas((27, 4 * TALL))
@@ -157,9 +160,9 @@
                     picks[dy][o], terms[o], preferred_element_type=jnp.float32
                 )
             total = jnp.where(distance == dy, values, total)
-        t2_ref[out * 6 * HALF : (out + 1) * 6 * HALF, :] = total.astype(jnp.bfloat16)
-    row, _ = iotas((2 * HALF, 2 * window))
-    bias2_ref[...] = jnp.where(((row >> 2) & 1) == 0, b2_ref[0], b2_ref[1])
+        t2_ref[out * 6 * HALF : (out + 1) * 6 * HALF, :] = (0.5 * total).astype(jnp.bfloat16)
+    row, _ = iotas((2 * HALF, BX))
+    bias2_ref[...] = 0.5 * jnp.where(((row >> 2) & 1) == 0, b2_ref[0], b2_ref[1])
 
 
 def edges_kernel(dims, *refs):
@@ -284,7 +287,7 @@
         bottom_refs = top_refs
     else:
         bottom_refs, refs = refs[:2], refs[2:]
-    t1_ref, bias_ref, t2_ref, bias2_ref, *refs = refs
+    t1_ref, t2_ref, bias2_ref, *refs = refs
     carbon_ref, oxygen_ref, carbon_around_ref, oxygen_around_ref, quarter_ref, *refs = refs
     fractions_ref, next_ref, *refs = refs
     (
@@ -360,6 +363,12 @@
         group = edge_rows[k, pl.ds(pl.multiple_of(at // 8 * 8, 8), 8), :]
         return pltpu.roll(group, lax.rem(8 - at % 8, 8), 0)[0:2]
 
+    row, _ = iotas((4, window))
+    constants = [
+        jnp.where((row == 0) | (row == 3), 1.0, jnp.where((row == 1 + h) & beyond, 1.0, 0.0))
+        for h, beyond in enumerate((g == 0, g == count_gy - 1))
+    ]
+
     def shifts(i, zz, slot, valid):
         z = i * depth + zz
         halves = []
@@ -383,7 +392,7 @@
             for dx, values in enumerate(moved(halves[h])):
                 shifted[slot, dx * HALF : (dx + 1) * HALF, lanes] = values.astype(jnp.bfloat16)
             values = jnp.concatenate(
-                [*moved(seams[h]), jnp.zeros((4, window), jnp.float32)], axis=0
+                [*moved(seams[h]), constants[h]], axis=0
             )
             shifted[slot, 3 * HALF : PART, lanes] = values.astype(jnp.bfloat16)
 
@@ -394,15 +403,13 @@
             preferred_element_type=jnp.float32,
         )
         for out in range(2):
-            values = jnp.maximum(total[out * TALL : (out + 1) * TALL] + bias_ref[...], 0.0)
+            values = jnp.maximum(total[out * TALL : (out + 1) * TALL], 0.0)
             if valid is not None:
                 values = values * valid(z + out)
             hidden[z + 1 + out] = values.astype(jnp.bfloat16)
 
     height = 2 * HALF
-    lane = lax.broadcasted_iota(jnp.int32, (height, 2 * window), 1)
-    left_edge = (lane == 0) | (lane == window)
-    right_edge = (lane == window - 1) | (lane == 2 * window - 1)
+    _, lane = iotas((height, BX))
 
     def second(z, tile):
         total = jnp.dot(
@@ -415,22 +422,25 @@
             place(total[3 * height * out : 3 * height * (out + 1)], tile + at // depth, at % depth)
 
     def place(total, t, zz):
-        before = pltpu.roll(total[0:height], 1, 1)
-        after = pltpu.roll(total[2 * height :], 2 * window - 1, 1)
-        total = total[height : 2 * height] + bias2_ref[...]
-        total = total + jnp.where(left_edge, 0.0, before)
-        total = total + jnp.where(right_edge, 0.0, after)
+        blocks = window // BX
         for h in range(2):
-            at = h * window
-            own = jnp.where(
-                c == 0, total[:, at : at + columns], total[:, at + BX : at + window]
-            )
-            values = 0.5 + 0.5 * jnp.tanh(0.5 * own)
-            values = values.astype(jnp.bfloat16).astype(jnp.float32)
-            for yb in range(brick_rows):
-                for xb in range(brick_columns):
+            part = [total[:, k * BX : (k + 1) * BX] for k in range(h * blocks, (h + 1) * blocks)]
+            left = [0.0] + [pltpu.roll(block[0:height], 1, 1) for block in part]
+            right = [pltpu.roll(block[2 * height :], BX - 1, 1) for block in part] + [0.0]
+            sums = [
+                part[k][height : 2 * height]
+                + (
+                    jnp.where(lane == 0, left[k], left[k + 1])
+                    + jnp.where(lane == BX - 1, right[k + 1], right[k])
+                )
+                for k in range(blocks)
+            ]
+            for xb in range(brick_columns):
+                own = jnp.where(c == 0, sums[xb], sums[xb + 1]) + bias2_ref[...]
+                values = 0.5 + 0.5 * jnp.tanh(own)
+                for yb in range(brick_rows):
                     b = (h * brick_rows + yb) * brick_columns + xb
-                    bricks[t, b, zz] = values[yb * 8 : yb * 8 + 8, xb * BX : (xb + 1) * BX]
+                    bricks[t, b, zz] = values[yb * 8 : yb * 8 + 8]
 
     def valid_slice(z):
         return ((z >= 0) & (z < count_gz * depth)).astype(jnp.float32)
@@ -500,7 +510,7 @@
     def _(j):
         brick = brick_of_slot[j]
         values = bricks[j // capacity, jnp.maximum(brick, 0)]
-        values = jnp.where(brick >= 0, values, 0.0)
+        values = jnp.where(brick >= 0, values, 0.0).astype(jnp.bfloat16).astype(jnp.float32)
         at = pl.multiple_of(j * (2 * size), 8)
         arrived[pl.ds(at, 2 * size), :] = values.reshape(2 * size, BX)
 
@@ -596,16 +606,15 @@
         tiles = [lax.all_gather(payload, "gz", axis=0, tiled=False)]
 
     cells = depth * BY
-    t1, bias, t2, bias2 = pl.pallas_call(
-        functools.partial(banded_kernel, (window, count_gy)),
+    t1, t2, bias2 = pl.pallas_call(
+        banded_kernel,
         out_shape=(
             shape((2 * TALL, 4 * PART), bf16),
-            shape((TALL, 2 * window), f32),
             shape((12 * HALF, 4 * TALL), bf16),
-            shape((2 * HALF, 2 * window), f32),
+            shape((2 * HALF, BX), f32),
         ),
         in_specs=[HBM, HBM, HBM, HBM, ANY],
-        out_specs=(VMEM, VMEM, VMEM, VMEM),
+        out_specs=(VMEM, VMEM, VMEM),
         scratch_shapes=[
             pltpu.VMEM((CHANNELS, 27), bf16),
             pltpu.SMEM((CHANNELS,), f32),
@@ -687,7 +696,7 @@
             shape((2, depth, rows, columns), bf16),
             shape((slots * 2 * cells, BX), f32),
         ),
-        in_specs=[VMEM] * (few + 1 + len(edges) + 9),
+        in_specs=[VMEM] * (few + 1 + len(edges) + 8),
         out_specs=(HBM, HBM),
         scratch_shapes=[
             pltpu.VMEM((2, 2 * depths, window), f32),
@@ -715,7 +724,6 @@
         near,
         *edges,
         t1,
-        bias,
         t2,
         bias2,
         *prepared,

time: 25.8 us -> 25.8 us (level)
  no operation moved by 1% of the time
where the time goes in v9:
time: 25.8 us; the launch traced here: 25.6 us
  Pallas kernels  13.1 us (51%)
  starting transfers between devices  8.74 us (34%)
  waiting for transfers between devices  3.05 us (12%)
  between operations  0.68 us (3%)
    pallas_call x1, Pallas kernels, per_device(): pl.pallas_call(functools.partial(column_kernel, (count_gz, count_gy, dept...  8.49 us
    ppermute x3, starting transfers between devices, per_device(): lax.ppermute(payload, 'gz', [((i + s) % count_gz, i) for i in range(count...  7.01 us
    pallas_call x1, Pallas kernels, per_device(): pl.pallas_call(functools.partial(prepare_kernel, (depth, slots)), out_sha...  2 us
    pallas_call x1, Pallas kernels, per_device(): pl.pallas_call(banded_kernel, out_shape=(shape((2 * TALL, 4 * PART), bf16...  1.78 us
    ppermute x3, waiting for transfers between devices, per_device(): lax.ppermute(payload, 'gz', [((i + s) % count_gz, i) for i in range(count...  1.74 us
    ppermute x1, starting transfers between devices, per_device(): edge = lax.ppermute(edge, 'gy', pairs)  1.6 us
    ppermute x1, waiting for transfers between devices, per_device(): edges += [edge, lax.ppermute(corner, 'col', swap)]  1.12 us
    pallas_call x1, Pallas kernels, per_device(): pl.pallas_call(pack_kernel, out_shape=shape((columns // BX * height + TIL...  0.82 us
  transfers between devices with their start and end apart: 6, of which 4 were waited for; matrix products, arithmetic and copies ran while one was open for 0% of the time, Pallas kernels for 15%

profile of v9, /device:TPU:0, one launch (start us, length us, event | category | flops | bytes accessed | tf_op | source)
XLA Modules:
  0.0 25.6 jit_solution(11734512469123032224)
XLA Ops:
  0.6 0.8 %pack.1.refs_4_.refs_0_ = bf16[272,128]{1,0:T(8,128)(2,1)S(1)} custom-call(bf16[128,256]{1,0:T(8,128)(2,1)} %bitcast.13, s32[1,16]{1,0:T(1,128)} %bitcast.14), custom_call_target="tpu_custom_call" | custom-call | tf_op jit(solution)/shard_map/pack/pallas_call | solution.py:586
  1.5 3.1 %collective-permute-start.2 = (bf16[272,128]{1,0:T(8,128)(2,1)S(1)}, bf16[272,128]{1,0:T(8,128)(2,1)S(1)}, u32[]{:S(2)}, u32[]{:S(2)}) collective-permute-start(bf16[272,128]{1,0:T(8,128)(2,1)S(1)} %pack.1.refs_4_.refs_0_), channel_id=1, source_target_pairs={{12,0},{0,4},{4,8},{8,12},{13,1},{1,5},{5,9},{9,13},{14,2},{2,6},{... | collective-permute-start | bytes 208904 | tf_op jit(solution)/shard_map/ppermute | solution.py:602
  4.5 2.6 %collective-permute-start.1 = (bf16[272,128]{1,0:T(8,128)(2,1)S(1)}, bf16[272,128]{1,0:T(8,128)(2,1)S(1)}, u32[]{:S(2)}, u32[]{:S(2)}) collective-permute-start(bf16[272,128]{1,0:T(8,128)(2,1)S(1)} %pack.1.refs_4_.refs_0_), channel_id=1, source_target_pairs={{8,0},{12,4},{0,8},{4,12},{9,1},{13,5},{1,9},{5,13},{10,2},{14,6},... | collective-permute-start | bytes 208904 | tf_op jit(solution)/shard_map/ppermute | solution.py:602
  7.1 1.3 %collective-permute-start = (bf16[272,128]{1,0:T(8,128)(2,1)S(1)}, bf16[272,128]{1,0:T(8,128)(2,1)S(1)}, u32[]{:S(2)}, u32[]{:S(2)}) collective-permute-start(bf16[272,128]{1,0:T(8,128)(2,1)S(1)} %pack.1.refs_4_.refs_0_), channel_id=1, source_target_pairs={{4,0},{8,4},{12,8},{0,12},{5,1},{9,5},{13,9},{1,13},{6,2},{10,6},{... | collective-permute-start | bytes 208904 | tf_op jit(solution)/shard_map/ppermute | solution.py:602
  8.5 1.8 %banded.1 = (bf16[288,256]{1,0:T(8,128)(2,1)S(1)}, bf16[192,576]{1,0:T(8,128)(2,1)S(1)}, f32[32,128]{1,0:T(8,128)S(1)}) custom-call(bf16[8,27]{1,0:T(8,128)(2,1)} %bitcast.16, f32[8]{0:T(128)} %refs_1_.1, bf16[16,27]{1,0:T(8,128)(2,1)} %bitcast.15, f32[2]{0:T(128)} %refs_3_.1, bf16[272,128]{1,0:T(8,128)(2,1)S(1)} %pack.1.refs_4_.refs_0_), custom_call_target="tpu_custom_call" | custom-call | flops 20971520 | bytes 4194304 | tf_op jit(solution)/shard_map/banded/pallas_call | solution.py:609
  10.3 0.0 collective-permute-done.2.refs_3_
  10.3 1.6 %collective-permute-done.1.refs_2_ = bf16[272,128]{1,0:T(8,128)(2,1)S(1)} collective-permute-done((bf16[272,128]{1,0:T(8,128)(2,1)S(1)}, bf16[272,128]{1,0:T(8,128)(2,1)S(1)}, u32[]{:S(2)}, u32[]{:S(2)}) %collective-permute-start.1) | collective-permute-done | bytes 69664 | tf_op jit(solution)/shard_map/ppermute | solution.py:602
  11.8 0.2 collective-permute-done.refs_1_
  12.0 0.1 collective-permute-start.3
  12.1 1.6 %collective-permute-start.4 = (bf16[32,256]{1,0:T(8,128)(2,1)S(1)}, bf16[32,256]{1,0:T(8,128)(2,1)S(1)}, u32[]{:S(2)}, u32[]{:S(2)}) collective-permute-start(bf16[32,256]{1,0:T(8,128)(2,1)S(1)} %get-tuple-element.16), channel_id=1, source_target_pairs={{0,2},{2,0},{1,3},{3,1},{4,6},{6,4},{5,7},{7,5},{8,10},{10,8},{9,1... | collective-permute-start | bytes 49160 | tf_op jit(solution)/shard_map/ppermute | solution.py:677
  13.7 2.0 %prepare.1 = (f32[512,128]{1,0:T(8,128)S(1)}, f32[512,128]{1,0:T(8,128)S(1)}, f32[512,128]{1,0:T(8,128)S(1)}, f32[512,128]{1,0:T(8,128)S(1)}, f32[512,128]{1,0:T(8,128)S(1)}) custom-call(f32[1024,128]{1,0:T(8,128)} %bitcast.11, bf16[512,128]{1,0:T(8,128)(2,1)} %bitcast.12, bf16[512,128]{1,0:T(8,128)(2,1)S(1)} %get-tuple-element.15._), custom_call_target="tpu_custom_call" | custom-call | flops 3932160 | bytes 1048576 | tf_op jit(solution)/shard_map/prepare/pallas_call | solution.py:654
  15.7 0.2 collective-permute-done.4.edge_ref.refs_5_
  15.9 0.1 collective-permute-start.5
  16.0 1.1 %collective-permute-done.5.refs_6_ = bf16[32,128]{1,0:T(8,128)(2,1)S(1)} collective-permute-done((bf16[32,128]{1,0:T(8,128)(2,1)S(1)}, bf16[32,128]{1,0:T(8,128)(2,1)S(1)}, u32[]{:S(2)}, u32[]{:S(2)}) %collective-permute-start.5) | collective-permute-done | bytes 8224 | tf_op jit(solution)/shard_map/ppermute | solution.py:686
  17.1 0.0 collective-permute-done.3.refs_4_
  17.1 8.5 %column.1 = (bf16[2,4,32,256]{3,2,1,0:T(8,128)(2,1)}, f32[1024,128]{1,0:T(8,128)}) custom-call(bf16[272,128]{1,0:T(8,128)(2,1)S(1)} %pack.1.refs_4_.refs_0_, bf16[272,128]{1,0:T(8,128)(2,1)S(1)} %collective-permute-done.refs_1_, bf16[272,128]{1,0:T(8,128)(2,1)S(1)} %collective-permute-done.1.refs_2_, bf16[272,128]{1,0:T(8,128)(2,1)S(1)} %collective-permute-done.2.refs_3_, ...), custom_call_target="tpu_custom_call" | custom-call | flops 2264924160 | bytes 4194304 | tf_op jit(solution)/shard_map/column/pallas_call | solution.py:689
  (2 shorter events, 0.0 us)
Async XLA Ops:
  1.5 8.8 %collective-permute-start.2 = (bf16[272,128]{1,0:T(8,128)(2,1)S(1)}, bf16[272,128]{1,0:T(8,128)(2,1)S(1)}, u32[]{:S(2)}, u32[]{:S(2)}) collective-permute-start(bf16[272,128]{1,0:T(8,128)(2,1)S(1)} %pack.1.refs_4_.refs_0_), channel_id=1, source_target_pairs={{12,0},{0,4},{4,8},{8,12},{13,1},{1,5},{5,9},{9,13},{14,2},{2,6},{... | collective-permute-start | bytes 208904 | tf_op jit(solution)/shard_map/ppermute | solution.py:602
  4.5 7.3 %collective-permute-start.1 = (bf16[272,128]{1,0:T(8,128)(2,1)S(1)}, bf16[272,128]{1,0:T(8,128)(2,1)S(1)}, u32[]{:S(2)}, u32[]{:S(2)}) collective-permute-start(bf16[272,128]{1,0:T(8,128)(2,1)S(1)} %pack.1.refs_4_.refs_0_), channel_id=1, source_target_pairs={{8,0},{12,4},{0,8},{4,12},{9,1},{13,5},{1,9},{5,13},{10,2},{14,6},... | collective-permute-start | bytes 208904 | tf_op jit(solution)/shard_map/ppermute | solution.py:602
  7.1 4.9 %collective-permute-start = (bf16[272,128]{1,0:T(8,128)(2,1)S(1)}, bf16[272,128]{1,0:T(8,128)(2,1)S(1)}, u32[]{:S(2)}, u32[]{:S(2)}) collective-permute-start(bf16[272,128]{1,0:T(8,128)(2,1)S(1)} %pack.1.refs_4_.refs_0_), channel_id=1, source_target_pairs={{4,0},{8,4},{12,8},{0,12},{5,1},{9,5},{13,9},{1,13},{6,2},{10,6},{... | collective-permute-start | bytes 208904 | tf_op jit(solution)/shard_map/ppermute | solution.py:602
  12.0 5.1 %collective-permute-start.3 = (bf16[512,128]{1,0:T(8,128)(2,1)S(1)}, bf16[512,128]{1,0:T(8,128)(2,1)S(1)}, u32[]{:S(2)}, u32[]{:S(2)}) collective-permute-start(bf16[512,128]{1,0:T(8,128)(2,1)S(1)} %get-tuple-element.15._), channel_id=1, source_target_pairs={{0,1},{1,0},{2,3},{3,2},{4,5},{5,4},{6,7},{7,6},{8,9},{9,8},{10,11... | collective-permute-start | bytes 393224 | tf_op jit(solution)/shard_map/ppermute | solution.py:687
  12.1 3.8 %collective-permute-start.4 = (bf16[32,256]{1,0:T(8,128)(2,1)S(1)}, bf16[32,256]{1,0:T(8,128)(2,1)S(1)}, u32[]{:S(2)}, u32[]{:S(2)}) collective-permute-start(bf16[32,256]{1,0:T(8,128)(2,1)S(1)} %get-tuple-element.16), channel_id=1, source_target_pairs={{0,2},{2,0},{1,3},{3,1},{4,6},{6,4},{5,7},{7,5},{8,10},{10,8},{9,1... | collective-permute-start | bytes 49160 | tf_op jit(solution)/shard_map/ppermute | solution.py:677
  15.9 1.2 %collective-permute-start.5 = (bf16[32,128]{1,0:T(8,128)(2,1)S(1)}, bf16[32,128]{1,0:T(8,128)(2,1)S(1)}, u32[]{:S(2)}, u32[]{:S(2)}) collective-permute-start(bf16[32,128]{1,0:T(8,128)(2,1)S(1)} %corner.1), channel_id=1, source_target_pairs={{0,1},{1,0},{2,3},{3,2},{4,5},{5,4},{6,7},{7,6},{8,9},{9,8},{10,11... | collective-permute-start | bytes 24584 | tf_op jit(solution)/shard_map/ppermute | solution.py:686

commit v10 on v9

--- a/solution.py
+++ b/solution.py
@@ -313,7 +313,10 @@
     brick_count = rows // BY * brick_columns
     capacity = slots // count_gz
     single = segment == count_gz
-    first_tile = z_index if few > 1 else 0
+
+    def tile_of(i):
+        return jnp.bitwise_xor(z_index, i) if few > 1 else i
+
     size = depth * BY
 
     def tile_rows(i, start, size):
@@ -452,15 +455,15 @@
         hidden[0] = jnp.zeros((TALL, 2 * window), jnp.bfloat16)
         hidden[depths + 1] = jnp.zeros((TALL, 2 * window), jnp.bfloat16)
         for i in range(count_gz):
-            tile = lax.rem(first_tile + i, count_gz)
+            tile = tile_of(i)
             for zz in range(depth):
                 shifts(i, zz, tile * depth + zz + 2, None)
 
-        @pl.loop(0, depths // 2, unroll=2)
+        @pl.loop(0, depths // 2, unroll=4)
         def _(k):
             first(2 * k, None)
 
-        @pl.loop(0, depths // 2, unroll=2)
+        @pl.loop(0, depths // 2, unroll=4)
         def _(k):
             second(2 * k, 0)
 
@@ -499,7 +502,7 @@
 
     @pl.loop(0, count_gz)
     def _(i):
-        first = lax.rem(first_tile + i, count_gz) * capacity
+        first = tile_of(i) * capacity
         rank = jnp.int32(0)
         for b in range(brick_count):
             mine = owner_table[i, 0, b] == z_index
@@ -596,10 +599,10 @@
         name="pack",
     )(in_hbm(density.reshape(height, columns)), in_hbm(owners.reshape(1, brick_count)))
 
-    few = count_gz if count_gz == segment else 1
+    few = count_gz if count_gz in (2, 4) else 1
     if few > 1:
         tiles = [payload] + [
-            lax.ppermute(payload, "gz", [((i + s) % count_gz, i) for i in range(count_gz)])
+            lax.ppermute(payload, "gz", [(i, i ^ s) for i in range(count_gz)])
             for s in range(1, count_gz)
         ]
     else:

time: 25.8 us -> 25.4 us (0.984)
  waiting for transfers between devices: 3.05 us -> 4.88 us
  starting transfers between devices: 8.74 us -> 7.4 us
  Pallas kernels: 13.1 us -> 12.3 us
    ppermute x3, waiting for transfers between devices: 1.74 us -> 3.47 us  [per_device(): lax.ppermute(payload, 'gz', [(i, i ^ s) for i in range(count_gz)])]
    ppermute x3, starting transfers between devices: 7.01 us -> 5.76 us  [per_device(): lax.ppermute(payload, 'gz', [(i, i ^ s) for i in range(count_gz)])]
    pallas_call x1, Pallas kernels: 8.49 us -> 7.63 us  [per_device(): pl.pallas_call(functools.partial(column_kernel, (count_gz, count_gy, dept...]
where the time goes in v10:
time: 25.4 us; the launch traced here: 25.2 us
  Pallas kernels  12.3 us (48%)
  starting transfers between devices  7.4 us (29%)
  waiting for transfers between devices  4.88 us (19%)
  between operations  0.67 us (3%)
    pallas_call x1, Pallas kernels, per_device(): pl.pallas_call(functools.partial(column_kernel, (count_gz, count_gy, dept...  7.63 us
    ppermute x3, starting transfers between devices, per_device(): lax.ppermute(payload, 'gz', [(i, i ^ s) for i in range(count_gz)])  5.76 us
    ppermute x3, waiting for transfers between devices, per_device(): lax.ppermute(payload, 'gz', [(i, i ^ s) for i in range(count_gz)])  3.47 us
    pallas_call x1, Pallas kernels, per_device(): pl.pallas_call(functools.partial(prepare_kernel, (depth, slots)), out_sha...  2 us
    pallas_call x1, Pallas kernels, per_device(): pl.pallas_call(banded_kernel, out_shape=(shape((2 * TALL, 4 * PART), bf16...  1.79 us
    ppermute x1, starting transfers between devices, per_device(): edge = lax.ppermute(edge, 'gy', pairs)  1.56 us
    ppermute x1, waiting for transfers between devices, per_device(): edges += [edge, lax.ppermute(corner, 'col', swap)]  1.16 us
    pallas_call x1, Pallas kernels, per_device(): pl.pallas_call(pack_kernel, out_shape=shape((columns // BX * height + TIL...  0.82 us
  transfers between devices with their start and end apart: 6, of which 4 were waited for; matrix products, arithmetic and copies ran while one was open for 0% of the time, Pallas kernels for 15%

profile of v10, /device:TPU:0, one launch (start us, length us, event | category | flops | bytes accessed | tf_op | source)
XLA Modules:
  0.0 25.2 jit_solution(9511853161184053726)
XLA Ops:
  0.6 0.8 %pack.1.refs_4_.refs_0_ = bf16[272,128]{1,0:T(8,128)(2,1)S(1)} custom-call(bf16[128,256]{1,0:T(8,128)(2,1)} %bitcast.13, s32[1,16]{1,0:T(1,128)} %bitcast.14), custom_call_target="tpu_custom_call" | custom-call | tf_op jit(solution)/shard_map/pack/pallas_call | solution.py:589
  1.5 5.1 %collective-permute-start.2 = (bf16[272,128]{1,0:T(8,128)(2,1)S(1)}, bf16[272,128]{1,0:T(8,128)(2,1)S(1)}, u32[]{:S(2)}, u32[]{:S(2)}) collective-permute-start(bf16[272,128]{1,0:T(8,128)(2,1)S(1)} %pack.1.refs_4_.refs_0_), channel_id=1, source_target_pairs={{0,12},{4,8},{8,4},{12,0},{1,13},{5,9},{9,5},{13,1},{2,14},{6,10},... | collective-permute-start | bytes 208904 | tf_op jit(solution)/shard_map/ppermute | solution.py:605
  6.6 0.0 collective-permute-start.1
  6.6 0.6 %collective-permute-start = (bf16[272,128]{1,0:T(8,128)(2,1)S(1)}, bf16[272,128]{1,0:T(8,128)(2,1)S(1)}, u32[]{:S(2)}, u32[]{:S(2)}) collective-permute-start(bf16[272,128]{1,0:T(8,128)(2,1)S(1)} %pack.1.refs_4_.refs_0_), channel_id=1, source_target_pairs={{0,4},{4,0},{8,12},{12,8},{1,5},{5,1},{9,13},{13,9},{2,6},{6,2},{1... | collective-permute-start | bytes 208904 | tf_op jit(solution)/shard_map/ppermute | solution.py:605
  7.2 1.8 %banded.1 = (bf16[288,256]{1,0:T(8,128)(2,1)S(1)}, bf16[192,576]{1,0:T(8,128)(2,1)S(1)}, f32[32,128]{1,0:T(8,128)S(1)}) custom-call(bf16[8,27]{1,0:T(8,128)(2,1)} %bitcast.16, f32[8]{0:T(128)} %refs_1_.1, bf16[16,27]{1,0:T(8,128)(2,1)} %bitcast.15, f32[2]{0:T(128)} %refs_3_.1, bf16[272,128]{1,0:T(8,128)(2,1)S(1)} %pack.1.refs_4_.refs_0_), custom_call_target="tpu_custom_call" | custom-call | flops 20971520 | bytes 4194304 | tf_op jit(solution)/shard_map/banded/pallas_call | solution.py:612
  9.0 0.2 collective-permute-done.2.refs_3_
  9.2 3.2 %collective-permute-done.1.refs_2_ = bf16[272,128]{1,0:T(8,128)(2,1)S(1)} collective-permute-done((bf16[272,128]{1,0:T(8,128)(2,1)S(1)}, bf16[272,128]{1,0:T(8,128)(2,1)S(1)}, u32[]{:S(2)}, u32[]{:S(2)}) %collective-permute-start.1) | collective-permute-done | bytes 69664 | tf_op jit(solution)/shard_map/ppermute | solution.py:605
  12.5 0.0 collective-permute-done.refs_1_
  12.5 0.1 collective-permute-start.3
  12.6 1.6 %collective-permute-start.4 = (bf16[32,256]{1,0:T(8,128)(2,1)S(1)}, bf16[32,256]{1,0:T(8,128)(2,1)S(1)}, u32[]{:S(2)}, u32[]{:S(2)}) collective-permute-start(bf16[32,256]{1,0:T(8,128)(2,1)S(1)} %get-tuple-element.16), channel_id=1, source_target_pairs={{0,2},{2,0},{1,3},{3,1},{4,6},{6,4},{5,7},{7,5},{8,10},{10,8},{9,1... | collective-permute-start | bytes 49160 | tf_op jit(solution)/shard_map/ppermute | solution.py:680
  14.2 2.0 %prepare.1 = (f32[512,128]{1,0:T(8,128)S(1)}, f32[512,128]{1,0:T(8,128)S(1)}, f32[512,128]{1,0:T(8,128)S(1)}, f32[512,128]{1,0:T(8,128)S(1)}, f32[512,128]{1,0:T(8,128)S(1)}) custom-call(f32[1024,128]{1,0:T(8,128)} %bitcast.11, bf16[512,128]{1,0:T(8,128)(2,1)} %bitcast.12, bf16[512,128]{1,0:T(8,128)(2,1)S(1)} %get-tuple-element.15._), custom_call_target="tpu_custom_call" | custom-call | flops 3932160 | bytes 1048576 | tf_op jit(solution)/shard_map/prepare/pallas_call | solution.py:657
  16.2 0.2 collective-permute-done.4.edge_ref.refs_5_
  16.4 0.0 collective-permute-start.5
  16.4 1.2 %collective-permute-done.5.refs_6_ = bf16[32,128]{1,0:T(8,128)(2,1)S(1)} collective-permute-done((bf16[32,128]{1,0:T(8,128)(2,1)S(1)}, bf16[32,128]{1,0:T(8,128)(2,1)S(1)}, u32[]{:S(2)}, u32[]{:S(2)}) %collective-permute-start.5) | collective-permute-done | bytes 8224 | tf_op jit(solution)/shard_map/ppermute | solution.py:689
  17.6 0.0 collective-permute-done.3.refs_4_
  17.6 7.6 %column.1 = (bf16[2,4,32,256]{3,2,1,0:T(8,128)(2,1)}, f32[1024,128]{1,0:T(8,128)}) custom-call(bf16[272,128]{1,0:T(8,128)(2,1)S(1)} %pack.1.refs_4_.refs_0_, bf16[272,128]{1,0:T(8,128)(2,1)S(1)} %collective-permute-done.refs_1_, bf16[272,128]{1,0:T(8,128)(2,1)S(1)} %collective-permute-done.1.refs_2_, bf16[272,128]{1,0:T(8,128)(2,1)S(1)} %collective-permute-done.2.refs_3_, ...), custom_call_target="tpu_custom_call" | custom-call | flops 2264924160 | bytes 4194304 | tf_op jit(solution)/shard_map/column/pallas_call | solution.py:692
  (2 shorter events, 0.0 us)
Async XLA Ops:
  1.5 7.8 %collective-permute-start.2 = (bf16[272,128]{1,0:T(8,128)(2,1)S(1)}, bf16[272,128]{1,0:T(8,128)(2,1)S(1)}, u32[]{:S(2)}, u32[]{:S(2)}) collective-permute-start(bf16[272,128]{1,0:T(8,128)(2,1)S(1)} %pack.1.refs_4_.refs_0_), channel_id=1, source_target_pairs={{0,12},{4,8},{8,4},{12,0},{1,13},{5,9},{9,5},{13,1},{2,14},{6,10},... | collective-permute-start | bytes 208904 | tf_op jit(solution)/shard_map/ppermute | solution.py:605
  6.6 5.9 %collective-permute-start.1 = (bf16[272,128]{1,0:T(8,128)(2,1)S(1)}, bf16[272,128]{1,0:T(8,128)(2,1)S(1)}, u32[]{:S(2)}, u32[]{:S(2)}) collective-permute-start(bf16[272,128]{1,0:T(8,128)(2,1)S(1)} %pack.1.refs_4_.refs_0_), channel_id=1, source_target_pairs={{0,8},{4,12},{8,0},{12,4},{1,9},{5,13},{9,1},{13,5},{2,10},{6,14},... | collective-permute-start | bytes 208904 | tf_op jit(solution)/shard_map/ppermute | solution.py:605
  6.6 5.9 %collective-permute-start = (bf16[272,128]{1,0:T(8,128)(2,1)S(1)}, bf16[272,128]{1,0:T(8,128)(2,1)S(1)}, u32[]{:S(2)}, u32[]{:S(2)}) collective-permute-start(bf16[272,128]{1,0:T(8,128)(2,1)S(1)} %pack.1.refs_4_.refs_0_), channel_id=1, source_target_pairs={{0,4},{4,0},{8,12},{12,8},{1,5},{5,1},{9,13},{13,9},{2,6},{6,2},{1... | collective-permute-start | bytes 208904 | tf_op jit(solution)/shard_map/ppermute | solution.py:605
  12.5 5.1 %collective-permute-start.3 = (bf16[512,128]{1,0:T(8,128)(2,1)S(1)}, bf16[512,128]{1,0:T(8,128)(2,1)S(1)}, u32[]{:S(2)}, u32[]{:S(2)}) collective-permute-start(bf16[512,128]{1,0:T(8,128)(2,1)S(1)} %get-tuple-element.15._), channel_id=1, source_target_pairs={{0,1},{1,0},{2,3},{3,2},{4,5},{5,4},{6,7},{7,6},{8,9},{9,8},{10,11... | collective-permute-start | bytes 393224 | tf_op jit(solution)/shard_map/ppermute | solution.py:690
  12.6 3.8 %collective-permute-start.4 = (bf16[32,256]{1,0:T(8,128)(2,1)S(1)}, bf16[32,256]{1,0:T(8,128)(2,1)S(1)}, u32[]{:S(2)}, u32[]{:S(2)}) collective-permute-start(bf16[32,256]{1,0:T(8,128)(2,1)S(1)} %get-tuple-element.16), channel_id=1, source_target_pairs={{0,2},{2,0},{1,3},{3,1},{4,6},{6,4},{5,7},{7,5},{8,10},{10,8},{9,1... | collective-permute-start | bytes 49160 | tf_op jit(solution)/shard_map/ppermute | solution.py:680
  16.4 1.2 %collective-permute-start.5 = (bf16[32,128]{1,0:T(8,128)(2,1)S(1)}, bf16[32,128]{1,0:T(8,128)(2,1)S(1)}, u32[]{:S(2)}, u32[]{:S(2)}) collective-permute-start(bf16[32,128]{1,0:T(8,128)(2,1)S(1)} %corner.1), channel_id=1, source_target_pairs={{0,1},{1,0},{2,3},{3,2},{4,5},{5,4},{6,7},{7,6},{8,9},{9,8},{10,11... | collective-permute-start | bytes 24584 | tf_op jit(solution)/shard_map/ppermute | solution.py:689

commit v11 on v10

--- a/solution.py
+++ b/solution.py
@@ -459,11 +459,11 @@
             for zz in range(depth):
                 shifts(i, zz, tile * depth + zz + 2, None)
 
-        @pl.loop(0, depths // 2, unroll=4)
+        @pl.loop(0, depths // 2, unroll=8)
         def _(k):
             first(2 * k, None)
 
-        @pl.loop(0, depths // 2, unroll=4)
+        @pl.loop(0, depths // 2, unroll=8)
         def _(k):
             second(2 * k, 0)
 

time: 25.4 us -> 25.7 us (1.012)
  no operation moved by 1% of the time
where the time goes in v11:
time: 25.7 us; the launch traced here: 25.4 us
  Pallas kernels  12.5 us (49%)
  starting transfers between devices  7.4 us (29%)
  waiting for transfers between devices  4.88 us (19%)
  between operations  0.67 us (3%)
    pallas_call x1, Pallas kernels, per_device(): pl.pallas_call(functools.partial(column_kernel, (count_gz, count_gy, dept...  7.85 us
    ppermute x3, starting transfers between devices, per_device(): lax.ppermute(payload, 'gz', [(i, i ^ s) for i in range(count_gz)])  5.76 us
    ppermute x3, waiting for transfers between devices, per_device(): lax.ppermute(payload, 'gz', [(i, i ^ s) for i in range(count_gz)])  3.47 us
    pallas_call x1, Pallas kernels, per_device(): pl.pallas_call(functools.partial(prepare_kernel, (depth, slots)), out_sha...  2 us
    pallas_call x1, Pallas kernels, per_device(): pl.pallas_call(banded_kernel, out_shape=(shape((2 * TALL, 4 * PART), bf16...  1.79 us
    ppermute x1, starting transfers between devices, per_device(): edge = lax.ppermute(edge, 'gy', pairs)  1.56 us
    ppermute x1, waiting for transfers between devices, per_device(): edges += [edge, lax.ppermute(corner, 'col', swap)]  1.16 us
    pallas_call x1, Pallas kernels, per_device(): pl.pallas_call(pack_kernel, out_shape=shape((columns // BX * height + TIL...  0.82 us
  transfers between devices with their start and end apart: 6, of which 4 were waited for; matrix products, arithmetic and copies ran while one was open for 0% of the time, Pallas kernels for 15%

profile of v11, /device:TPU:0, one launch (start us, length us, event | category | flops | bytes accessed | tf_op | source)
XLA Modules:
  0.0 25.4 jit_solution(5953271063698128376)
XLA Ops:
  0.6 0.8 %pack.1.refs_4_.refs_0_ = bf16[272,128]{1,0:T(8,128)(2,1)S(1)} custom-call(bf16[128,256]{1,0:T(8,128)(2,1)} %bitcast.13, s32[1,16]{1,0:T(1,128)} %bitcast.14), custom_call_target="tpu_custom_call" | custom-call | tf_op jit(solution)/shard_map/pack/pallas_call | solution.py:589
  1.5 5.1 %collective-permute-start.2 = (bf16[272,128]{1,0:T(8,128)(2,1)S(1)}, bf16[272,128]{1,0:T(8,128)(2,1)S(1)}, u32[]{:S(2)}, u32[]{:S(2)}) collective-permute-start(bf16[272,128]{1,0:T(8,128)(2,1)S(1)} %pack.1.refs_4_.refs_0_), channel_id=1, source_target_pairs={{0,12},{4,8},{8,4},{12,0},{1,13},{5,9},{9,5},{13,1},{2,14},{6,10},... | collective-permute-start | bytes 208904 | tf_op jit(solution)/shard_map/ppermute | solution.py:605
  6.6 0.0 collective-permute-start.1
  6.6 0.6 %collective-permute-start = (bf16[272,128]{1,0:T(8,128)(2,1)S(1)}, bf16[272,128]{1,0:T(8,128)(2,1)S(1)}, u32[]{:S(2)}, u32[]{:S(2)}) collective-permute-start(bf16[272,128]{1,0:T(8,128)(2,1)S(1)} %pack.1.refs_4_.refs_0_), channel_id=1, source_target_pairs={{0,4},{4,0},{8,12},{12,8},{1,5},{5,1},{9,13},{13,9},{2,6},{6,2},{1... | collective-permute-start | bytes 208904 | tf_op jit(solution)/shard_map/ppermute | solution.py:605
  7.2 1.8 %banded.1 = (bf16[288,256]{1,0:T(8,128)(2,1)S(1)}, bf16[192,576]{1,0:T(8,128)(2,1)S(1)}, f32[32,128]{1,0:T(8,128)S(1)}) custom-call(bf16[8,27]{1,0:T(8,128)(2,1)} %bitcast.16, f32[8]{0:T(128)} %refs_1_.1, bf16[16,27]{1,0:T(8,128)(2,1)} %bitcast.15, f32[2]{0:T(128)} %refs_3_.1, bf16[272,128]{1,0:T(8,128)(2,1)S(1)} %pack.1.refs_4_.refs_0_), custom_call_target="tpu_custom_call" | custom-call | flops 20971520 | bytes 4194304 | tf_op jit(solution)/shard_map/banded/pallas_call | solution.py:612
  9.0 0.2 collective-permute-done.2.refs_3_
  9.2 3.2 %collective-permute-done.1.refs_2_ = bf16[272,128]{1,0:T(8,128)(2,1)S(1)} collective-permute-done((bf16[272,128]{1,0:T(8,128)(2,1)S(1)}, bf16[272,128]{1,0:T(8,128)(2,1)S(1)}, u32[]{:S(2)}, u32[]{:S(2)}) %collective-permute-start.1) | collective-permute-done | bytes 69664 | tf_op jit(solution)/shard_map/ppermute | solution.py:605
  12.5 0.0 collective-permute-done.refs_1_
  12.5 0.1 collective-permute-start.3
  12.6 1.6 %collective-permute-start.4 = (bf16[32,256]{1,0:T(8,128)(2,1)S(1)}, bf16[32,256]{1,0:T(8,128)(2,1)S(1)}, u32[]{:S(2)}, u32[]{:S(2)}) collective-permute-start(bf16[32,256]{1,0:T(8,128)(2,1)S(1)} %get-tuple-element.16), channel_id=1, source_target_pairs={{0,2},{2,0},{1,3},{3,1},{4,6},{6,4},{5,7},{7,5},{8,10},{10,8},{9,1... | collective-permute-start | bytes 49160 | tf_op jit(solution)/shard_map/ppermute | solution.py:680
  14.2 2.0 %prepare.1 = (f32[512,128]{1,0:T(8,128)S(1)}, f32[512,128]{1,0:T(8,128)S(1)}, f32[512,128]{1,0:T(8,128)S(1)}, f32[512,128]{1,0:T(8,128)S(1)}, f32[512,128]{1,0:T(8,128)S(1)}) custom-call(f32[1024,128]{1,0:T(8,128)} %bitcast.11, bf16[512,128]{1,0:T(8,128)(2,1)} %bitcast.12, bf16[512,128]{1,0:T(8,128)(2,1)S(1)} %get-tuple-element.15._), custom_call_target="tpu_custom_call" | custom-call | flops 3932160 | bytes 1048576 | tf_op jit(solution)/shard_map/prepare/pallas_call | solution.py:657
  16.2 0.2 collective-permute-done.4.edge_ref.refs_5_
  16.4 0.0 collective-permute-start.5
  16.4 1.2 %collective-permute-done.5.refs_6_ = bf16[32,128]{1,0:T(8,128)(2,1)S(1)} collective-permute-done((bf16[32,128]{1,0:T(8,128)(2,1)S(1)}, bf16[32,128]{1,0:T(8,128)(2,1)S(1)}, u32[]{:S(2)}, u32[]{:S(2)}) %collective-permute-start.5) | collective-permute-done | bytes 8224 | tf_op jit(solution)/shard_map/ppermute | solution.py:689
  17.6 0.0 collective-permute-done.3.refs_4_
  17.6 7.8 %column.1 = (bf16[2,4,32,256]{3,2,1,0:T(8,128)(2,1)}, f32[1024,128]{1,0:T(8,128)}) custom-call(bf16[272,128]{1,0:T(8,128)(2,1)S(1)} %pack.1.refs_4_.refs_0_, bf16[272,128]{1,0:T(8,128)(2,1)S(1)} %collective-permute-done.refs_1_, bf16[272,128]{1,0:T(8,128)(2,1)S(1)} %collective-permute-done.1.refs_2_, bf16[272,128]{1,0:T(8,128)(2,1)S(1)} %collective-permute-done.2.refs_3_, ...), custom_call_target="tpu_custom_call" | custom-call | flops 2264924160 | bytes 4194304 | tf_op jit(solution)/shard_map/column/pallas_call | solution.py:692
  (2 shorter events, 0.0 us)
Async XLA Ops:
  1.5 7.8 %collective-permute-start.2 = (bf16[272,128]{1,0:T(8,128)(2,1)S(1)}, bf16[272,128]{1,0:T(8,128)(2,1)S(1)}, u32[]{:S(2)}, u32[]{:S(2)}) collective-permute-start(bf16[272,128]{1,0:T(8,128)(2,1)S(1)} %pack.1.refs_4_.refs_0_), channel_id=1, source_target_pairs={{0,12},{4,8},{8,4},{12,0},{1,13},{5,9},{9,5},{13,1},{2,14},{6,10},... | collective-permute-start | bytes 208904 | tf_op jit(solution)/shard_map/ppermute | solution.py:605
  6.6 5.9 %collective-permute-start.1 = (bf16[272,128]{1,0:T(8,128)(2,1)S(1)}, bf16[272,128]{1,0:T(8,128)(2,1)S(1)}, u32[]{:S(2)}, u32[]{:S(2)}) collective-permute-start(bf16[272,128]{1,0:T(8,128)(2,1)S(1)} %pack.1.refs_4_.refs_0_), channel_id=1, source_target_pairs={{0,8},{4,12},{8,0},{12,4},{1,9},{5,13},{9,1},{13,5},{2,10},{6,14},... | collective-permute-start | bytes 208904 | tf_op jit(solution)/shard_map/ppermute | solution.py:605
  6.6 5.9 %collective-permute-start = (bf16[272,128]{1,0:T(8,128)(2,1)S(1)}, bf16[272,128]{1,0:T(8,128)(2,1)S(1)}, u32[]{:S(2)}, u32[]{:S(2)}) collective-permute-start(bf16[272,128]{1,0:T(8,128)(2,1)S(1)} %pack.1.refs_4_.refs_0_), channel_id=1, source_target_pairs={{0,4},{4,0},{8,12},{12,8},{1,5},{5,1},{9,13},{13,9},{2,6},{6,2},{1... | collective-permute-start | bytes 208904 | tf_op jit(solution)/shard_map/ppermute | solution.py:605
  12.5 5.1 %collective-permute-start.3 = (bf16[512,128]{1,0:T(8,128)(2,1)S(1)}, bf16[512,128]{1,0:T(8,128)(2,1)S(1)}, u32[]{:S(2)}, u32[]{:S(2)}) collective-permute-start(bf16[512,128]{1,0:T(8,128)(2,1)S(1)} %get-tuple-element.15._), channel_id=1, source_target_pairs={{0,1},{1,0},{2,3},{3,2},{4,5},{5,4},{6,7},{7,6},{8,9},{9,8},{10,11... | collective-permute-start | bytes 393224 | tf_op jit(solution)/shard_map/ppermute | solution.py:690
  12.6 3.8 %collective-permute-start.4 = (bf16[32,256]{1,0:T(8,128)(2,1)S(1)}, bf16[32,256]{1,0:T(8,128)(2,1)S(1)}, u32[]{:S(2)}, u32[]{:S(2)}) collective-permute-start(bf16[32,256]{1,0:T(8,128)(2,1)S(1)} %get-tuple-element.16), channel_id=1, source_target_pairs={{0,2},{2,0},{1,3},{3,1},{4,6},{6,4},{5,7},{7,5},{8,10},{10,8},{9,1... | collective-permute-start | bytes 49160 | tf_op jit(solution)/shard_map/ppermute | solution.py:680
  16.4 1.2 %collective-permute-start.5 = (bf16[32,128]{1,0:T(8,128)(2,1)S(1)}, bf16[32,128]{1,0:T(8,128)(2,1)S(1)}, u32[]{:S(2)}, u32[]{:S(2)}) collective-permute-start(bf16[32,128]{1,0:T(8,128)(2,1)S(1)} %corner.1), channel_id=1, source_target_pairs={{0,1},{1,0},{2,3},{3,2},{4,5},{5,4},{6,7},{7,6},{8,9},{9,8},{10,11... | collective-permute-start | bytes 24584 | tf_op jit(solution)/shard_map/ppermute | solution.py:689

commit v12 on v10

--- a/solution.py
+++ b/solution.py
@@ -167,7 +167,7 @@
 
 def edges_kernel(dims, *refs):
     count_gy, depth, rows, columns, few, count = dims
-    tiles, outs = refs[:few], refs[few + 1 :]
+    tiles, outs = refs[:few], refs[few + 2 :]
     g = lax.axis_index("gy")
     c = lax.axis_index("col")
     height = depth * rows
@@ -208,7 +208,7 @@
         pl.loop(0, count // 2)(pair)
 
 
-def corner_kernel(edge_ref, _, corner_ref):
+def corner_kernel(edge_ref, corner_ref):
     c = lax.axis_index("col")
     corner_ref[...] = jnp.where(c == 0, edge_ref[:, BX:], edge_ref[:, 0:BX])
 
@@ -609,6 +609,27 @@
         tiles = [lax.all_gather(payload, "gz", axis=0, tiled=False)]
 
     cells = depth * BY
+    prepared = pl.pallas_call(
+        functools.partial(prepare_kernel, (depth, slots)),
+        out_shape=[shape((slots * cells, BX), f32)] * 5,
+        in_specs=[HBM, HBM, ANY],
+        out_specs=[VMEM] * 5,
+        scratch_shapes=[
+            pltpu.VMEM((slots * 2 * cells, BX), f32),
+            pltpu.VMEM((slots * cells, BX), bf16),
+            pltpu.VMEM((slots * cells, BX), f32),
+            pltpu.SemaphoreType.DMA((slots // 8, 2)),
+        ],
+        compiler_params=pltpu.CompilerParams(vmem_limit_bytes=12 * 2**20),
+        cost_estimate=pl.CostEstimate(
+            flops=60 * slots * cells * BX, bytes_accessed=2**20, transcendentals=0
+        ),
+        name="prepare",
+    )(
+        in_hbm(solutes.reshape(slots * 2 * cells, BX)),
+        in_hbm(biomass.reshape(slots * cells, BX)),
+        payload,
+    )
     t1, t2, bias2 = pl.pallas_call(
         banded_kernel,
         out_shape=(
@@ -649,44 +670,28 @@
         functools.partial(edges_kernel, (count_gy, depth, rows, columns, few, count_gz)),
         out_shape=[shape((depths * rows, BX), bf16)]
         + [shape((2 * depths, columns), bf16)] * directions,
-        in_specs=[VMEM] * few + [ANY],
+        in_specs=[VMEM] * few + [ANY, ANY],
         out_specs=[VMEM] * (1 + directions),
         compiler_params=pltpu.CompilerParams(vmem_limit_bytes=16 * 2**20),
         name="edges",
-    )(*tiles, bias2)
-    prepared = pl.pallas_call(
-        functools.partial(prepare_kernel, (depth, slots)),
-        out_shape=[shape((slots * cells, BX), f32)] * 5,
-        in_specs=[HBM, HBM, ANY],
-        out_specs=[VMEM] * 5,
-        scratch_shapes=[
-            pltpu.VMEM((slots * 2 * cells, BX), f32),
-            pltpu.VMEM((slots * cells, BX), bf16),
-            pltpu.VMEM((slots * cells, BX), f32),
-            pltpu.SemaphoreType.DMA((slots // 8, 2)),
-        ],
-        compiler_params=pltpu.CompilerParams(vmem_limit_bytes=12 * 2**20),
-        cost_estimate=pl.CostEstimate(
-            flops=60 * slots * cells * BX, bytes_accessed=2**20, transcendentals=0
-        ),
-        name="prepare",
-    )(
-        in_hbm(solutes.reshape(slots * 2 * cells, BX)),
-        in_hbm(biomass.reshape(slots * cells, BX)),
-        near,
-    )
+    )(*tiles, bias2, prepared[-1])
     edges = []
     for pairs, edge in zip(ways, sent):
-        edge = lax.ppermute(edge, "gy", pairs)
         corner = pl.pallas_call(
             corner_kernel,
             out_shape=shape((2 * depths, BX), bf16),
-            in_specs=[VMEM, ANY],
+            in_specs=[VMEM],
             out_specs=VMEM,
             compiler_params=pltpu.CompilerParams(vmem_limit_bytes=4 * 2**20),
             name="corner",
-        )(edge, prepared[-1])
-        edges += [edge, lax.ppermute(corner, "col", swap)]
+        )(edge)
+        over = [
+            (gy * count_col + col, to * count_col + 1 - col)
+            for gy, to in pairs
+            for col in range(count_col)
+        ]
+        corner = lax.ppermute(corner, ("gy", "col"), over)
+        edges += [lax.ppermute(edge, "gy", pairs), corner]
     near = lax.ppermute(near, "col", swap)
 
     fractions, solutes_next = pl.pallas_call(

time: 25.4 us -> 25.1 us (0.988)
  waiting for transfers between devices: 4.88 us -> 4.23 us
  starting transfers between devices: 7.4 us -> 7.69 us
    ppermute x3, waiting for transfers between devices: 3.47 us -> 1.45 us  [per_device(): lax.ppermute(payload, 'gz', [(i, i ^ s) for i in range(count_gz)])]
    ppermute x2, waiting for transfers between devices: 1.4 us -> 2.77 us  [the longest x1 2.77 us: per_device(): corner = lax.ppermute(corner, ('gy', 'col'), over)]
    ppermute x2, starting transfers between devices: 1.57 us -> 1.86 us  [the longest x1 1.56 us: per_device(): edges += [lax.ppermute(edge, 'gy', pairs), corner]]
  transfers between devices with their start and end apart: 6 -> 6, of which waited for: 4 -> 2; matrix products, arithmetic and copies ran while one was open for 0% -> 0% of each run, Pallas kernels for 15% -> 15%
where the time goes in v12:
time: 25.1 us; the launch traced here: 24.9 us
  Pallas kernels  12.3 us (49%)
  starting transfers between devices  7.69 us (31%)
  waiting for transfers between devices  4.23 us (17%)
  between operations  0.68 us (3%)
    pallas_call x1, Pallas kernels, per_device(): pl.pallas_call(functools.partial(column_kernel, (count_gz, count_gy, dept...  7.67 us
    ppermute x3, starting transfers between devices, per_device(): lax.ppermute(payload, 'gz', [(i, i ^ s) for i in range(count_gz)])  5.76 us
    ppermute x1, waiting for transfers between devices, per_device(): corner = lax.ppermute(corner, ('gy', 'col'), over)  2.77 us
    pallas_call x1, Pallas kernels, per_device(): pl.pallas_call(functools.partial(prepare_kernel, (depth, slots)), out_sha...  2 us
    pallas_call x1, Pallas kernels, per_device(): pl.pallas_call(banded_kernel, out_shape=(shape((2 * TALL, 4 * PART), bf16...  1.79 us
    ppermute x1, starting transfers between devices, per_device(): edges += [lax.ppermute(edge, 'gy', pairs), corner]  1.56 us
    ppermute x3, waiting for transfers between devices, per_device(): lax.ppermute(payload, 'gz', [(i, i ^ s) for i in range(count_gz)])  1.45 us
    pallas_call x1, Pallas kernels, per_device(): pl.pallas_call(pack_kernel, out_shape=shape((columns // BX * height + TIL...  0.82 us
  transfers between devices with their start and end apart: 6, of which 2 were waited for; matrix products, arithmetic and copies ran while one was open for 0% of the time, Pallas kernels for 15%

profile of v12, /device:TPU:0, one launch (start us, length us, event | category | flops | bytes accessed | tf_op | source)
XLA Modules:
  0.0 24.9 jit_solution(5804192671255933230)
XLA Ops:
  0.6 0.8 %pack.1.refs_4_._.refs_0_ = bf16[272,128]{1,0:T(8,128)(2,1)S(1)} custom-call(bf16[128,256]{1,0:T(8,128)(2,1)} %bitcast.13, s32[1,16]{1,0:T(1,128)} %bitcast.14), custom_call_target="tpu_custom_call" | custom-call | tf_op jit(solution)/shard_map/pack/pallas_call | solution.py:589
  1.5 5.1 %collective-permute-start.2 = (bf16[272,128]{1,0:T(8,128)(2,1)S(1)}, bf16[272,128]{1,0:T(8,128)(2,1)S(1)}, u32[]{:S(2)}, u32[]{:S(2)}) collective-permute-start(bf16[272,128]{1,0:T(8,128)(2,1)S(1)} %pack.1.refs_4_._.refs_0_), channel_id=1, source_target_pairs={{0,12},{4,8},{8,4},{12,0},{1,13},{5,9},{9,5},{13,1},{2,14},{6,10},... | collective-permute-start | bytes 208904 | tf_op jit(solution)/shard_map/ppermute | solution.py:605
  6.6 0.0 collective-permute-start.1
  6.6 0.6 %collective-permute-start = (bf16[272,128]{1,0:T(8,128)(2,1)S(1)}, bf16[272,128]{1,0:T(8,128)(2,1)S(1)}, u32[]{:S(2)}, u32[]{:S(2)}) collective-permute-start(bf16[272,128]{1,0:T(8,128)(2,1)S(1)} %pack.1.refs_4_._.refs_0_), channel_id=1, source_target_pairs={{0,4},{4,0},{8,12},{12,8},{1,5},{5,1},{9,13},{13,9},{2,6},{6,2},{1... | collective-permute-start | bytes 208904 | tf_op jit(solution)/shard_map/ppermute | solution.py:605
  7.2 2.0 %prepare.1 = (f32[512,128]{1,0:T(8,128)S(1)}, f32[512,128]{1,0:T(8,128)S(1)}, f32[512,128]{1,0:T(8,128)S(1)}, f32[512,128]{1,0:T(8,128)S(1)}, f32[512,128]{1,0:T(8,128)S(1)}) custom-call(f32[1024,128]{1,0:T(8,128)} %bitcast.11, bf16[512,128]{1,0:T(8,128)(2,1)} %bitcast.12, bf16[272,128]{1,0:T(8,128)(2,1)S(1)} %pack.1.refs_4_._.refs_0_), custom_call_target="tpu_custom_call" | custom-call | flops 3932160 | bytes 1048576 | tf_op jit(solution)/shard_map/prepare/pallas_call | solution.py:612
  9.2 1.8 %banded.1 = (bf16[288,256]{1,0:T(8,128)(2,1)S(1)}, bf16[192,576]{1,0:T(8,128)(2,1)S(1)}, f32[32,128]{1,0:T(8,128)S(1)}) custom-call(bf16[8,27]{1,0:T(8,128)(2,1)} %bitcast.16, f32[8]{0:T(128)} %refs_1_.1, bf16[16,27]{1,0:T(8,128)(2,1)} %bitcast.15, f32[2]{0:T(128)} %refs_3_.1, bf16[272,128]{1,0:T(8,128)(2,1)S(1)} %pack.1.refs_4_._.refs_0_), custom_call_target="tpu_custom_call" | custom-call | flops 20971520 | bytes 4194304 | tf_op jit(solution)/shard_map/banded/pallas_call | solution.py:633
  11.0 0.0 collective-permute-done.2.refs_3_
  11.0 1.4 %collective-permute-done.1.refs_2_ = bf16[272,128]{1,0:T(8,128)(2,1)S(1)} collective-permute-done((bf16[272,128]{1,0:T(8,128)(2,1)S(1)}, bf16[272,128]{1,0:T(8,128)(2,1)S(1)}, u32[]{:S(2)}, u32[]{:S(2)}) %collective-permute-start.1) | collective-permute-done | bytes 69664 | tf_op jit(solution)/shard_map/ppermute | solution.py:605
  12.5 0.0 collective-permute-done.refs_1_
  12.5 0.1 collective-permute-start.3
  12.6 1.6 %collective-permute-start.4 = (bf16[32,256]{1,0:T(8,128)(2,1)S(1)}, bf16[32,256]{1,0:T(8,128)(2,1)S(1)}, u32[]{:S(2)}, u32[]{:S(2)}) collective-permute-start(bf16[32,256]{1,0:T(8,128)(2,1)S(1)} %get-tuple-element.17.edge_ref), channel_id=1, source_target_pairs={{0,2},{2,0},{1,3},{3,1},{4,6},{6,4},{5,7},{7,5},{8,10},{10,8},{9,1... | collective-permute-start | bytes 49160 | tf_op jit(solution)/shard_map/ppermute | solution.py:694
  14.2 0.3 %collective-permute-start.5 = (bf16[32,128]{1,0:T(8,128)(2,1)S(1)}, bf16[32,128]{1,0:T(8,128)(2,1)S(1)}, u32[]{:S(2)}, u32[]{:S(2)}) collective-permute-start(bf16[32,128]{1,0:T(8,128)(2,1)S(1)} %corner.1), channel_id=1, source_target_pairs={{0,3},{1,2},{2,1},{3,0},{4,7},{5,6},{6,5},{7,4},{8,11},{9,10},{10,... | collective-permute-start | bytes 24584 | tf_op jit(solution)/shard_map/ppermute | solution.py:693
  14.5 2.8 %collective-permute-done.5.refs_6_ = bf16[32,128]{1,0:T(8,128)(2,1)S(1)} collective-permute-done((bf16[32,128]{1,0:T(8,128)(2,1)S(1)}, bf16[32,128]{1,0:T(8,128)(2,1)S(1)}, u32[]{:S(2)}, u32[]{:S(2)}) %collective-permute-start.5) | collective-permute-done | bytes 8224 | tf_op jit(solution)/shard_map/ppermute | solution.py:693
  17.2 0.0 collective-permute-done.4.refs_5_
  17.2 0.0 collective-permute-done.3.refs_4_
  17.2 7.7 %column.1 = (bf16[2,4,32,256]{3,2,1,0:T(8,128)(2,1)}, f32[1024,128]{1,0:T(8,128)}) custom-call(bf16[272,128]{1,0:T(8,128)(2,1)S(1)} %pack.1.refs_4_._.refs_0_, bf16[272,128]{1,0:T(8,128)(2,1)S(1)} %collective-permute-done.refs_1_, bf16[272,128]{1,0:T(8,128)(2,1)S(1)} %collective-permute-done.1.refs_2_, bf16[272,128]{1,0:T(8,128)(2,1)S(1)} %collective-permute-done.2.refs_3_, ...), custom_call_target="tpu_custom_call" | custom-call | flops 2264924160 | bytes 4194304 | tf_op jit(solution)/shard_map/column/pallas_call | solution.py:697
  (2 shorter events, 0.0 us)
Async XLA Ops:
  1.5 9.6 %collective-permute-start.2 = (bf16[272,128]{1,0:T(8,128)(2,1)S(1)}, bf16[272,128]{1,0:T(8,128)(2,1)S(1)}, u32[]{:S(2)}, u32[]{:S(2)}) collective-permute-start(bf16[272,128]{1,0:T(8,128)(2,1)S(1)} %pack.1.refs_4_._.refs_0_), channel_id=1, source_target_pairs={{0,12},{4,8},{8,4},{12,0},{1,13},{5,9},{9,5},{13,1},{2,14},{6,10},... | collective-permute-start | bytes 208904 | tf_op jit(solution)/shard_map/ppermute | solution.py:605
  6.6 5.9 %collective-permute-start.1 = (bf16[272,128]{1,0:T(8,128)(2,1)S(1)}, bf16[272,128]{1,0:T(8,128)(2,1)S(1)}, u32[]{:S(2)}, u32[]{:S(2)}) collective-permute-start(bf16[272,128]{1,0:T(8,128)(2,1)S(1)} %pack.1.refs_4_._.refs_0_), channel_id=1, source_target_pairs={{0,8},{4,12},{8,0},{12,4},{1,9},{5,13},{9,1},{13,5},{2,10},{6,14},... | collective-permute-start | bytes 208904 | tf_op jit(solution)/shard_map/ppermute | solution.py:605
  6.6 5.9 %collective-permute-start = (bf16[272,128]{1,0:T(8,128)(2,1)S(1)}, bf16[272,128]{1,0:T(8,128)(2,1)S(1)}, u32[]{:S(2)}, u32[]{:S(2)}) collective-permute-start(bf16[272,128]{1,0:T(8,128)(2,1)S(1)} %pack.1.refs_4_._.refs_0_), channel_id=1, source_target_pairs={{0,4},{4,0},{8,12},{12,8},{1,5},{5,1},{9,13},{13,9},{2,6},{6,2},{1... | collective-permute-start | bytes 208904 | tf_op jit(solution)/shard_map/ppermute | solution.py:605
  12.5 4.7 %collective-permute-start.3 = (bf16[512,128]{1,0:T(8,128)(2,1)S(1)}, bf16[512,128]{1,0:T(8,128)(2,1)S(1)}, u32[]{:S(2)}, u32[]{:S(2)}) collective-permute-start(bf16[512,128]{1,0:T(8,128)(2,1)S(1)} %get-tuple-element.16), channel_id=1, source_target_pairs={{0,1},{1,0},{2,3},{3,2},{4,5},{5,4},{6,7},{7,6},{8,9},{9,8},{10,11... | collective-permute-start | bytes 393224 | tf_op jit(solution)/shard_map/ppermute | solution.py:695
  12.6 4.6 %collective-permute-start.4 = (bf16[32,256]{1,0:T(8,128)(2,1)S(1)}, bf16[32,256]{1,0:T(8,128)(2,1)S(1)}, u32[]{:S(2)}, u32[]{:S(2)}) collective-permute-start(bf16[32,256]{1,0:T(8,128)(2,1)S(1)} %get-tuple-element.17.edge_ref), channel_id=1, source_target_pairs={{0,2},{2,0},{1,3},{3,1},{4,6},{6,4},{5,7},{7,5},{8,10},{10,8},{9,1... | collective-permute-start | bytes 49160 | tf_op jit(solution)/shard_map/ppermute | solution.py:694
  14.2 3.1 %collective-permute-start.5 = (bf16[32,128]{1,0:T(8,128)(2,1)S(1)}, bf16[32,128]{1,0:T(8,128)(2,1)S(1)}, u32[]{:S(2)}, u32[]{:S(2)}) collective-permute-start(bf16[32,128]{1,0:T(8,128)(2,1)S(1)} %corner.1), channel_id=1, source_target_pairs={{0,3},{1,2},{2,1},{3,0},{4,7},{5,6},{6,5},{7,4},{8,11},{9,10},{10,... | collective-permute-start | bytes 24584 | tf_op jit(solution)/shard_map/ppermute | solution.py:693

commit v13 on v12

--- a/solution.py
+++ b/solution.py
@@ -315,7 +315,7 @@
     single = segment == count_gz
 
     def tile_of(i):
-        return jnp.bitwise_xor(z_index, i) if few > 1 else i
+        return lax.rem(z_index + i, count_gz) if few > 1 else i
 
     size = depth * BY
 
@@ -602,7 +602,7 @@
     few = count_gz if count_gz in (2, 4) else 1
     if few > 1:
         tiles = [payload] + [
-            lax.ppermute(payload, "gz", [(i, i ^ s) for i in range(count_gz)])
+            lax.ppermute(payload, "gz", [((i + s) % count_gz, i) for i in range(count_gz)])
             for s in range(1, count_gz)
         ]
     else:

time: 25.1 us -> 25 us (level)
  waiting for transfers between devices: 4.23 us -> 2.78 us
  starting transfers between devices: 7.69 us -> 8.95 us
    ppermute x3, waiting for transfers between devices: 1.45 us -> 0.01 us  [per_device(): lax.ppermute(payload, 'gz', [((i + s) % count_gz, i) for i in range(count...]
    ppermute x3, starting transfers between devices: 5.76 us -> 7.01 us  [per_device(): lax.ppermute(payload, 'gz', [((i + s) % count_gz, i) for i in range(count...]
  transfers between devices with their start and end apart: 6 -> 6, of which waited for: 2 -> 1; matrix products, arithmetic and copies ran while one was open for 0% -> 0% of each run, Pallas kernels for 15% -> 15%
where the time goes in v13:
time: 25 us; the launch traced here: 24.7 us
  Pallas kernels  12.3 us (49%)
  starting transfers between devices  8.95 us (36%)
  waiting for transfers between devices  2.78 us (11%)
  between operations  0.7 us (3%)
    pallas_call x1, Pallas kernels, per_device(): pl.pallas_call(functools.partial(column_kernel, (count_gz, count_gy, dept...  7.67 us
    ppermute x3, starting transfers between devices, per_device(): lax.ppermute(payload, 'gz', [((i + s) % count_gz, i) for i in range(count...  7.01 us
    ppermute x1, waiting for transfers between devices, per_device(): corner = lax.ppermute(corner, ('gy', 'col'), over)  2.77 us
    pallas_call x1, Pallas kernels, per_device(): pl.pallas_call(functools.partial(prepare_kernel, (depth, slots)), out_sha...  2 us
    pallas_call x1, Pallas kernels, per_device(): pl.pallas_call(banded_kernel, out_shape=(shape((2 * TALL, 4 * PART), bf16...  1.79 us
    ppermute x1, starting transfers between devices, per_device(): edges += [lax.ppermute(edge, 'gy', pairs), corner]  1.55 us
    pallas_call x1, Pallas kernels, per_device(): pl.pallas_call(pack_kernel, out_shape=shape((columns // BX * height + TIL...  0.82 us
  transfers between devices with their start and end apart: 6, of which 1 were waited for; matrix products, arithmetic and copies ran while one was open for 0% of the time, Pallas kernels for 15%

profile of v13, /device:TPU:0, one launch (start us, length us, event | category | flops | bytes accessed | tf_op | source)
XLA Modules:
  0.0 24.7 jit_solution(15659973392406199213)
XLA Ops:
  0.6 0.8 %pack.1.refs_4_._.refs_0_ = bf16[272,128]{1,0:T(8,128)(2,1)S(1)} custom-call(bf16[128,256]{1,0:T(8,128)(2,1)} %bitcast.13, s32[1,16]{1,0:T(1,128)} %bitcast.14), custom_call_target="tpu_custom_call" | custom-call | tf_op jit(solution)/shard_map/pack/pallas_call | solution.py:589
  1.5 3.1 %collective-permute-start.2 = (bf16[272,128]{1,0:T(8,128)(2,1)S(1)}, bf16[272,128]{1,0:T(8,128)(2,1)S(1)}, u32[]{:S(2)}, u32[]{:S(2)}) collective-permute-start(bf16[272,128]{1,0:T(8,128)(2,1)S(1)} %pack.1.refs_4_._.refs_0_), channel_id=1, source_target_pairs={{12,0},{0,4},{4,8},{8,12},{13,1},{1,5},{5,9},{9,13},{14,2},{2,6},{... | collective-permute-start | bytes 208904 | tf_op jit(solution)/shard_map/ppermute | solution.py:605
  4.5 2.6 %collective-permute-start.1 = (bf16[272,128]{1,0:T(8,128)(2,1)S(1)}, bf16[272,128]{1,0:T(8,128)(2,1)S(1)}, u32[]{:S(2)}, u32[]{:S(2)}) collective-permute-start(bf16[272,128]{1,0:T(8,128)(2,1)S(1)} %pack.1.refs_4_._.refs_0_), channel_id=1, source_target_pairs={{8,0},{12,4},{0,8},{4,12},{9,1},{13,5},{1,9},{5,13},{10,2},{14,6},... | collective-permute-start | bytes 208904 | tf_op jit(solution)/shard_map/ppermute | solution.py:605
  7.1 1.3 %collective-permute-start = (bf16[272,128]{1,0:T(8,128)(2,1)S(1)}, bf16[272,128]{1,0:T(8,128)(2,1)S(1)}, u32[]{:S(2)}, u32[]{:S(2)}) collective-permute-start(bf16[272,128]{1,0:T(8,128)(2,1)S(1)} %pack.1.refs_4_._.refs_0_), channel_id=1, source_target_pairs={{4,0},{8,4},{12,8},{0,12},{5,1},{9,5},{13,9},{1,13},{6,2},{10,6},{... | collective-permute-start | bytes 208904 | tf_op jit(solution)/shard_map/ppermute | solution.py:605
  8.5 2.0 %prepare.1 = (f32[512,128]{1,0:T(8,128)S(1)}, f32[512,128]{1,0:T(8,128)S(1)}, f32[512,128]{1,0:T(8,128)S(1)}, f32[512,128]{1,0:T(8,128)S(1)}, f32[512,128]{1,0:T(8,128)S(1)}) custom-call(f32[1024,128]{1,0:T(8,128)} %bitcast.11, bf16[512,128]{1,0:T(8,128)(2,1)} %bitcast.12, bf16[272,128]{1,0:T(8,128)(2,1)S(1)} %pack.1.refs_4_._.refs_0_), custom_call_target="tpu_custom_call" | custom-call | flops 3932160 | bytes 1048576 | tf_op jit(solution)/shard_map/prepare/pallas_call | solution.py:612
  10.5 1.8 %banded.1 = (bf16[288,256]{1,0:T(8,128)(2,1)S(1)}, bf16[192,576]{1,0:T(8,128)(2,1)S(1)}, f32[32,128]{1,0:T(8,128)S(1)}) custom-call(bf16[8,27]{1,0:T(8,128)(2,1)} %bitcast.16, f32[8]{0:T(128)} %refs_1_.1, bf16[16,27]{1,0:T(8,128)(2,1)} %bitcast.15, f32[2]{0:T(128)} %refs_3_.1, bf16[272,128]{1,0:T(8,128)(2,1)S(1)} %pack.1.refs_4_._.refs_0_), custom_call_target="tpu_custom_call" | custom-call | flops 20971520 | bytes 4194304 | tf_op jit(solution)/shard_map/banded/pallas_call | solution.py:633
  12.3 0.0 collective-permute-done.2.refs_3_
  12.3 0.0 collective-permute-done.1.refs_2_
  12.3 0.0 collective-permute-done.refs_1_
  12.3 0.1 collective-permute-start.3
  12.4 1.6 %collective-permute-start.4 = (bf16[32,256]{1,0:T(8,128)(2,1)S(1)}, bf16[32,256]{1,0:T(8,128)(2,1)S(1)}, u32[]{:S(2)}, u32[]{:S(2)}) collective-permute-start(bf16[32,256]{1,0:T(8,128)(2,1)S(1)} %get-tuple-element.17.edge_ref), channel_id=1, source_target_pairs={{0,2},{2,0},{1,3},{3,1},{4,6},{6,4},{5,7},{7,5},{8,10},{10,8},{9,1... | collective-permute-start | bytes 49160 | tf_op jit(solution)/shard_map/ppermute | solution.py:694
  14.0 0.3 %collective-permute-start.5 = (bf16[32,128]{1,0:T(8,128)(2,1)S(1)}, bf16[32,128]{1,0:T(8,128)(2,1)S(1)}, u32[]{:S(2)}, u32[]{:S(2)}) collective-permute-start(bf16[32,128]{1,0:T(8,128)(2,1)S(1)} %corner.1), channel_id=1, source_target_pairs={{0,3},{1,2},{2,1},{3,0},{4,7},{5,6},{6,5},{7,4},{8,11},{9,10},{10,... | collective-permute-start | bytes 24584 | tf_op jit(solution)/shard_map/ppermute | solution.py:693
  14.3 2.8 %collective-permute-done.5.refs_6_ = bf16[32,128]{1,0:T(8,128)(2,1)S(1)} collective-permute-done((bf16[32,128]{1,0:T(8,128)(2,1)S(1)}, bf16[32,128]{1,0:T(8,128)(2,1)S(1)}, u32[]{:S(2)}, u32[]{:S(2)}) %collective-permute-start.5) | collective-permute-done | bytes 8224 | tf_op jit(solution)/shard_map/ppermute | solution.py:693
  17.1 0.0 collective-permute-done.4.refs_5_
  17.1 0.0 collective-permute-done.3.refs_4_
  17.1 7.7 %column.1 = (bf16[2,4,32,256]{3,2,1,0:T(8,128)(2,1)}, f32[1024,128]{1,0:T(8,128)}) custom-call(bf16[272,128]{1,0:T(8,128)(2,1)S(1)} %pack.1.refs_4_._.refs_0_, bf16[272,128]{1,0:T(8,128)(2,1)S(1)} %collective-permute-done.refs_1_, bf16[272,128]{1,0:T(8,128)(2,1)S(1)} %collective-permute-done.1.refs_2_, bf16[272,128]{1,0:T(8,128)(2,1)S(1)} %collective-permute-done.2.refs_3_, ...), custom_call_target="tpu_custom_call" | custom-call | flops 2264924160 | bytes 4194304 | tf_op jit(solution)/shard_map/column/pallas_call | solution.py:697
  (2 shorter events, 0.0 us)
Async XLA Ops:
  1.5 10.8 %collective-permute-start.2 = (bf16[272,128]{1,0:T(8,128)(2,1)S(1)}, bf16[272,128]{1,0:T(8,128)(2,1)S(1)}, u32[]{:S(2)}, u32[]{:S(2)}) collective-permute-start(bf16[272,128]{1,0:T(8,128)(2,1)S(1)} %pack.1.refs_4_._.refs_0_), channel_id=1, source_target_pairs={{12,0},{0,4},{4,8},{8,12},{13,1},{1,5},{5,9},{9,13},{14,2},{2,6},{... | collective-permute-start | bytes 208904 | tf_op jit(solution)/shard_map/ppermute | solution.py:605
  4.5 7.8 %collective-permute-start.1 = (bf16[272,128]{1,0:T(8,128)(2,1)S(1)}, bf16[272,128]{1,0:T(8,128)(2,1)S(1)}, u32[]{:S(2)}, u32[]{:S(2)}) collective-permute-start(bf16[272,128]{1,0:T(8,128)(2,1)S(1)} %pack.1.refs_4_._.refs_0_), channel_id=1, source_target_pairs={{8,0},{12,4},{0,8},{4,12},{9,1},{13,5},{1,9},{5,13},{10,2},{14,6},... | collective-permute-start | bytes 208904 | tf_op jit(solution)/shard_map/ppermute | solution.py:605
  7.1 5.2 %collective-permute-start = (bf16[272,128]{1,0:T(8,128)(2,1)S(1)}, bf16[272,128]{1,0:T(8,128)(2,1)S(1)}, u32[]{:S(2)}, u32[]{:S(2)}) collective-permute-start(bf16[272,128]{1,0:T(8,128)(2,1)S(1)} %pack.1.refs_4_._.refs_0_), channel_id=1, source_target_pairs={{4,0},{8,4},{12,8},{0,12},{5,1},{9,5},{13,9},{1,13},{6,2},{10,6},{... | collective-permute-start | bytes 208904 | tf_op jit(solution)/shard_map/ppermute | solution.py:605
  12.3 4.7 %collective-permute-start.3 = (bf16[512,128]{1,0:T(8,128)(2,1)S(1)}, bf16[512,128]{1,0:T(8,128)(2,1)S(1)}, u32[]{:S(2)}, u32[]{:S(2)}) collective-permute-start(bf16[512,128]{1,0:T(8,128)(2,1)S(1)} %get-tuple-element.16), channel_id=1, source_target_pairs={{0,1},{1,0},{2,3},{3,2},{4,5},{5,4},{6,7},{7,6},{8,9},{9,8},{10,11... | collective-permute-start | bytes 393224 | tf_op jit(solution)/shard_map/ppermute | solution.py:695
  12.4 4.6 %collective-permute-start.4 = (bf16[32,256]{1,0:T(8,128)(2,1)S(1)}, bf16[32,256]{1,0:T(8,128)(2,1)S(1)}, u32[]{:S(2)}, u32[]{:S(2)}) collective-permute-start(bf16[32,256]{1,0:T(8,128)(2,1)S(1)} %get-tuple-element.17.edge_ref), channel_id=1, source_target_pairs={{0,2},{2,0},{1,3},{3,1},{4,6},{6,4},{5,7},{7,5},{8,10},{10,8},{9,1... | collective-permute-start | bytes 49160 | tf_op jit(solution)/shard_map/ppermute | solution.py:694
  14.0 3.1 %collective-permute-start.5 = (bf16[32,128]{1,0:T(8,128)(2,1)S(1)}, bf16[32,128]{1,0:T(8,128)(2,1)S(1)}, u32[]{:S(2)}, u32[]{:S(2)}) collective-permute-start(bf16[32,128]{1,0:T(8,128)(2,1)S(1)} %corner.1), channel_id=1, source_target_pairs={{0,3},{1,2},{2,1},{3,0},{4,7},{5,6},{6,5},{7,4},{8,11},{9,10},{10,... | collective-permute-start | bytes 24584 | tf_op jit(solution)/shard_map/ppermute | solution.py:693

commit v14 on v13

--- a/solution.py
+++ b/solution.py
@@ -167,7 +167,7 @@
 
 def edges_kernel(dims, *refs):
     count_gy, depth, rows, columns, few, count = dims
-    tiles, outs = refs[:few], refs[few + 2 :]
+    tiles, outs = refs[:few], refs[few + 1 :]
     g = lax.axis_index("gy")
     c = lax.axis_index("col")
     height = depth * rows
@@ -630,6 +630,22 @@
         in_hbm(biomass.reshape(slots * cells, BX)),
         payload,
     )
+    if count_gy == 2:
+        ways = [[(0, 1), (1, 0)]]
+    else:
+        up = [(i, i + 1) for i in range(count_gy - 1)]
+        ways = [up, [(j, i) for i, j in up]]
+    directions = len(ways)
+    swap = [(0, 1), (1, 0)]
+    near, *sent = pl.pallas_call(
+        functools.partial(edges_kernel, (count_gy, depth, rows, columns, few, count_gz)),
+        out_shape=[shape((depths * rows, BX), bf16)]
+        + [shape((2 * depths, columns), bf16)] * directions,
+        in_specs=[VMEM] * few + [ANY],
+        out_specs=[VMEM] * (1 + directions),
+        compiler_params=pltpu.CompilerParams(vmem_limit_bytes=16 * 2**20),
+        name="edges",
+    )(*tiles, prepared[-1])
     t1, t2, bias2 = pl.pallas_call(
         banded_kernel,
         out_shape=(
@@ -656,25 +672,9 @@
         in_hbm(first_bias),
         in_hbm(second_kernel.transpose(1, 2, 0).reshape(2 * CHANNELS, 27)),
         in_hbm(second_bias),
-        payload,
+        sent[0],
     )
 
-    if count_gy == 2:
-        ways = [[(0, 1), (1, 0)]]
-    else:
-        up = [(i, i + 1) for i in range(count_gy - 1)]
-        ways = [up, [(j, i) for i, j in up]]
-    directions = len(ways)
-    swap = [(0, 1), (1, 0)]
-    near, *sent = pl.pallas_call(
-        functools.partial(edges_kernel, (count_gy, depth, rows, columns, few, count_gz)),
-        out_shape=[shape((depths * rows, BX), bf16)]
-        + [shape((2 * depths, columns), bf16)] * directions,
-        in_specs=[VMEM] * few + [ANY, ANY],
-        out_specs=[VMEM] * (1 + directions),
-        compiler_params=pltpu.CompilerParams(vmem_limit_bytes=16 * 2**20),
-        name="edges",
-    )(*tiles, bias2, prepared[-1])
     edges = []
     for pairs, edge in zip(ways, sent):
         corner = pl.pallas_call(

time: 25 us -> 24.6 us (0.984)
    ppermute x1, waiting for transfers between devices: 2.77 us -> 1.02 us  [per_device(): corner = lax.ppermute(corner, ('gy', 'col'), over)]
    ppermute x3, waiting for transfers between devices: 0.01 us -> 1.52 us  [per_device(): lax.ppermute(payload, 'gz', [((i + s) % count_gz, i) for i in range(count...]
  transfers between devices with their start and end apart: 6 -> 6, of which waited for: 1 -> 3; matrix products, arithmetic and copies ran while one was open for 0% -> 0% of each run, Pallas kernels for 15% -> 16%
where the time goes in v14:
time: 24.6 us; the launch traced here: 24.4 us
  Pallas kernels  12.2 us (50%)
  starting transfers between devices  8.95 us (36%)
  waiting for transfers between devices  2.55 us (10%)
  between operations  0.68 us (3%)
    pallas_call x1, Pallas kernels, per_device(): pl.pallas_call(functools.partial(column_kernel, (count_gz, count_gy, dept...  7.6 us
    ppermute x3, starting transfers between devices, per_device(): lax.ppermute(payload, 'gz', [((i + s) % count_gz, i) for i in range(count...  7.01 us
    pallas_call x1, Pallas kernels, per_device(): pl.pallas_call(functools.partial(prepare_kernel, (depth, slots)), out_sha...  2 us
    pallas_call x1, Pallas kernels, per_device(): pl.pallas_call(banded_kernel, out_shape=(shape((2 * TALL, 4 * PART), bf16...  1.79 us
    ppermute x1, starting transfers between devices, per_device(): edges += [lax.ppermute(edge, 'gy', pairs), corner]  1.6 us
    ppermute x3, waiting for transfers between devices, per_device(): lax.ppermute(payload, 'gz', [((i + s) % count_gz, i) for i in range(count...  1.52 us
    ppermute x1, waiting for transfers between devices, per_device(): corner = lax.ppermute(corner, ('gy', 'col'), over)  1.02 us
    pallas_call x1, Pallas kernels, per_device(): pl.pallas_call(pack_kernel, out_shape=shape((columns // BX * height + TIL...  0.82 us
  transfers between devices with their start and end apart: 6, of which 3 were waited for; matrix products, arithmetic and copies ran while one was open for 0% of the time, Pallas kernels for 16%

profile of v14, /device:TPU:0, one launch (start us, length us, event | category | flops | bytes accessed | tf_op | source)
XLA Modules:
  0.0 24.4 jit_solution(14447733887910274434)
XLA Ops:
  0.6 0.8 %pack.1._.refs_0_ = bf16[272,128]{1,0:T(8,128)(2,1)S(1)} custom-call(bf16[128,256]{1,0:T(8,128)(2,1)} %bitcast.13, s32[1,16]{1,0:T(1,128)} %bitcast.14), custom_call_target="tpu_custom_call" | custom-call | tf_op jit(solution)/shard_map/pack/pallas_call | solution.py:589
  1.5 3.1 %collective-permute-start.2 = (bf16[272,128]{1,0:T(8,128)(2,1)S(1)}, bf16[272,128]{1,0:T(8,128)(2,1)S(1)}, u32[]{:S(2)}, u32[]{:S(2)}) collective-permute-start(bf16[272,128]{1,0:T(8,128)(2,1)S(1)} %pack.1._.refs_0_), channel_id=1, source_target_pairs={{12,0},{0,4},{4,8},{8,12},{13,1},{1,5},{5,9},{9,13},{14,2},{2,6},{... | collective-permute-start | bytes 208904 | tf_op jit(solution)/shard_map/ppermute | solution.py:605
  4.5 2.6 %collective-permute-start.1 = (bf16[272,128]{1,0:T(8,128)(2,1)S(1)}, bf16[272,128]{1,0:T(8,128)(2,1)S(1)}, u32[]{:S(2)}, u32[]{:S(2)}) collective-permute-start(bf16[272,128]{1,0:T(8,128)(2,1)S(1)} %pack.1._.refs_0_), channel_id=1, source_target_pairs={{8,0},{12,4},{0,8},{4,12},{9,1},{13,5},{1,9},{5,13},{10,2},{14,6},... | collective-permute-start | bytes 208904 | tf_op jit(solution)/shard_map/ppermute | solution.py:605
  7.1 1.3 %collective-permute-start = (bf16[272,128]{1,0:T(8,128)(2,1)S(1)}, bf16[272,128]{1,0:T(8,128)(2,1)S(1)}, u32[]{:S(2)}, u32[]{:S(2)}) collective-permute-start(bf16[272,128]{1,0:T(8,128)(2,1)S(1)} %pack.1._.refs_0_), channel_id=1, source_target_pairs={{4,0},{8,4},{12,8},{0,12},{5,1},{9,5},{13,9},{1,13},{6,2},{10,6},{... | collective-permute-start | bytes 208904 | tf_op jit(solution)/shard_map/ppermute | solution.py:605
  8.5 2.0 %prepare.1 = (f32[512,128]{1,0:T(8,128)S(1)}, f32[512,128]{1,0:T(8,128)S(1)}, f32[512,128]{1,0:T(8,128)S(1)}, f32[512,128]{1,0:T(8,128)S(1)}, f32[512,128]{1,0:T(8,128)S(1)}) custom-call(f32[1024,128]{1,0:T(8,128)} %bitcast.11, bf16[512,128]{1,0:T(8,128)(2,1)} %bitcast.12, bf16[272,128]{1,0:T(8,128)(2,1)S(1)} %pack.1._.refs_0_), custom_call_target="tpu_custom_call" | custom-call | flops 3932160 | bytes 1048576 | tf_op jit(solution)/shard_map/prepare/pallas_call | solution.py:612
  10.5 0.0 collective-permute-done.2.refs_3_
  10.5 1.3 %collective-permute-done.1.refs_2_ = bf16[272,128]{1,0:T(8,128)(2,1)S(1)} collective-permute-done((bf16[272,128]{1,0:T(8,128)(2,1)S(1)}, bf16[272,128]{1,0:T(8,128)(2,1)S(1)}, u32[]{:S(2)}, u32[]{:S(2)}) %collective-permute-start.1) | collective-permute-done | bytes 69664 | tf_op jit(solution)/shard_map/ppermute | solution.py:605
  11.8 0.2 collective-permute-done.refs_1_
  12.0 0.1 collective-permute-start.3
  12.1 1.6 %collective-permute-start.4 = (bf16[32,256]{1,0:T(8,128)(2,1)S(1)}, bf16[32,256]{1,0:T(8,128)(2,1)S(1)}, u32[]{:S(2)}, u32[]{:S(2)}) collective-permute-start(bf16[32,256]{1,0:T(8,128)(2,1)S(1)} %get-tuple-element.16.edge_ref.refs_4_), channel_id=1, source_target_pairs={{0,2},{2,0},{1,3},{3,1},{4,6},{6,4},{5,7},{7,5},{8,10},{10,8},{9,1... | collective-permute-start | bytes 49160 | tf_op jit(solution)/shard_map/ppermute | solution.py:694
  13.7 0.3 %collective-permute-start.5 = (bf16[32,128]{1,0:T(8,128)(2,1)S(1)}, bf16[32,128]{1,0:T(8,128)(2,1)S(1)}, u32[]{:S(2)}, u32[]{:S(2)}) collective-permute-start(bf16[32,128]{1,0:T(8,128)(2,1)S(1)} %corner.1), channel_id=1, source_target_pairs={{0,3},{1,2},{2,1},{3,0},{4,7},{5,6},{6,5},{7,4},{8,11},{9,10},{10,... | collective-permute-start | bytes 24584 | tf_op jit(solution)/shard_map/ppermute | solution.py:693
  14.0 1.8 %banded.1 = (bf16[288,256]{1,0:T(8,128)(2,1)S(1)}, bf16[192,576]{1,0:T(8,128)(2,1)S(1)}, f32[32,128]{1,0:T(8,128)S(1)}) custom-call(bf16[8,27]{1,0:T(8,128)(2,1)} %bitcast.16, f32[8]{0:T(128)} %refs_1_.1, bf16[16,27]{1,0:T(8,128)(2,1)} %bitcast.15, f32[2]{0:T(128)} %refs_3_.1, bf16[32,256]{1,0:T(8,128)(2,1)S(1)} %get-tuple-element.16.edge_ref.refs_4_), custom_call_target="tpu_custom_call" | custom-call | flops 20971520 | bytes 4194304 | tf_op jit(solution)/shard_map/banded/pallas_call | solution.py:649
  15.8 1.0 %collective-permute-done.5.refs_6_ = bf16[32,128]{1,0:T(8,128)(2,1)S(1)} collective-permute-done((bf16[32,128]{1,0:T(8,128)(2,1)S(1)}, bf16[32,128]{1,0:T(8,128)(2,1)S(1)}, u32[]{:S(2)}, u32[]{:S(2)}) %collective-permute-start.5) | collective-permute-done | bytes 8224 | tf_op jit(solution)/shard_map/ppermute | solution.py:693
  16.8 0.0 collective-permute-done.4.refs_5_
  16.8 0.0 collective-permute-done.3.refs_4_
  16.8 7.6 %column.1 = (bf16[2,4,32,256]{3,2,1,0:T(8,128)(2,1)}, f32[1024,128]{1,0:T(8,128)}) custom-call(bf16[272,128]{1,0:T(8,128)(2,1)S(1)} %pack.1._.refs_0_, bf16[272,128]{1,0:T(8,128)(2,1)S(1)} %collective-permute-done.refs_1_, bf16[272,128]{1,0:T(8,128)(2,1)S(1)} %collective-permute-done.1.refs_2_, bf16[272,128]{1,0:T(8,128)(2,1)S(1)} %collective-permute-done.2.refs_3_, ...), custom_call_target="tpu_custom_call" | custom-call | flops 2264924160 | bytes 4194304 | tf_op jit(solution)/shard_map/column/pallas_call | solution.py:697
  (2 shorter events, 0.0 us)
Async XLA Ops:
  1.5 9.0 %collective-permute-start.2 = (bf16[272,128]{1,0:T(8,128)(2,1)S(1)}, bf16[272,128]{1,0:T(8,128)(2,1)S(1)}, u32[]{:S(2)}, u32[]{:S(2)}) collective-permute-start(bf16[272,128]{1,0:T(8,128)(2,1)S(1)} %pack.1._.refs_0_), channel_id=1, source_target_pairs={{12,0},{0,4},{4,8},{8,12},{13,1},{1,5},{5,9},{9,13},{14,2},{2,6},{... | collective-permute-start | bytes 208904 | tf_op jit(solution)/shard_map/ppermute | solution.py:605
  4.5 7.3 %collective-permute-start.1 = (bf16[272,128]{1,0:T(8,128)(2,1)S(1)}, bf16[272,128]{1,0:T(8,128)(2,1)S(1)}, u32[]{:S(2)}, u32[]{:S(2)}) collective-permute-start(bf16[272,128]{1,0:T(8,128)(2,1)S(1)} %pack.1._.refs_0_), channel_id=1, source_target_pairs={{8,0},{12,4},{0,8},{4,12},{9,1},{13,5},{1,9},{5,13},{10,2},{14,6},... | collective-permute-start | bytes 208904 | tf_op jit(solution)/shard_map/ppermute | solution.py:605
  7.1 4.9 %collective-permute-start = (bf16[272,128]{1,0:T(8,128)(2,1)S(1)}, bf16[272,128]{1,0:T(8,128)(2,1)S(1)}, u32[]{:S(2)}, u32[]{:S(2)}) collective-permute-start(bf16[272,128]{1,0:T(8,128)(2,1)S(1)} %pack.1._.refs_0_), channel_id=1, source_target_pairs={{4,0},{8,4},{12,8},{0,12},{5,1},{9,5},{13,9},{1,13},{6,2},{10,6},{... | collective-permute-start | bytes 208904 | tf_op jit(solution)/shard_map/ppermute | solution.py:605
  12.0 4.8 %collective-permute-start.3 = (bf16[512,128]{1,0:T(8,128)(2,1)S(1)}, bf16[512,128]{1,0:T(8,128)(2,1)S(1)}, u32[]{:S(2)}, u32[]{:S(2)}) collective-permute-start(bf16[512,128]{1,0:T(8,128)(2,1)S(1)} %get-tuple-element.15), channel_id=1, source_target_pairs={{0,1},{1,0},{2,3},{3,2},{4,5},{5,4},{6,7},{7,6},{8,9},{9,8},{10,11... | collective-permute-start | bytes 393224 | tf_op jit(solution)/shard_map/ppermute | solution.py:695
  12.1 4.7 %collective-permute-start.4 = (bf16[32,256]{1,0:T(8,128)(2,1)S(1)}, bf16[32,256]{1,0:T(8,128)(2,1)S(1)}, u32[]{:S(2)}, u32[]{:S(2)}) collective-permute-start(bf16[32,256]{1,0:T(8,128)(2,1)S(1)} %get-tuple-element.16.edge_ref.refs_4_), channel_id=1, source_target_pairs={{0,2},{2,0},{1,3},{3,1},{4,6},{6,4},{5,7},{7,5},{8,10},{10,8},{9,1... | collective-permute-start | bytes 49160 | tf_op jit(solution)/shard_map/ppermute | solution.py:694
  13.7 3.1 %collective-permute-start.5 = (bf16[32,128]{1,0:T(8,128)(2,1)S(1)}, bf16[32,128]{1,0:T(8,128)(2,1)S(1)}, u32[]{:S(2)}, u32[]{:S(2)}) collective-permute-start(bf16[32,128]{1,0:T(8,128)(2,1)S(1)} %corner.1), channel_id=1, source_target_pairs={{0,3},{1,2},{2,1},{3,0},{4,7},{5,6},{6,5},{7,4},{8,11},{9,10},{10,... | collective-permute-start | bytes 24584 | tf_op jit(solution)/shard_map/ppermute | solution.py:693

commit v15 on v14

--- a/solution.py
+++ b/solution.py
@@ -521,7 +521,7 @@
         at = pl.ds(pl.multiple_of(group * 16 * size, 16 * size), 16 * size)
         return pltpu.make_async_copy(state.at[at], next_ref.at[at], group_sems.at[group])
 
-    @pl.loop(0, slots // 8)
+    @pl.loop(0, slots // 8, unroll=2)
     def _(group):
         grid = [(z, y) for z in range(depth) for y in range(BY)]
 

time: 24.6 us -> 24.3 us (0.988)
  Pallas kernels: 12.2 us -> 11.8 us
    pallas_call x1, Pallas kernels: 7.6 us -> 7.22 us  [per_device(): pl.pallas_call(functools.partial(column_kernel, (count_gz, count_gy, dept...]
where the time goes in v15:
time: 24.3 us; the launch traced here: 24 us
  Pallas kernels  11.8 us (49%)
  starting transfers between devices  8.95 us (37%)
  waiting for transfers between devices  2.55 us (10%)
  between operations  0.68 us (3%)
    pallas_call x1, Pallas kernels, per_device(): pl.pallas_call(functools.partial(column_kernel, (count_gz, count_gy, dept...  7.22 us
    ppermute x3, starting transfers between devices, per_device(): lax.ppermute(payload, 'gz', [((i + s) % count_gz, i) for i in range(count...  7.01 us
    pallas_call x1, Pallas kernels, per_device(): pl.pallas_call(functools.partial(prepare_kernel, (depth, slots)), out_sha...  2 us
    pallas_call x1, Pallas kernels, per_device(): pl.pallas_call(banded_kernel, out_shape=(shape((2 * TALL, 4 * PART), bf16...  1.79 us
    ppermute x1, starting transfers between devices, per_device(): edges += [lax.ppermute(edge, 'gy', pairs), corner]  1.6 us
    ppermute x3, waiting for transfers between devices, per_device(): lax.ppermute(payload, 'gz', [((i + s) % count_gz, i) for i in range(count...  1.52 us
    ppermute x1, waiting for transfers between devices, per_device(): corner = lax.ppermute(corner, ('gy', 'col'), over)  1.02 us
    pallas_call x1, Pallas kernels, per_device(): pl.pallas_call(pack_kernel, out_shape=shape((columns // BX * height + TIL...  0.82 us
  transfers between devices with their start and end apart: 6, of which 3 were waited for; matrix products, arithmetic and copies ran while one was open for 0% of the time, Pallas kernels for 16%

profile of v15, /device:TPU:0, one launch (start us, length us, event | category | flops | bytes accessed | tf_op | source)
XLA Modules:
  0.0 24.0 jit_solution(13941694046887855539)
XLA Ops:
  0.6 0.8 %pack.1._.refs_0_ = bf16[272,128]{1,0:T(8,128)(2,1)S(1)} custom-call(bf16[128,256]{1,0:T(8,128)(2,1)} %bitcast.13, s32[1,16]{1,0:T(1,128)} %bitcast.14), custom_call_target="tpu_custom_call" | custom-call | tf_op jit(solution)/shard_map/pack/pallas_call | solution.py:589
  1.5 3.1 %collective-permute-start.2 = (bf16[272,128]{1,0:T(8,128)(2,1)S(1)}, bf16[272,128]{1,0:T(8,128)(2,1)S(1)}, u32[]{:S(2)}, u32[]{:S(2)}) collective-permute-start(bf16[272,128]{1,0:T(8,128)(2,1)S(1)} %pack.1._.refs_0_), channel_id=1, source_target_pairs={{12,0},{0,4},{4,8},{8,12},{13,1},{1,5},{5,9},{9,13},{14,2},{2,6},{... | collective-permute-start | bytes 208904 | tf_op jit(solution)/shard_map/ppermute | solution.py:605
  4.5 2.6 %collective-permute-start.1 = (bf16[272,128]{1,0:T(8,128)(2,1)S(1)}, bf16[272,128]{1,0:T(8,128)(2,1)S(1)}, u32[]{:S(2)}, u32[]{:S(2)}) collective-permute-start(bf16[272,128]{1,0:T(8,128)(2,1)S(1)} %pack.1._.refs_0_), channel_id=1, source_target_pairs={{8,0},{12,4},{0,8},{4,12},{9,1},{13,5},{1,9},{5,13},{10,2},{14,6},... | collective-permute-start | bytes 208904 | tf_op jit(solution)/shard_map/ppermute | solution.py:605
  7.1 1.3 %collective-permute-start = (bf16[272,128]{1,0:T(8,128)(2,1)S(1)}, bf16[272,128]{1,0:T(8,128)(2,1)S(1)}, u32[]{:S(2)}, u32[]{:S(2)}) collective-permute-start(bf16[272,128]{1,0:T(8,128)(2,1)S(1)} %pack.1._.refs_0_), channel_id=1, source_target_pairs={{4,0},{8,4},{12,8},{0,12},{5,1},{9,5},{13,9},{1,13},{6,2},{10,6},{... | collective-permute-start | bytes 208904 | tf_op jit(solution)/shard_map/ppermute | solution.py:605
  8.5 2.0 %prepare.1 = (f32[512,128]{1,0:T(8,128)S(1)}, f32[512,128]{1,0:T(8,128)S(1)}, f32[512,128]{1,0:T(8,128)S(1)}, f32[512,128]{1,0:T(8,128)S(1)}, f32[512,128]{1,0:T(8,128)S(1)}) custom-call(f32[1024,128]{1,0:T(8,128)} %bitcast.11, bf16[512,128]{1,0:T(8,128)(2,1)} %bitcast.12, bf16[272,128]{1,0:T(8,128)(2,1)S(1)} %pack.1._.refs_0_), custom_call_target="tpu_custom_call" | custom-call | flops 3932160 | bytes 1048576 | tf_op jit(solution)/shard_map/prepare/pallas_call | solution.py:612
  10.5 0.0 collective-permute-done.2.refs_3_
  10.5 1.3 %collective-permute-done.1.refs_2_ = bf16[272,128]{1,0:T(8,128)(2,1)S(1)} collective-permute-done((bf16[272,128]{1,0:T(8,128)(2,1)S(1)}, bf16[272,128]{1,0:T(8,128)(2,1)S(1)}, u32[]{:S(2)}, u32[]{:S(2)}) %collective-permute-start.1) | collective-permute-done | bytes 69664 | tf_op jit(solution)/shard_map/ppermute | solution.py:605
  11.8 0.2 collective-permute-done.refs_1_
  12.0 0.1 collective-permute-start.3
  12.1 1.6 %collective-permute-start.4 = (bf16[32,256]{1,0:T(8,128)(2,1)S(1)}, bf16[32,256]{1,0:T(8,128)(2,1)S(1)}, u32[]{:S(2)}, u32[]{:S(2)}) collective-permute-start(bf16[32,256]{1,0:T(8,128)(2,1)S(1)} %get-tuple-element.16.edge_ref.refs_4_), channel_id=1, source_target_pairs={{0,2},{2,0},{1,3},{3,1},{4,6},{6,4},{5,7},{7,5},{8,10},{10,8},{9,1... | collective-permute-start | bytes 49160 | tf_op jit(solution)/shard_map/ppermute | solution.py:694
  13.7 0.3 %collective-permute-start.5 = (bf16[32,128]{1,0:T(8,128)(2,1)S(1)}, bf16[32,128]{1,0:T(8,128)(2,1)S(1)}, u32[]{:S(2)}, u32[]{:S(2)}) collective-permute-start(bf16[32,128]{1,0:T(8,128)(2,1)S(1)} %corner.1), channel_id=1, source_target_pairs={{0,3},{1,2},{2,1},{3,0},{4,7},{5,6},{6,5},{7,4},{8,11},{9,10},{10,... | collective-permute-start | bytes 24584 | tf_op jit(solution)/shard_map/ppermute | solution.py:693
  14.0 1.8 %banded.1 = (bf16[288,256]{1,0:T(8,128)(2,1)S(1)}, bf16[192,576]{1,0:T(8,128)(2,1)S(1)}, f32[32,128]{1,0:T(8,128)S(1)}) custom-call(bf16[8,27]{1,0:T(8,128)(2,1)} %bitcast.16, f32[8]{0:T(128)} %refs_1_.1, bf16[16,27]{1,0:T(8,128)(2,1)} %bitcast.15, f32[2]{0:T(128)} %refs_3_.1, bf16[32,256]{1,0:T(8,128)(2,1)S(1)} %get-tuple-element.16.edge_ref.refs_4_), custom_call_target="tpu_custom_call" | custom-call | flops 20971520 | bytes 4194304 | tf_op jit(solution)/shard_map/banded/pallas_call | solution.py:649
  15.8 1.0 %collective-permute-done.5.refs_6_ = bf16[32,128]{1,0:T(8,128)(2,1)S(1)} collective-permute-done((bf16[32,128]{1,0:T(8,128)(2,1)S(1)}, bf16[32,128]{1,0:T(8,128)(2,1)S(1)}, u32[]{:S(2)}, u32[]{:S(2)}) %collective-permute-start.5) | collective-permute-done | bytes 8224 | tf_op jit(solution)/shard_map/ppermute | solution.py:693
  16.8 0.0 collective-permute-done.4.refs_5_
  16.8 0.0 collective-permute-done.3.refs_4_
  16.8 7.2 %column.1 = (bf16[2,4,32,256]{3,2,1,0:T(8,128)(2,1)}, f32[1024,128]{1,0:T(8,128)}) custom-call(bf16[272,128]{1,0:T(8,128)(2,1)S(1)} %pack.1._.refs_0_, bf16[272,128]{1,0:T(8,128)(2,1)S(1)} %collective-permute-done.refs_1_, bf16[272,128]{1,0:T(8,128)(2,1)S(1)} %collective-permute-done.1.refs_2_, bf16[272,128]{1,0:T(8,128)(2,1)S(1)} %collective-permute-done.2.refs_3_, ...), custom_call_target="tpu_custom_call" | custom-call | flops 2264924160 | bytes 4194304 | tf_op jit(solution)/shard_map/column/pallas_call | solution.py:697
  (2 shorter events, 0.0 us)
Async XLA Ops:
  1.5 9.0 %collective-permute-start.2 = (bf16[272,128]{1,0:T(8,128)(2,1)S(1)}, bf16[272,128]{1,0:T(8,128)(2,1)S(1)}, u32[]{:S(2)}, u32[]{:S(2)}) collective-permute-start(bf16[272,128]{1,0:T(8,128)(2,1)S(1)} %pack.1._.refs_0_), channel_id=1, source_target_pairs={{12,0},{0,4},{4,8},{8,12},{13,1},{1,5},{5,9},{9,13},{14,2},{2,6},{... | collective-permute-start | bytes 208904 | tf_op jit(solution)/shard_map/ppermute | solution.py:605
  4.5 7.3 %collective-permute-start.1 = (bf16[272,128]{1,0:T(8,128)(2,1)S(1)}, bf16[272,128]{1,0:T(8,128)(2,1)S(1)}, u32[]{:S(2)}, u32[]{:S(2)}) collective-permute-start(bf16[272,128]{1,0:T(8,128)(2,1)S(1)} %pack.1._.refs_0_), channel_id=1, source_target_pairs={{8,0},{12,4},{0,8},{4,12},{9,1},{13,5},{1,9},{5,13},{10,2},{14,6},... | collective-permute-start | bytes 208904 | tf_op jit(solution)/shard_map/ppermute | solution.py:605
  7.1 4.9 %collective-permute-start = (bf16[272,128]{1,0:T(8,128)(2,1)S(1)}, bf16[272,128]{1,0:T(8,128)(2,1)S(1)}, u32[]{:S(2)}, u32[]{:S(2)}) collective-permute-start(bf16[272,128]{1,0:T(8,128)(2,1)S(1)} %pack.1._.refs_0_), channel_id=1, source_target_pairs={{4,0},{8,4},{12,8},{0,12},{5,1},{9,5},{13,9},{1,13},{6,2},{10,6},{... | collective-permute-start | bytes 208904 | tf_op jit(solution)/shard_map/ppermute | solution.py:605
  12.0 4.8 %collective-permute-start.3 = (bf16[512,128]{1,0:T(8,128)(2,1)S(1)}, bf16[512,128]{1,0:T(8,128)(2,1)S(1)}, u32[]{:S(2)}, u32[]{:S(2)}) collective-permute-start(bf16[512,128]{1,0:T(8,128)(2,1)S(1)} %get-tuple-element.15), channel_id=1, source_target_pairs={{0,1},{1,0},{2,3},{3,2},{4,5},{5,4},{6,7},{7,6},{8,9},{9,8},{10,11... | collective-permute-start | bytes 393224 | tf_op jit(solution)/shard_map/ppermute | solution.py:695
  12.1 4.7 %collective-permute-start.4 = (bf16[32,256]{1,0:T(8,128)(2,1)S(1)}, bf16[32,256]{1,0:T(8,128)(2,1)S(1)}, u32[]{:S(2)}, u32[]{:S(2)}) collective-permute-start(bf16[32,256]{1,0:T(8,128)(2,1)S(1)} %get-tuple-element.16.edge_ref.refs_4_), channel_id=1, source_target_pairs={{0,2},{2,0},{1,3},{3,1},{4,6},{6,4},{5,7},{7,5},{8,10},{10,8},{9,1... | collective-permute-start | bytes 49160 | tf_op jit(solution)/shard_map/ppermute | solution.py:694
  13.7 3.1 %collective-permute-start.5 = (bf16[32,128]{1,0:T(8,128)(2,1)S(1)}, bf16[32,128]{1,0:T(8,128)(2,1)S(1)}, u32[]{:S(2)}, u32[]{:S(2)}) collective-permute-start(bf16[32,128]{1,0:T(8,128)(2,1)S(1)} %corner.1), channel_id=1, source_target_pairs={{0,3},{1,2},{2,1},{3,0},{4,7},{5,6},{6,5},{7,4},{8,11},{9,10},{10,... | collective-permute-start | bytes 24584 | tf_op jit(solution)/shard_map/ppermute | solution.py:693
